TPU v7x, 32 devices: a whole 2x2x4 slice. The times are simulated.
32 devices in a mesh: groups: 2 (over x), tensor: 8 (over z, y), replica: 2 (over core).
Axes of the slice: x: 2, y: 2, z: 4, core: 2. Of those that a mesh axis runs over, the one named last changes fastest.
Arguments:
- inputs: bfloat16 [2048, 8192], P(('groups', 'replica'), 'tensor'), parts along dimension 0, may hold values from -34 to 34, as said below
- entry_gain: bfloat16 [8192], replicated, may hold values from 0.099609375 to 1.8984375
- exit_gain: bfloat16 [8192], replicated, may hold values from 0.099609375 to 1.8984375
- query_weight: bfloat16 [8192, 8192], P(None, 'tensor'), may hold values from -0.0625 to 0.0625
- key_value_matrix: bfloat16 [8192, 2048], P('tensor'), may hold values from -0.0625 to 0.0625
- output_weight: bfloat16 [8192, 8192], P('tensor'), may hold values from -0.09375 to 0.09375
- page_pool: bfloat16 [384, 16, 2048], P(('groups', 'replica')), parts along dimension 0, may hold values from -300 to 300, as said below
- page_table: int32 [1024, 4], P(('groups', 'replica')), parts along dimension 0, may hold values from 0 to 95
- positions: int32 [1024], P(('groups', 'replica')), parts along dimension 0, may hold values from 1 to 64
- request_lengths: int32 [4, 8], P(('groups', 'replica')), parts along dimension 0, may hold values from 1 to 128, 256 in all within a row
- prefix_pages: int32 [4, 8], P(('groups', 'replica')), parts along dimension 0, may hold values from 1 to 4, as said below
- source_pages: int32 [4, 8, 4], P(('groups', 'replica')), parts along dimension 0, may hold values from 0 to 95
- target_pages: int32 [4, 8, 4], P(('groups', 'replica')), parts along dimension 0, may hold values from 0 to 95, as said below
Outputs:
- hidden: bfloat16 [2048, 8192], P(('groups', 'replica'), 'tensor'), parts along dimension 0
- normed_out: bfloat16 [2048, 8192], P(('groups', 'replica'), 'tensor'), parts along dimension 0
There are 2 independent parts, one for each index of `groups`. A program takes and returns all parts, laid end to end along the dimension named above; an argument that names none is the same for every part. Nothing has to cross between parts.
Inputs may be any that keep to these rules, and one draw needn't show every extreme that they name: `inputs`: real-valued activations. `page_pool`: real-valued cached keys and values. `prefix_pages`: in each replica some request has exactly 4 prefix pages. `target_pages`: all distinct within a replica. `request_lengths`: each replica's requests fill its 256 prefill tokens, in order.
All inputs are finite; a program needn't handle non-finite values.
Results may differ from a plain program's by a relative error of at most 0.012.
The roundings to bfloat16 on the way count: a program that leaves them out, or rounds other values in their place, can miss the bound.
Values may be sent and summed in bfloat16 or wider, within the bound.
No kernel may reach another device: no remote copies, remote signals or barrier semaphores. Data moves between devices by JAX's collectives and lax.ppermute only.
A program may use at most 192 MiB of HBM per device.

v0:
```python
import math

import jax
import jax.numpy as jnp
from jax import lax
from jax.sharding import PartitionSpec as P

QUERY_HEADS = 64
KEY_VALUE_HEADS = 8
HEAD_SIZE = 128


EPS = 1e-06
THETA = 1000000.0
NEGATIVE = -1e30


def from_partner(block, axis, stride):
    count = lax.axis_size(axis)
    route = []
    for low in range(count):
        high = low | 1 << stride
        if high != low and high < count:
            route += [(low, high), (high, low)]
    return lax.ppermute(block, axis, route)


def norm_rows(values, gain):
    inv_norm = lax.rsqrt(jnp.mean(values * values, axis=-1, keepdims=True) + EPS)
    return values * inv_norm * gain.astype(jnp.float32)


def rotate(values, positions):
    half_dim = values.shape[-1] // 2
    frequency = jnp.exp(
        jnp.arange(half_dim, dtype=jnp.float32) * (-2.0 * math.log(THETA) / values.shape[-1])
    )
    angles = positions.astype(jnp.float32)[:, None] * frequency[None, :]
    cosine = jnp.cos(angles)[:, None, :]
    sine_part = jnp.sin(angles)[:, None, :]
    first_half = values[..., :half_dim]
    second = values[..., half_dim:]
    return jnp.concatenate(
        [first_half * cosine - second * sine_part, second * cosine + first_half * sine_part],
        axis=-1,
    )


def span_layout(lengths, prefix, prefill, page_size):
    request_end = jnp.cumsum(lengths)
    request_start = request_end - lengths
    token_index = jnp.arange(prefill, dtype=jnp.int32)
    request = jnp.sum((token_index[:, None] >= request_end[None, :]).astype(jnp.int32), axis=1)
    onehot = (request[:, None] == jnp.arange(lengths.shape[0], dtype=jnp.int32)[None, :]).astype(
        jnp.int32
    )
    token_start = jnp.sum(onehot * request_start[None, :], axis=1)
    token_prefix = jnp.sum(onehot * prefix[None, :], axis=1)
    return (request, token_prefix * page_size + token_index - token_start)


def prefix_keys(prefix, pages, page_size):
    slot_count = prefix.shape[0] * pages * page_size
    key_index = jnp.arange(slot_count, dtype=jnp.int32)
    key_owner = key_index // (pages * page_size)
    within = key_index // page_size % pages
    onehot = (key_owner[:, None] == jnp.arange(prefix.shape[0], dtype=jnp.int32)[None, :]).astype(
        jnp.int32
    )
    page_limit = jnp.sum(onehot * prefix[None, :], axis=1)
    return (key_owner, within < page_limit)


def product(form, left, right):
    return jnp.einsum(form, left, right, preferred_element_type=jnp.float32)


def attend(
    query_rows,
    new_keys,
    new_vals,
    pre_keys,
    pre_vals,
    cache_keys,
    cache_vals,
    request,
    key_owner,
    usable,
    filled,
):
    prefill = request.shape[0]
    factor = 1.0 / math.sqrt(query_rows.shape[-1])
    head_q = query_rows[:prefill]
    score_prefix = product("qhd,md->qhm", head_q, pre_keys) * factor
    score_span = product("qhd,kd->qhk", head_q, new_keys[:prefill]) * factor
    token_index = jnp.arange(prefill, dtype=jnp.int32)
    mask_prefix = ((request[:, None] == key_owner[None, :]) & usable[None, :])[:, None, :]
    mask_span = (
        (request[:, None] == request[None, :]) & (token_index[None, :] <= token_index[:, None])
    )[:, None, :]
    score_prefix = jnp.where(mask_prefix, score_prefix, NEGATIVE)
    score_span = jnp.where(mask_span, score_span, NEGATIVE)
    peak_score = jnp.maximum(
        jnp.max(score_prefix, axis=-1, keepdims=True), jnp.max(score_span, axis=-1, keepdims=True)
    )
    exp_prefix = jnp.where(mask_prefix, jnp.exp(score_prefix - peak_score), 0.0)
    exp_span = jnp.where(mask_span, jnp.exp(score_span - peak_score), 0.0)
    denominator = jnp.sum(exp_prefix, axis=-1, keepdims=True) + jnp.sum(
        exp_span, axis=-1, keepdims=True
    )
    weight_prefix = (exp_prefix / denominator).astype(jnp.bfloat16)
    weight_span = (exp_span / denominator).astype(jnp.bfloat16)
    context_pre = product("qhm,md->qhd", weight_prefix, pre_vals) + product(
        "qhk,kd->qhd", weight_span, new_vals[:prefill]
    )
    head_d = query_rows[prefill:]
    score_cache = product("dhx,dtx->dht", head_d, cache_keys) * factor
    score_own = product("dhx,dx->dh", head_d, new_keys[prefill:])[..., None] * factor
    mask_cache = (jnp.arange(cache_keys.shape[1], dtype=jnp.int32)[None, :] < filled[:, None])[
        :, None, :
    ]
    score_cache = jnp.where(mask_cache, score_cache, NEGATIVE)
    peak_dec = jnp.maximum(jnp.max(score_cache, axis=-1, keepdims=True), score_own)
    exp_cache = jnp.where(mask_cache, jnp.exp(score_cache - peak_dec), 0.0)
    exp_own = jnp.exp(score_own - peak_dec)
    denom_dec = jnp.sum(exp_cache, axis=-1, keepdims=True) + exp_own
    weight_cache = (exp_cache / denom_dec).astype(jnp.bfloat16)
    weight_own = (exp_own / denom_dec).astype(jnp.bfloat16)
    context_dec = product("dht,dtx->dhx", weight_cache, cache_vals) + weight_own.astype(
        jnp.float32
    ) * new_vals[prefill:][:, None, :].astype(jnp.float32)
    return jnp.concatenate([context_pre, context_dec], axis=0).astype(jnp.bfloat16)


def body(
    inputs,
    entry_gain,
    exit_gain,
    query_weight,
    key_value_matrix,
    output_weight,
    page_pool,
    page_table,
    positions,
    request_lengths,
    prefix_pages,
    source_pages,
    target_pages,
):
    decode = page_table.shape[0]
    decode_row_count = inputs.shape[0]
    prefill = decode_row_count - decode
    page_size = page_pool.shape[1]
    per_device = query_weight.shape[1] // HEAD_SIZE
    query_group_width = QUERY_HEADS // KEY_VALUE_HEADS
    group_index = lax.axis_index("tensor") * per_device // query_group_width
    full_rows = lax.all_gather(inputs, "tensor", axis=1, tiled=True)
    normed = norm_rows(full_rows.astype(jnp.float32), entry_gain).astype(jnp.bfloat16)
    query_rows = jnp.dot(normed, query_weight, preferred_element_type=jnp.float32).reshape(
        decode_row_count, per_device, HEAD_SIZE
    )
    feature_width = key_value_matrix.shape[0]
    normed_slice = lax.dynamic_slice_in_dim(
        normed, lax.axis_index("tensor") * feature_width, feature_width, 1
    )
    partial_pairs = jnp.dot(normed_slice, key_value_matrix, preferred_element_type=jnp.float32)
    summed_pairs = lax.psum(partial_pairs, "tensor").astype(jnp.bfloat16)
    own_pairs = lax.dynamic_slice_in_dim(
        summed_pairs, group_index * 2 * HEAD_SIZE, 2 * HEAD_SIZE, 1
    )
    lengths_here = request_lengths[0]
    prefix_here = prefix_pages[0]
    request, span_pos = span_layout(lengths_here, prefix_here, prefill, page_size)
    all_pos = jnp.concatenate([span_pos, positions])
    query_rows = rotate(query_rows, all_pos).astype(jnp.bfloat16)
    new_keys = rotate(own_pairs[:, None, :HEAD_SIZE].astype(jnp.float32), all_pos)[:, 0].astype(
        jnp.bfloat16
    )
    new_vals = own_pairs[:, HEAD_SIZE:]
    wanted = from_partner(source_pages, "replica", 0)
    outgoing = page_pool[wanted.reshape(-1)]
    arrived_all = from_partner(outgoing, "replica", 0)
    arrived = lax.dynamic_slice_in_dim(arrived_all, group_index * 2 * HEAD_SIZE, 2 * HEAD_SIZE, 2)
    migp = target_pages.shape[2]
    usable_page = (jnp.arange(migp, dtype=jnp.int32)[None, :] < prefix_here[:, None]).reshape(-1)
    target = jnp.where(usable_page, target_pages[0].reshape(-1), page_pool.shape[0])
    own_pool = lax.dynamic_slice_in_dim(page_pool, group_index * 2 * HEAD_SIZE, 2 * HEAD_SIZE, 2)
    own_pool = own_pool.at[target].set(arrived, mode="drop")
    cached = own_pool[page_table].reshape(decode, -1, 2 * HEAD_SIZE)
    prefix_flat = arrived.reshape(-1, 2 * HEAD_SIZE)
    key_owner, usable = prefix_keys(prefix_here, migp, page_size)
    context = attend(
        query_rows,
        new_keys,
        new_vals,
        prefix_flat[:, :HEAD_SIZE],
        prefix_flat[:, HEAD_SIZE:],
        cached[..., :HEAD_SIZE],
        cached[..., HEAD_SIZE:],
        request,
        key_owner,
        usable,
        positions,
    )
    context = context.reshape(decode_row_count, per_device * HEAD_SIZE)
    partial_sum = jnp.dot(context, output_weight, preferred_element_type=jnp.float32)
    summed = lax.psum_scatter(partial_sum, "tensor", scatter_dimension=1, tiled=True)
    mixed_sum = inputs.astype(jnp.float32) + summed
    squares = lax.psum(jnp.sum(mixed_sum * mixed_sum, axis=1), "tensor")
    inv_norm = lax.rsqrt(squares / exit_gain.shape[0] + EPS)
    col_width = summed.shape[1]
    gain_slice = lax.dynamic_slice_in_dim(
        exit_gain, lax.axis_index("tensor") * col_width, col_width, 0
    )
    hidden = mixed_sum.astype(jnp.bfloat16)
    normed_out = (mixed_sum * inv_norm[:, None] * gain_slice.astype(jnp.float32)[None, :]).astype(
        jnp.bfloat16
    )
    return (hidden, normed_out)


def solution(mesh):
    return jax.shard_map(
        body,
        mesh=mesh,
        in_specs=(
            P(("groups", "replica"), "tensor"),
            P(),
            P(),
            P(None, "tensor"),
            P("tensor", None),
            P("tensor", None),
            P(("groups", "replica"), None, None),
            P(("groups", "replica"), None),
            P(("groups", "replica")),
            P(("groups", "replica"), None),
            P(("groups", "replica"), None),
            P(("groups", "replica"), None, None),
            P(("groups", "replica"), None, None),
        ),
        out_specs=(P(("groups", "replica"), "tensor"), P(("groups", "replica"), "tensor")),
        check_vma=False,
    )
```

profile of v0, /device:TPU:0, one launch (start us, length us, event | category | flops | bytes accessed | tf_op | source)
XLA Modules:
  0.0 689.5 jit_solution(18379631937055991992)
XLA Ops:
  8.5 0.8 reduce-window.4
  10.1 0.7 select_reduce_fusion.2
  11.5 0.7 iota_compare_fusion.5
  12.4 3.5 gather_fusion
  17.3 1.2 constant_dynamic-slice_fusion
  19.3 0.7 fusion.41
  20.1 1.0 multiply_cosine_fusion
  21.1 1.0 constant_dynamic-slice_fusion.1
  22.2 1.5 scatter_fusion
  23.7 9.7 %gather_fusion.1 = bf16[1024,16,256]{2,1,0:T(8,128)(2,1)} fusion(bf16[96,16,256]{2,1,0:T(8,128)(2,1)S(1)} %scatter_fusion, s32[1024]{0:T(1024)S(1)} %broadcast_clamp_fusion), kind=kCustom, calls=%fused_computation.1 | custom fusion | bytes 16781312 | tf_op jit(solution)/shard_map/gather | solution.py:189
  33.4 104.5 %all-gather.2.cloned.1.call-done = bf16[512,8192]{1,0:T(8,128)(2,1)} async-done(((bf16[512,1024]{1,0:T(8,128)(2,1)}), bf16[512,8192]{1,0:T(8,128)(2,1)}) %all-gather.2.cloned.1.call-update) | async-done | bytes 8388624 | tf_op jit(solution)/shard_map/all_gather | solution.py:157
  137.9 5.1 fusion
  143.0 9.8 %fusion.2 = bf16[512,8192]{1,0:T(8,128)(2,1)} fusion(bf16[512,8192]{1,0:T(8,128)(2,1)} %all-gather.2.cloned.1.call-done, f32[8192]{0:T(1024)S(1)} %copy-done.9, f32[512]{0:T(512)S(1)} %add_rsqrt_fusion.1), kind=kLoop, calls=%fused_computation.7 | loop fusion | flops 16777216 | bytes 16812032 | tf_op jit(solution)/shard_map/convert_element_type | solution.py:158
  152.8 6.9 fusion.30
  159.7 165.9 %all-reduce.1 = bf16[512,2048]{0,1:T(8,128)(2,1)S(1)} all-reduce(f32[512,2048]{0,1:T(8,128)} %fusion.30), channel_id=1, replica_groups=mesh['groups'=2,'tensor'=8,'replica'=2] {'tensor'}, use_global_device_ids=true, to_apply=%region_7.8 | all-reduce | flops 1048576 | bytes 6291456 | tf_op jit(solution)/shard_map/psum | solution.py:167
  326.3 14.3 %convolution_bitcast_fusion = f32[64,8,8,128]{3,1,2,0:T(8,128)S(1)} fusion(bf16[512,8192]{1,0:T(8,128)(2,1)} %fusion.2, bf16[8192,1024]{1,0:T(8,128)(2,1)} %param.16), kind=kOutput, calls=%fused_computation.27 | convolution fusion | flops 8589934592 | bytes 27262976 | tf_op jit(solution)/shard_map/dot_general | solution.py:159
  341.1 1.7 copy.74
  344.0 0.8 copy.89
  345.4 0.8 subtract_convert_fusion
  347.6 1.1 fusion.7
  349.3 1.6 fusion.8
  350.9 0.8 fusion.32
  351.7 2.1 fusion.22
  353.8 0.7 slice-done.1
  354.5 2.4 fusion.83
  358.2 3.5 fusion.23
  362.0 15.8 %fusion.26 = f32[512,8192]{1,0:T(8,128)} fusion(bf16[1024,8192]{1,0:T(8,128)(2,1)} %param.18, bf16[256,1024]{0,1:T(8,128)(2,1)S(1)} %bitcast.59, bf16[256,1024]{0,1:T(8,128)(2,1)S(1)} %bitcast.62), kind=kOutput, calls=%fused_computation.37 | convolution fusion | flops 8592031744 | bytes 34603008 | tf_op jit(solution)/shard_map/dot_general | solution.py:206
  377.8 0.8 dynamic-slice_convert_fusion.1
  378.5 280.9 %reduce-scatter.2.cloned.1.call-done = f32[512,1024]{1,0:T(8,128)} async-done(((f32[512,8192]{1,0:T(8,128)}), f32[512,1024]{1,0:T(8,128)}) %reduce-scatter.2.cloned.1.call-update) | async-done | bytes 2097168 | tf_op jit(solution)/shard_map/reduce_scatter | solution.py:207
  659.5 2.1 multiply_reduce_fusion
  661.5 19.5 %psum.15 = f32[512]{0:T(512)S(1)} all-reduce(f32[512]{0:T(512)S(1)} %multiply_reduce_fusion), channel_id=1, replica_groups=mesh['groups'=2,'tensor'=8,'replica'=2] {'tensor'}, use_global_device_ids=true, to_apply=%region_16.17 | all-reduce | flops 512 | bytes 4096 | tf_op jit(solution)/shard_map/psum | solution.py:209
  681.0 1.7 multiply_convert_fusion
  (88 shorter events, 11.7 us)
Async XLA Ops:
  7.2 10.1 %copy-start.14 = (s32[1,8]{1,0:T(1,128)S(1)}, s32[1,8]{1,0:T(1,128)}, u32[]{:S(2)}) copy-start(s32[1,8]{1,0:T(1,128)} %param.23) | copy-start | bytes 100
  7.2 8.9 %copy-start.13 = (s32[1,8,4]{1,2,0:T(4,128)S(1)}, s32[1,8,4]{1,2,0:T(4,128)}, u32[]{:S(2)}) copy-start(s32[1,8,4]{1,2,0:T(4,128)} %param.25) | copy-start | bytes 388
  7.2 9.1 %copy-start.11 = (bf16[8192]{0:T(1024)(128)(2,1)S(1)}, bf16[8192]{0:T(1024)(128)(2,1)}, u32[]{:S(2)}) copy-start(bf16[8192]{0:T(1024)(128)(2,1)} %param.14) | copy-start | bytes 49156
  7.2 10.0 %copy-start.12 = (s32[256]{0:T(256)S(1)}, s32[256]{0:T(256)}, u32[]{:S(2)}) copy-start(s32[256]{0:T(256)} %param.21) | copy-start | bytes 3076
  7.2 130.7 %all-gather.2.cloned.1.call-start = ((), (), s32[]{:S(2)}) async-start(), calls=%async_computation.1 | async-start | bytes 9437184 | tf_op jit(solution)/shard_map/all_gather | solution.py:157
  7.9 651.5 %reduce-scatter.2.cloned.1.call-start = ((), (), s32[]{:S(2)}) async-start(), calls=%async_computation.2 | async-start | bytes 18874368 | tf_op jit(solution)/shard_map/reduce_scatter | solution.py:207
  8.0 4.3 collective-permute-start
  15.9 5.2 collective-permute-start.1
  33.4 109.6 %copy-start.9 = (f32[8192]{0:T(1024)S(1)}, f32[8192]{0:T(1024)}, u32[]{:S(2)}) copy-start(f32[8192]{0:T(1024)} %convert_element_type.72) | copy-start | bytes 98308
  343.3 0.6 copy-start.3
  343.3 0.6 copy-start.5
  345.4 0.9 copy-start.7
  345.4 1.5 copy-start.2
  345.4 1.5 copy-start.4
  345.4 1.5 copy-start.6
  350.9 2.9 slice-start
  351.7 2.9 slice-start.1
  351.7 2.8 copy-start.8
  353.8 4.4 copy-start.10
  377.7 281.7 %copy-start = (bf16[512,1024]{1,0:T(8,128)(2,1)S(1)}, bf16[512,1024]{1,0:T(8,128)(2,1)}, u32[]{:S(2)}) copy-start(bf16[512,1024]{1,0:T(8,128)(2,1)} %param.13) | copy-start | bytes 3145732
  659.5 21.6 %copy-start.1 = (f32[512,1024]{1,0:T(8,128)S(1)}, f32[512,1024]{1,0:T(8,128)}, u32[]{:S(2)}) copy-start(f32[512,1024]{1,0:T(8,128)} %reduce-scatter.2.cloned.1.call-done) | copy-start | bytes 6291460
Sparse Core Ops, SparseCore 0:
  10.2 127.6 all-gather.1
  377.9 281.5 reduce-scatter.1
where the time goes:
time: 690 us
  waiting for transfers between devices  386 us (56%)
  blocking collectives  185 us (27%)
  matrix products  47.4 us (7%)
  other arithmetic  32.1 us (5%)
  local copies, waits for them, and re-layouts  23.4 us (3%)
  between operations  14.5 us (2%)
    reduce_scatter x1, waiting for transfers between devices, body(): lax.psum_scatter(partial_sum, 'tensor', scatter_dimension=1, tiled=True)  281 us
    psum x1, blocking collectives, body(): summed_pairs = lax.psum(partial_pairs, 'tensor').astype(jnp.bfloat16)  166 us
    all_gather x1, waiting for transfers between devices, body(): full_rows = lax.all_gather(inputs, 'tensor', axis=1, tiled=True)  105 us
    psum x1, blocking collectives, body(): squares = lax.psum(jnp.sum(mixed_sum * mixed_sum, axis=1), 'tensor')  19.5 us
    dot_general x1, matrix products, body(): jnp.dot(context, output_weight, preferred_element_type=jnp.float32)  15.8 us
    dot_general x1, matrix products, body(): jnp.dot(normed, query_weight, preferred_element_type=jnp.float32)  14.3 us
  transfers between devices with their start and end apart: 4, of which 2 were waited for; matrix products, arithmetic and copies ran while one was open for 4% of the time, Pallas kernels for 0%

commit v1 on v0

v1 whole, which is shorter than its diff:
```python
import functools
import math

import jax
import jax.numpy as jnp
import numpy as np
from jax import lax
from jax.experimental import pallas as pl
from jax.experimental.pallas import tpu as pltpu
from jax.sharding import PartitionSpec as P

QUERY_HEADS = 64
KEY_VALUE_HEADS = 8
HEAD_SIZE = 128
EPS = 1e-06
THETA = 1000000.0
NEGATIVE = -1e30
FACTOR = 1.0 / math.sqrt(HEAD_SIZE)

ORDER = (0, 2, 4, 6, 7, 5, 3, 1)
RING = len(ORDER)
PLACE = tuple(ORDER.index(t) for t in range(RING))
FORWARD = [(ORDER[i], ORDER[(i + 1) % RING]) for i in range(RING)]
BACKWARD = [(b, a) for a, b in FORWARD]

VMEM = pltpu.CompilerParams(vmem_limit_bytes=48 * 1024 * 1024)


def dot(left, right):
    return jnp.dot(left, right, preferred_element_type=jnp.float32)


def dot_t(left, right):
    return lax.dot_general(
        left, right, (((1,), (1,)), ((), ())), preferred_element_type=jnp.float32
    )


def turned(values, cosine, sine):
    return values * cosine + pltpu.roll(values, HEAD_SIZE // 2, 1) * sine


def span_layout(lengths, prefix, prefill, page_size):
    request_end = jnp.cumsum(lengths)
    request_start = request_end - lengths
    token_index = jnp.arange(prefill, dtype=jnp.int32)
    request = jnp.sum((token_index[:, None] >= request_end[None, :]).astype(jnp.int32), axis=1)
    onehot = (request[:, None] == jnp.arange(lengths.shape[0], dtype=jnp.int32)[None, :]).astype(
        jnp.int32
    )
    token_start = jnp.sum(onehot * request_start[None, :], axis=1)
    token_prefix = jnp.sum(onehot * prefix[None, :], axis=1)
    return (request, token_prefix * page_size + token_index - token_start)


def tables(positions):
    half_dim = HEAD_SIZE // 2
    frequency = jnp.exp(
        jnp.arange(half_dim, dtype=jnp.float32) * (-2.0 * math.log(THETA) / HEAD_SIZE)
    )
    angles = positions.astype(jnp.float32)[:, None] * frequency[None, :]
    cosine, sine = jnp.cos(angles), jnp.sin(angles)
    return (
        jnp.concatenate([cosine, cosine], axis=1),
        jnp.concatenate([-sine, sine], axis=1),
    )


def pairs_kernel(blocks, x_ref, gain_ref, w_ref, out_ref):
    scaled = (x_ref[...].astype(jnp.float32) * gain_ref[...].astype(jnp.float32)).astype(
        jnp.bfloat16
    )
    out_ref[0] = dot(scaled, w_ref[...])


def pairs_partial(x, gain_row, matrix, blocks, me):
    rows, width = x.shape
    columns = matrix.shape[1] // RING
    return pl.pallas_call(
        pairs_kernel,
        grid_spec=pltpu.PrefetchScalarGridSpec(
            num_scalar_prefetch=1,
            grid=(RING,),
            in_specs=[
                pl.BlockSpec((rows, width), lambda k, b: (0, 0)),
                pl.BlockSpec((1, width), lambda k, b: (0, b[0])),
                pl.BlockSpec((width, columns), lambda k, b: (0, b[k])),
            ],
            out_specs=pl.BlockSpec((1, rows, columns), lambda k, b: (k, 0, 0)),
        ),
        out_shape=jax.ShapeDtypeStruct((RING, rows, columns), jnp.float32),
        compiler_params=VMEM,
        name="pairs_partial",
    )(blocks, x, gain_row, matrix)


def add_kernel(arrived_ref, part_ref, out_ref):
    out_ref[...] = (arrived_ref[...].astype(jnp.float32) + part_ref[0]).astype(out_ref.dtype)


def add_part(arrived, parts, k, half, dtype=jnp.bfloat16):
    rows, columns = arrived.shape
    return pl.pallas_call(
        add_kernel,
        grid=(1,),
        in_specs=[
            pl.BlockSpec((rows, columns), lambda i: (0, 0)),
            pl.BlockSpec((1, rows, columns), lambda i: (k, half, 0)),
        ],
        out_specs=pl.BlockSpec((rows, columns), lambda i: (0, 0)),
        out_shape=jax.ShapeDtypeStruct((rows, columns), dtype),
        compiler_params=VMEM,
        name="add_part",
    )(arrived, parts)


def last_kernel(arrived_ref, part_ref, x_ref, mixed_ref, hidden_ref, square_ref):
    mixed = x_ref[...].astype(jnp.float32) + (arrived_ref[...].astype(jnp.float32) + part_ref[0])
    mixed_ref[...] = mixed
    hidden_ref[...] = mixed.astype(jnp.bfloat16)
    square_ref[...] = jnp.sum(mixed * mixed, axis=1, keepdims=True)


def last_part(arrived, parts, half, x):
    rows, columns = arrived.shape
    flat = pl.BlockSpec((rows, columns), lambda i: (0, 0))
    return pl.pallas_call(
        last_kernel,
        grid=(1,),
        in_specs=[flat, pl.BlockSpec((1, rows, columns), lambda i: (0, half, 0)), flat],
        out_specs=[flat, flat, pl.BlockSpec((rows, 1), lambda i: (0, 0))],
        out_shape=[
            jax.ShapeDtypeStruct((rows, columns), jnp.float32),
            jax.ShapeDtypeStruct((rows, columns), jnp.bfloat16),
            jax.ShapeDtypeStruct((rows, 1), jnp.float32),
        ],
        compiler_params=VMEM,
        name="last_part",
    )(arrived, parts, x)


def query_kernel(width, blocks, *refs):
    pieces, (gain_ref, w_ref, cos_ref, sin_ref) = refs[: 2 * RING], refs[2 * RING : 2 * RING + 4]
    q_ref, inv_ref, scaled, total, squares = refs[2 * RING + 4 :]
    step = pl.program_id(0)
    half = pieces[0].shape[0]
    gain = gain_ref[...].astype(jnp.float32)

    @pl.when(step == 0)
    def _():
        total[...] = jnp.zeros_like(total)
        squares[...] = jnp.zeros_like(squares)

    for k in range(RING):

        @pl.when(step == k)
        def _(k=k):
            for side, piece in enumerate((pieces[(RING - k) % RING], pieces[RING + k])):
                rows = slice(side * half, (side + 1) * half)
                values = piece[...].astype(jnp.float32)
                squares[rows] += jnp.sum(values * values, axis=1, keepdims=True)
                scaled[rows] = (values * gain).astype(jnp.bfloat16)

    total[...] += dot(scaled[...], w_ref[...])

    @pl.when(step == RING - 1)
    def _():
        inv = lax.rsqrt(squares[...] / width + EPS)
        inv_ref[...] = inv
        for head in range(q_ref.shape[1] // HEAD_SIZE):
            at = slice(head * HEAD_SIZE, (head + 1) * HEAD_SIZE)
            q_ref[:, at] = turned(total[:, at] * inv, cos_ref[...], sin_ref[...]).astype(
                jnp.bfloat16
            )


def query_rows(forward, backward, gain_row, weight, cosine, sine, blocks):
    half, depth = forward[0].shape
    rows, width = 2 * half, weight.shape[1]
    whole = pl.BlockSpec((half, depth), lambda k, b: (0, 0), pipeline_mode=pl.Buffered(1))
    table = pl.BlockSpec((rows, HEAD_SIZE), lambda k, b: (0, 0))
    return pl.pallas_call(
        functools.partial(query_kernel, weight.shape[0]),
        grid_spec=pltpu.PrefetchScalarGridSpec(
            num_scalar_prefetch=1,
            grid=(RING,),
            in_specs=[whole] * (2 * RING)
            + [
                pl.BlockSpec((1, depth), lambda k, b: (0, b[k])),
                pl.BlockSpec((depth, width), lambda k, b: (b[k], 0)),
                table,
                table,
            ],
            out_specs=[
                pl.BlockSpec((rows, width), lambda k, b: (0, 0)),
                pl.BlockSpec((rows, 1), lambda k, b: (0, 0)),
            ],
            scratch_shapes=[
                pltpu.VMEM((rows, depth), jnp.bfloat16),
                pltpu.VMEM((rows, width), jnp.float32),
                pltpu.VMEM((rows, 1), jnp.float32),
            ],
        ),
        out_shape=[
            jax.ShapeDtypeStruct((rows, width), jnp.bfloat16),
            jax.ShapeDtypeStruct((rows, 1), jnp.float32),
        ],
        compiler_params=VMEM,
        name="query_rows",
    )(blocks, *forward, *backward, gain_row, weight, cosine, sine)


def new_pairs(pairs_ref, inv_ref, cos_ref, sin_ref):
    pairs = (pairs_ref[...] * inv_ref[...]).astype(jnp.bfloat16)
    keys = turned(pairs[:, :HEAD_SIZE].astype(jnp.float32), cos_ref[...], sin_ref[...])
    return keys.astype(jnp.bfloat16), pairs[:, HEAD_SIZE:]


def decode_kernel(
    page_size, q_ref, cache_ref, pairs_ref, inv_ref, cos_ref, sin_ref, page_ref, pos_ref,
    out_ref, count, new_key, new_value,
):
    @pl.when(pl.program_id(0) == 0)
    def _():
        token = lax.broadcasted_iota(jnp.int32, count.shape, 1)
        page, offset = token // page_size, token % page_size
        times = jnp.zeros(count.shape, jnp.float32)
        for j in range(page_ref.shape[1]):
            hit = (page == page_ref[:, j : j + 1]) & (offset + j * page_size < pos_ref[...])
            times += jnp.where(hit, 1.0, 0.0)
        count[...] = times
        keys, values = new_pairs(pairs_ref, inv_ref, cos_ref, sin_ref)
        new_key[...] = keys.astype(jnp.float32)
        new_value[...] = values.astype(jnp.float32)

    q = q_ref[...]
    times = count[...]
    score = jnp.where(times > 0, dot_t(q, cache_ref[:, :HEAD_SIZE]) * FACTOR, NEGATIVE)
    own = jnp.sum(q.astype(jnp.float32) * new_key[...], axis=1, keepdims=True) * FACTOR
    peak = jnp.maximum(jnp.max(score, axis=1, keepdims=True), own)
    grown, grown_own = jnp.exp(score - peak), jnp.exp(own - peak)
    scale = 1.0 / (jnp.sum(grown * times, axis=1, keepdims=True) + grown_own)
    weight = (grown * scale).astype(jnp.bfloat16).astype(jnp.float32) * times
    weight_own = (grown_own * scale).astype(jnp.bfloat16).astype(jnp.float32)
    context = dot(weight.astype(jnp.bfloat16), cache_ref[:, HEAD_SIZE:])
    out_ref[...] = (context + weight_own * new_value[...]).astype(jnp.bfloat16)


def decode_context(q, cache, pairs, inv, cosine, sine, page_table, positions, page_size):
    rows, width = q.shape
    tokens = cache.shape[0]
    whole = lambda array: pl.BlockSpec(array.shape, lambda h: (0, 0))
    head = pl.BlockSpec((rows, HEAD_SIZE), lambda h: (0, h))
    return pl.pallas_call(
        functools.partial(decode_kernel, page_size),
        grid=(width // HEAD_SIZE,),
        in_specs=[head]
        + [whole(a) for a in (cache, pairs, inv, cosine, sine, page_table, positions)],
        out_specs=head,
        scratch_shapes=[
            pltpu.VMEM((rows, tokens), jnp.float32),
            pltpu.VMEM((rows, HEAD_SIZE), jnp.float32),
            pltpu.VMEM((rows, HEAD_SIZE), jnp.float32),
        ],
        out_shape=jax.ShapeDtypeStruct((rows, width), jnp.bfloat16),
        compiler_params=VMEM,
        name="decode_context",
    )(q, cache, pairs, inv, cosine, sine, page_table, positions)


def prefill_kernel(
    q_ref, prefix_ref, pairs_ref, inv_ref, cos_ref, sin_ref, request_ref, column_ref, owner_ref,
    out_ref, bias, keys, values,
):
    old = prefix_ref.shape[0]

    @pl.when(pl.program_id(0) == 0)
    def _():
        rows = request_ref.shape[0]
        request = request_ref[...]
        bias[:, :old] = jnp.where(request == owner_ref[...], 0.0, NEGATIVE)
        row = lax.broadcasted_iota(jnp.int32, (rows, rows), 0)
        column = lax.broadcasted_iota(jnp.int32, (rows, rows), 1)
        allowed = (request == column_ref[...]) & (column <= row)
        bias[:, old:] = jnp.where(allowed, 0.0, NEGATIVE)
        new_keys, new_values = new_pairs(pairs_ref, inv_ref, cos_ref, sin_ref)
        keys[:old] = prefix_ref[:, :HEAD_SIZE]
        keys[old:] = new_keys
        values[:old] = prefix_ref[:, HEAD_SIZE:]
        values[old:] = new_values

    score = dot_t(q_ref[...], keys[...]) * FACTOR + bias[...]
    grown = jnp.exp(score - jnp.max(score, axis=1, keepdims=True))
    scale = 1.0 / jnp.sum(grown, axis=1, keepdims=True)
    weight = (grown * scale).astype(jnp.bfloat16)
    out_ref[...] = dot(weight, values[...]).astype(jnp.bfloat16)


def prefill_context(q, prefix, pairs, inv, cosine, sine, request, owner):
    rows, width = q.shape
    tokens = prefix.shape[0] + rows
    operands = (prefix, pairs, inv, cosine, sine, request[:, None], request[None, :], owner[None, :])
    head = pl.BlockSpec((rows, HEAD_SIZE), lambda h: (0, h))
    return pl.pallas_call(
        prefill_kernel,
        grid=(width // HEAD_SIZE,),
        in_specs=[head] + [pl.BlockSpec(a.shape, lambda h: (0, 0)) for a in operands],
        out_specs=head,
        scratch_shapes=[
            pltpu.VMEM((rows, tokens), jnp.float32),
            pltpu.VMEM((tokens, HEAD_SIZE), jnp.bfloat16),
            pltpu.VMEM((tokens, HEAD_SIZE), jnp.bfloat16),
        ],
        out_shape=jax.ShapeDtypeStruct((rows, width), jnp.bfloat16),
        compiler_params=VMEM,
        name="prefill_context",
    )(q, *operands)


def output_kernel(blocks, context_ref, w_ref, out_ref):
    out_ref[0] = dot(context_ref[...], w_ref[...])


def output_partial(context, weight, blocks):
    rows, depth = context.shape
    columns = weight.shape[1] // RING
    return pl.pallas_call(
        output_kernel,
        grid_spec=pltpu.PrefetchScalarGridSpec(
            num_scalar_prefetch=1,
            grid=(RING,),
            in_specs=[
                pl.BlockSpec((rows, depth), lambda k, b: (0, 0)),
                pl.BlockSpec((depth, columns), lambda k, b: (0, b[k])),
            ],
            out_specs=pl.BlockSpec((1, rows, columns), lambda k, b: (k, 0, 0)),
        ),
        out_shape=jax.ShapeDtypeStruct((RING, rows, columns), jnp.float32),
        compiler_params=VMEM,
        name="output_partial",
    )(blocks, context, weight)


def gather_ring(piece, route):
    pieces = [piece]
    for _ in range(RING - 1):
        pieces.append(lax.ppermute(pieces[-1], "tensor", route))
    return pieces


def first_part(parts, k, half, rows):
    return parts[k, half * rows : (half + 1) * rows].astype(jnp.bfloat16)


def scatter_ring(parts, half, rows, last):
    route = BACKWARD if half else FORWARD
    places = range(1, RING) if half else range(RING - 1, 0, -1)
    running = None
    for k in places:
        if running is None:
            running = first_part(parts, k, half, rows)
        else:
            running = add_part(running, parts, k, half)
        running = lax.ppermute(running, "tensor", route)
    return last(running)


def sum_squares(squares):
    for low in (1, 2, 4):
        squares = squares + lax.ppermute(
            squares, "tensor", [(t, t ^ low) for t in range(RING)]
        )
    return squares


def body(
    inputs,
    entry_gain,
    exit_gain,
    query_weight,
    key_value_matrix,
    output_weight,
    page_pool,
    page_table,
    positions,
    request_lengths,
    prefix_pages,
    source_pages,
    target_pages,
):
    decode = page_table.shape[0]
    prefill = inputs.shape[0] - decode
    page_count, page_size, _ = page_pool.shape
    me = lax.axis_index("tensor")
    width = inputs.shape[1]
    per_device = query_weight.shape[1] // HEAD_SIZE
    group = me * per_device // (QUERY_HEADS // KEY_VALUE_HEADS)
    pair = 2 * HEAD_SIZE

    own_pool = lax.dynamic_slice_in_dim(page_pool, group * pair, pair, 2)
    peer_pool = lax.ppermute(own_pool, "replica", [(0, 1), (1, 0)])
    prefix = prefix_pages[0]
    page_max = target_pages.shape[2]
    arrived = peer_pool[source_pages.reshape(-1)]
    usable = jnp.arange(page_max, dtype=jnp.int32)[None, :] < prefix[:, None]
    target = jnp.where(usable.reshape(-1), target_pages.reshape(-1), page_count)
    cache = own_pool.at[target].set(arrived, mode="drop").reshape(-1, pair)
    prefix_rows = arrived.reshape(-1, pair)
    slots = jnp.where(usable, jnp.arange(prefix.shape[0], dtype=jnp.int32)[:, None], -1)
    owner = jnp.repeat(slots.reshape(-1), page_size)

    request, span = span_layout(request_lengths[0], prefix, prefill, page_size)
    cosine, sine = tables(jnp.concatenate([span, positions]))
    gain_row = entry_gain[None, :]
    spans = (slice(0, prefill), slice(prefill, prefill + decode))

    def attend(which, q, pairs, inv):
        at = spans[which]
        if which == 0:
            return prefill_context(
                q, prefix_rows, pairs, inv, cosine[at], sine[at], request, owner
            )
        return decode_context(
            q, cache, pairs, inv, cosine[at], sine[at], page_table, positions[:, None], page_size
        )

    exit_row = lax.dynamic_slice_in_dim(exit_gain, me * width, width, 0).astype(jnp.float32)

    def normed(mixed, squares):
        inv = lax.rsqrt(squares / exit_gain.shape[0] + EPS)
        return (mixed * inv * exit_row[None, :]).astype(jnp.bfloat16)

    if lax.axis_size("tensor") == RING:
        blocks = jnp.asarray(ORDER, jnp.int32)[
            (jnp.asarray(PLACE, jnp.int32)[me] + jnp.arange(RING)) % RING
        ]
        parts = pairs_partial(inputs, gain_row, key_value_matrix, blocks, me)
        pairs = [
            scatter_ring(
                parts, which, prefill, lambda r, w=which: add_part(r, parts, 0, w, jnp.float32)
            )
            for which in (0, 1)
        ]
        half = prefill // 2
        hidden, out = [None, None], [None, None]
        for which in (1, 0):
            low = spans[which].start
            ahead, back = inputs[low : low + half], inputs[low + half : low + 2 * half]
            at = spans[which]
            q, inv = query_rows(
                gather_ring(ahead, FORWARD), gather_ring(back, BACKWARD),
                gain_row, query_weight, cosine[at], sine[at], blocks,
            )
            context = attend(which, q, pairs[which], inv)
            partial = output_partial(context, output_weight, blocks)
            sides = [
                scatter_ring(
                    partial, side, half, lambda r, s=side, x=x: last_part(r, partial, s, x)
                )
                for side, x in enumerate((ahead, back))
            ]
            mixed, kept, squares = [jnp.concatenate(both, axis=0) for both in zip(*sides)]
            hidden[which] = kept
            out[which] = normed(mixed, sum_squares(squares[:, 0])[:, None])
        return jnp.concatenate(hidden, axis=0), jnp.concatenate(out, axis=0)

    rows = lax.all_gather(inputs, "tensor", axis=1, tiled=True).astype(jnp.float32)
    inv = lax.rsqrt(jnp.mean(rows * rows, axis=1, keepdims=True) + EPS)
    scaled = (rows * inv * entry_gain.astype(jnp.float32)).astype(jnp.bfloat16)
    own = lax.dynamic_slice_in_dim(scaled, me * width, width, 1)
    pairs = lax.psum(dot(own, key_value_matrix), "tensor")
    pairs = lax.dynamic_slice_in_dim(pairs, group * pair, pair, 1)
    q = dot(scaled, query_weight).reshape(-1, per_device, HEAD_SIZE)
    swapped = jnp.roll(q, HEAD_SIZE // 2, 2)
    q = (q * cosine[:, None] + swapped * sine[:, None]).astype(jnp.bfloat16)
    q = q.reshape(-1, per_device * HEAD_SIZE)
    one = jnp.ones_like(inv)
    context = jnp.concatenate([attend(w, q[spans[w]], pairs[spans[w]], one[spans[w]]) for w in (0, 1)])
    summed = lax.psum_scatter(
        dot(context, output_weight), "tensor", scatter_dimension=1, tiled=True
    )
    mixed = inputs.astype(jnp.float32) + summed
    squares = lax.psum(jnp.sum(mixed * mixed, axis=1), "tensor")[:, None]
    return mixed.astype(jnp.bfloat16), normed(mixed, squares)


def solution(mesh):
    rows = ("groups", "replica")
    return jax.shard_map(
        body,
        mesh=mesh,
        in_specs=(
            P(rows, "tensor"),
            P(),
            P(),
            P(None, "tensor"),
            P("tensor", None),
            P("tensor", None),
            P(rows, None, None),
            P(rows, None),
            P(rows),
            P(rows, None),
            P(rows, None),
            P(rows, None, None),
            P(rows, None, None),
        ),
        out_specs=(P(rows, "tensor"), P(rows, "tensor")),
        check_vma=False,
    )
```

time: 690 us -> 300 us (0.43)
  waiting for transfers between devices: 386 us -> 65.7 us
  blocking collectives: 185 us -> 0 us
  Pallas kernels: 0 us -> 112 us
  starting transfers between devices: 0.72 us -> 80.2 us
  matrix products: 47.4 us -> 0 us
  other arithmetic: 32.1 us -> 15.7 us
  between operations: 14.5 us -> 1.39 us
    reduce_scatter x1 -> x0, waiting for transfers between devices: 281 us -> none  [body(): lax.psum_scatter(partial_sum, 'tensor', scatter_dimension=1, tiled=True)]
    psum x2 -> x0, blocking collectives: 185 us -> none  [the longest x1 166 us: body(): summed_pairs = lax.psum(partial_pairs, 'tensor').astype(jnp.bfloat16)]
    pallas_call x0 -> x49, Pallas kernels: none -> 112 us  [the longest x38 28.8 us: add_part(): pl.pallas_call(add_kernel, grid=(1,), in_specs=[pl.BlockSpec((rows, colum...]
    all_gather x1 -> x0, waiting for transfers between devices: 105 us -> none  [body(): full_rows = lax.all_gather(inputs, 'tensor', axis=1, tiled=True)]
    ppermute x2 -> x77, starting transfers between devices: 0.64 us -> 80.2 us  [the longest x42 44.1 us: scatter_ring(): running = lax.ppermute(running, 'tensor', route)]
    ppermute x2 -> x77, waiting for transfers between devices: 0.01 us -> 65.7 us  [the longest x42 44.6 us: scatter_ring(): running = lax.ppermute(running, 'tensor', route)]
    dot_general x9 -> x0, matrix products: 47.4 us -> none  [the longest x1 15.8 us: body(): jnp.dot(context, output_weight, preferred_element_type=jnp.float32)]
    convert_element_type x7 -> x3, other arithmetic: 13.6 us -> 0.94 us  [the longest x1 0.68 us: body(): lax.dynamic_slice_in_dim(exit_gain, me * width, width, 0)]
  transfers between devices with their start and end apart: 4 -> 77, of which waited for: 2 -> 31; matrix products, arithmetic and copies ran while one was open for 4% -> 7% of each run, Pallas kernels for 0% -> 35%
where the time goes in v1:
time: 300 us; the launch traced here: 297 us
  Pallas kernels  112 us (37%)
  starting transfers between devices  80.2 us (27%)
  waiting for transfers between devices  65.7 us (22%)
  local copies, waits for them, and re-layouts  21.7 us (7%)
  other arithmetic  15.7 us (5%)
    ppermute x42, waiting for transfers between devices, scatter_ring(): running = lax.ppermute(running, 'tensor', route)  44.6 us
    ppermute x42, starting transfers between devices, scatter_ring(): running = lax.ppermute(running, 'tensor', route)  44.1 us
    pallas_call x38, Pallas kernels, add_part(): pl.pallas_call(add_kernel, grid=(1,), in_specs=[pl.BlockSpec((rows, colum...  28.8 us
    ppermute x28, starting transfers between devices, gather_ring(): pieces.append(lax.ppermute(pieces[-1], 'tensor', route))  28.7 us
    pallas_call x2, Pallas kernels, output_partial(): pl.pallas_call(output_kernel, grid_spec=pltpu.PrefetchScalarGridSpec(num_...  27.6 us
    pallas_call x2, Pallas kernels, query_rows(): pl.pallas_call(functools.partial(query_kernel, weight.shape[0]), grid_spe...  26.2 us
    ppermute x28, waiting for transfers between devices, gather_ring(): pieces.append(lax.ppermute(pieces[-1], 'tensor', route))  17.6 us
    unnamed x95, local copies, waits for them, and re-layouts  12.9 us
  transfers between devices with their start and end apart: 77, of which 31 were waited for; matrix products, arithmetic and copies ran while one was open for 7% of the time, Pallas kernels for 35%

profile of v1, /device:TPU:0, one launch (start us, length us, event | category | flops | bytes accessed | tf_op | source)
XLA Modules:
  0.0 297.2 jit_solution(8779494263491588151)
XLA Ops:
  5.8 7.1 %pairs_partial.1.part_ref = f32[8,512,256]{2,1,0:T(8,128)S(1)} custom-call(s32[8]{0:T(128)S(1)} %gather_fusion, bf16[512,1024]{1,0:T(8,128)(2,1)S(1)} %copy-done.5, bf16[1,8192]{1,0:T(2,128)(2,1)S(1)} %broadcast_in_dim.22.refs_16_.gain_ref, bf16[1024,2048]{1,0:T(8,128)(2,1)} %w_ref.3), custom_call_target="tpu_custom_call" | custom-call | tf_op jit(solution)/shard_map/pairs_partial/pallas_call | solution.py:79
  13.2 3.1 %collective-permute-start.15 = (bf16[256,256]{1,0:T(8,128)(2,1)S(1)}, bf16[256,256]{1,0:T(8,128)(2,1)S(1)}, u32[]{:S(2)}, u32[]{:S(2)}) collective-permute-start(bf16[256,256]{1,0:T(8,128)(2,1)S(1)} %get-tuple-element.40), channel_id=1, source_target_pairs={{0,4},{4,8},{8,12},{12,14},{14,10},{10,6},{6,2},{2,0},{1,5},{5,9},... | collective-permute-start | bytes 393224 | tf_op jit(solution)/shard_map/ppermute | solution.py:364
  16.4 2.0 collective-permute-start.7
  22.8 6.9 %collective-permute-done.16.arrived_ref = bf16[256,256]{1,0:T(8,128)(2,1)S(1)} collective-permute-done((bf16[256,256]{1,0:T(8,128)(2,1)S(1)}, bf16[256,256]{1,0:T(8,128)(2,1)S(1)}, u32[]{:S(2)}, u32[]{:S(2)}) %collective-permute-start.16) | collective-permute-done | bytes 131104 | tf_op jit(solution)/shard_map/ppermute | solution.py:364
  30.4 2.2 copy-done.1
  32.6 2.7 collective-permute-done.51.arrived_ref
  37.7 1.7 collective-permute-start.37
  39.8 1.8 collective-permute-done.17.arrived_ref
  43.2 2.2 copy-done.2
  49.9 4.0 %collective-permute-done.18.arrived_ref = bf16[256,256]{1,0:T(8,128)(2,1)S(1)} collective-permute-done((bf16[256,256]{1,0:T(8,128)(2,1)S(1)}, bf16[256,256]{1,0:T(8,128)(2,1)S(1)}, u32[]{:S(2)}, u32[]{:S(2)}) %collective-permute-start.18) | collective-permute-done | bytes 131104 | tf_op jit(solution)/shard_map/ppermute | solution.py:364
  55.4 2.0 collective-permute-done.53.arrived_ref
  59.6 3.9 %collective-permute-done.19.arrived_ref = bf16[256,256]{1,0:T(8,128)(2,1)S(1)} collective-permute-done((bf16[256,256]{1,0:T(8,128)(2,1)S(1)}, bf16[256,256]{1,0:T(8,128)(2,1)S(1)}, u32[]{:S(2)}, u32[]{:S(2)}) %collective-permute-start.19) | collective-permute-done | bytes 131104 | tf_op jit(solution)/shard_map/ppermute | solution.py:364
  68.4 4.3 %collective-permute-done.9.refs_11_ = bf16[128,1024]{1,0:T(8,128)(2,1)S(1)} collective-permute-done((bf16[128,1024]{1,0:T(8,128)(2,1)S(1)}, bf16[128,1024]{1,0:T(8,128)(2,1)S(1)}, u32[]{:S(2)}, u32[]{:S(2)}) %collective-permute-start.9) | collective-permute-done | bytes 262176 | tf_op jit(solution)/shard_map/ppermute | solution.py:347
  75.5 2.8 collective-permute-done.46.refs_12_
  81.2 1.9 fusion.6
  86.9 2.8 collective-permute-done.47.refs_13_
  93.0 2.2 copy-done.3
  95.9 6.4 %collective-permute-done.55.arrived_ref = bf16[256,256]{1,0:T(8,128)(2,1)S(1)} collective-permute-done((bf16[256,256]{1,0:T(8,128)(2,1)S(1)}, bf16[256,256]{1,0:T(8,128)(2,1)S(1)}, u32[]{:S(2)}, u32[]{:S(2)}) %collective-permute-start.55) | collective-permute-done | bytes 131104 | tf_op jit(solution)/shard_map/ppermute | solution.py:364
  109.5 4.0 %collective-permute-done.12.refs_14_ = bf16[128,1024]{1,0:T(8,128)(2,1)} collective-permute-done((bf16[128,1024]{1,0:T(8,128)(2,1)}, bf16[128,1024]{1,0:T(8,128)(2,1)}, u32[]{:S(2)}, u32[]{:S(2)}) %collective-permute-start.12) | collective-permute-done | bytes 262176 | tf_op jit(solution)/shard_map/ppermute | solution.py:347
  119.9 2.2 copy-done.4
  123.6 13.1 %query_rows.3 = (bf16[256,1024]{1,0:T(8,128)(2,1)S(1)}, f32[256,1]{1,0:T(8,128)S(1)}) custom-call(s32[8]{0:T(128)S(1)} %gather_fusion, bf16[128,1024]{1,0:T(8,128)(2,1)S(1)} %get-tuple-element.45.refs_0_.x_ref, bf16[128,1024]{1,0:T(8,128)(2,1)S(1)} %copy-done.11, bf16[128,1024]{1,0:T(8,128)(2,1)} %collective-permute-done.37.refs_2_, ...), custom_call_target="tpu_custom_call" | custom-call | tf_op jit(solution)/shard_map/query_rows/pallas_call | solution.py:182
  136.7 11.3 %decode_context.1.context_ref = bf16[256,1024]{1,0:T(8,128)(2,1)S(1)} custom-call(bf16[256,1024]{1,0:T(8,128)(2,1)S(1)} %get-tuple-element.22.q_ref, bf16[1536,256]{1,0:T(8,128)(2,1)S(1)} %bitcast.36, f32[256,256]{1,0:T(8,128)S(1)} %add_part.63.pairs_ref, f32[256,1]{1,0:T(8,128)S(1)} %get-tuple-element.23.inv_ref, ...), custom_call_target="tpu_custom_call" | custom-call | tf_op jit(solution)/shard_map/decode_context/pallas_call | solution.py:254
  148.0 13.8 %output_partial.3.part_ref = f32[8,256,1024]{2,1,0:T(8,128)} custom-call(s32[8]{0:T(128)S(1)} %gather_fusion, bf16[256,1024]{1,0:T(8,128)(2,1)S(1)} %decode_context.1.context_ref, bf16[1024,8192]{1,0:T(8,128)(2,1)} %w_ref.5), custom_call_target="tpu_custom_call" | custom-call | tf_op jit(solution)/shard_map/output_partial/pallas_call | solution.py:327
  161.8 4.2 %convert.14 = bf16[8,256,1024]{2,1,0:T(8,128)(2,1)S(1)} convert(f32[8,256,1024]{2,1,0:T(8,128)} %output_partial.3.part_ref) | non-fusion elementwise | flops 2097152 | bytes 12582912 | tf_op jit(solution)/shard_map/convert.1
  168.2 13.1 %query_rows.2 = (bf16[256,1024]{1,0:T(8,128)(2,1)S(1)}, f32[256,1]{1,0:T(8,128)S(1)}) custom-call(s32[8]{0:T(128)S(1)} %gather_fusion, bf16[128,1024]{1,0:T(8,128)(2,1)S(1)} %get-tuple-element.43.refs_0_.x_ref, bf16[128,1024]{1,0:T(8,128)(2,1)S(1)} %copy-done.7, bf16[128,1024]{1,0:T(8,128)(2,1)S(1)} %copy-done.17, bf16[128,1024]{1,0:T(8,128)(2,1)S(1)} %copy-done.23, ...), custom_call_target="tpu_custom_call" | custom-call | tf_op jit(solution)/shard_map/query_rows/pallas_call | solution.py:182
  181.3 6.4 %prefill_context.1.context_ref = bf16[256,1024]{1,0:T(8,128)(2,1)S(1)} custom-call(bf16[256,1024]{1,0:T(8,128)(2,1)S(1)} %get-tuple-element.18.q_ref, bf16[512,256]{1,0:T(8,128)(2,1)S(1)} %bitcast.37, f32[256,256]{1,0:T(8,128)S(1)} %add_part.44.pairs_ref, f32[256,1]{1,0:T(8,128)S(1)} %get-tuple-element.19.inv_ref, ...), custom_call_target="tpu_custom_call" | custom-call | tf_op jit(solution)/shard_map/prefill_context/pallas_call | solution.py:304
  187.7 13.8 %output_partial.2.part_ref = f32[8,256,1024]{2,1,0:T(8,128)} custom-call(s32[8]{0:T(128)S(1)} %gather_fusion, bf16[256,1024]{1,0:T(8,128)(2,1)S(1)} %prefill_context.1.context_ref, bf16[1024,8192]{1,0:T(8,128)(2,1)} %w_ref.5), custom_call_target="tpu_custom_call" | custom-call | tf_op jit(solution)/shard_map/output_partial/pallas_call | solution.py:327
  201.6 4.0 %convert.13 = bf16[8,256,1024]{2,1,0:T(8,128)(2,1)S(1)} convert(f32[8,256,1024]{2,1,0:T(8,128)} %output_partial.2.part_ref) | non-fusion elementwise | flops 2097152 | bytes 12582912 | tf_op jit(solution)/shard_map/convert.4
  210.4 1.9 collective-permute-start.58
  212.3 2.0 collective-permute-done.29.arrived_ref
  289.4 2.0 pad_maximum_fusion
  292.8 3.0 %collective-permute-done.73 = f32[256]{0:T(256)S(1)} collective-permute-done((f32[256]{0:T(256)S(1)}, f32[256]{0:T(256)S(1)}, u32[]{:S(2)}, u32[]{:S(2)}) %collective-permute-start.73) | collective-permute-done | bytes 1056 | tf_op jit(solution)/shard_map/ppermute | solution.py:370
  (319 shorter events, 141.1 us)
Async XLA Ops:
  16.4 20.5 %collective-permute-start.7 = (bf16[128,1024]{1,0:T(8,128)(2,1)S(1)}, bf16[128,1024]{1,0:T(8,128)(2,1)S(1)}, u32[]{:S(2)}, u32[]{:S(2)}) collective-permute-start(bf16[128,1024]{1,0:T(8,128)(2,1)S(1)} %get-tuple-element.42.refs_8_.x_ref), channel_id=1, source_target_pairs={{4,0},{8,4},{12,8},{14,12},{10,14},{6,10},{2,6},{0,2},{5,1},{9,5},... | collective-permute-start | bytes 786440 | tf_op jit(solution)/shard_map/ppermute | solution.py:347
  18.4 19.0 %collective-permute-start.43 = (bf16[128,1024]{1,0:T(8,128)(2,1)S(1)}, bf16[128,1024]{1,0:T(8,128)(2,1)S(1)}, u32[]{:S(2)}, u32[]{:S(2)}) collective-permute-start(bf16[128,1024]{1,0:T(8,128)(2,1)S(1)} %get-tuple-element.44.refs_8_.x_ref), channel_id=1, source_target_pairs={{4,0},{8,4},{12,8},{14,12},{10,14},{6,10},{2,6},{0,2},{5,1},{9,5},... | collective-permute-start | bytes 786440 | tf_op jit(solution)/shard_map/ppermute | solution.py:347
  20.0 17.7 %collective-permute-start.36 = (bf16[128,1024]{1,0:T(8,128)(2,1)S(1)}, bf16[128,1024]{1,0:T(8,128)(2,1)S(1)}, u32[]{:S(2)}, u32[]{:S(2)}) collective-permute-start(bf16[128,1024]{1,0:T(8,128)(2,1)S(1)} %get-tuple-element.45.refs_0_.x_ref), channel_id=1, source_target_pairs={{0,4},{4,8},{8,12},{12,14},{14,10},{10,6},{6,2},{2,0},{1,5},{5,9},... | collective-permute-start | bytes 786440 | tf_op jit(solution)/shard_map/ppermute | solution.py:347
  22.7 12.5 %collective-permute-start.51 = (bf16[256,256]{1,0:T(8,128)(2,1)S(1)}, bf16[256,256]{1,0:T(8,128)(2,1)S(1)}, u32[]{:S(2)}, u32[]{:S(2)}) collective-permute-start(bf16[256,256]{1,0:T(8,128)(2,1)S(1)} %add_part.57), channel_id=1, source_target_pairs={{4,0},{8,4},{12,8},{14,12},{10,14},{6,10},{2,6},{0,2},{5,1},{9,5},... | collective-permute-start | bytes 393224 | tf_op jit(solution)/shard_map/ppermute | solution.py:364
  37.4 11.6 %collective-permute-start.44 = (bf16[128,1024]{1,0:T(8,128)(2,1)S(1)}, bf16[128,1024]{1,0:T(8,128)(2,1)S(1)}, u32[]{:S(2)}, u32[]{:S(2)}) collective-permute-start(bf16[128,1024]{1,0:T(8,128)(2,1)S(1)} %collective-permute-done.43.refs_9_), channel_id=1, source_target_pairs={{4,0},{8,4},{12,8},{14,12},{10,14},{6,10},{2,6},{0,2},{5,1},{9,5},... | collective-permute-start | bytes 786440 | tf_op jit(solution)/shard_map/ppermute | solution.py:347
  37.7 11.8 %collective-permute-start.37 = (bf16[128,1024]{1,0:T(8,128)(2,1)S(1)}, bf16[128,1024]{1,0:T(8,128)(2,1)}, u32[]{:S(2)}, u32[]{:S(2)}) collective-permute-start(bf16[128,1024]{1,0:T(8,128)(2,1)S(1)} %collective-permute-done.36.refs_1_), channel_id=1, source_target_pairs={{0,4},{4,8},{8,12},{12,14},{14,10},{10,6},{6,2},{2,0},{1,5},{5,9},... | collective-permute-start | bytes 786440 | tf_op jit(solution)/shard_map/ppermute | solution.py:347
  39.5 18.0 %collective-permute-start.8 = (bf16[128,1024]{1,0:T(8,128)(2,1)S(1)}, bf16[128,1024]{1,0:T(8,128)(2,1)S(1)}, u32[]{:S(2)}, u32[]{:S(2)}) collective-permute-start(bf16[128,1024]{1,0:T(8,128)(2,1)S(1)} %collective-permute-done.7.refs_9_), channel_id=1, source_target_pairs={{4,0},{8,4},{12,8},{14,12},{10,14},{6,10},{2,6},{0,2},{5,1},{9,5},... | collective-permute-start | bytes 786440 | tf_op jit(solution)/shard_map/ppermute | solution.py:347
  41.6 17.6 %collective-permute-start.1 = (bf16[128,1024]{1,0:T(8,128)(2,1)S(1)}, bf16[128,1024]{1,0:T(8,128)(2,1)S(1)}, u32[]{:S(2)}, u32[]{:S(2)}) collective-permute-start(bf16[128,1024]{1,0:T(8,128)(2,1)S(1)} %collective-permute-done.refs_1_), channel_id=1, source_target_pairs={{0,4},{4,8},{8,12},{12,14},{14,10},{10,6},{6,2},{2,0},{1,5},{5,9},... | collective-permute-start | bytes 786440 | tf_op jit(solution)/shard_map/ppermute | solution.py:347
  49.5 16.7 %collective-permute-start.45 = (bf16[128,1024]{1,0:T(8,128)(2,1)S(1)}, bf16[128,1024]{1,0:T(8,128)(2,1)S(1)}, u32[]{:S(2)}, u32[]{:S(2)}) collective-permute-start(bf16[128,1024]{1,0:T(8,128)(2,1)S(1)} %collective-permute-done.44.refs_10_), channel_id=1, source_target_pairs={{4,0},{8,4},{12,8},{14,12},{10,14},{6,10},{2,6},{0,2},{5,1},{9,5},... | collective-permute-start | bytes 786440 | tf_op jit(solution)/shard_map/ppermute | solution.py:347
  53.9 12.9 %collective-permute-start.38 = (bf16[128,1024]{1,0:T(8,128)(2,1)}, bf16[128,1024]{1,0:T(8,128)(2,1)S(1)}, u32[]{:S(2)}, u32[]{:S(2)}) collective-permute-start(bf16[128,1024]{1,0:T(8,128)(2,1)} %collective-permute-done.37.refs_2_), channel_id=1, source_target_pairs={{0,4},{4,8},{8,12},{12,14},{14,10},{10,6},{6,2},{2,0},{1,5},{5,9},... | collective-permute-start | bytes 786440 | tf_op jit(solution)/shard_map/ppermute | solution.py:347
  57.5 26.3 %collective-permute-start.14 = (bf16[96,16,256]{2,1,0:T(8,128)(2,1)S(1)}, bf16[96,16,256]{2,1,0:T(8,128)(2,1)}, u32[]{:S(2)}, u32[]{:S(2)}) collective-permute-start(bf16[96,16,256]{2,1,0:T(8,128)(2,1)S(1)} %constant_dynamic-slice_fusion), channel_id=1, source_target_pairs={{0,1},{1,0},{2,3},{3,2},{4,5},{5,4},{6,7},{7,6},{8,9},{9,8},{10,11... | collective-permute-start | bytes 2359304 | tf_op jit(solution)/shard_map/ppermute | solution.py:401
  66.3 12.0 %collective-permute-start.46 = (bf16[128,1024]{1,0:T(8,128)(2,1)S(1)}, bf16[128,1024]{1,0:T(8,128)(2,1)S(1)}, u32[]{:S(2)}, u32[]{:S(2)}) collective-permute-start(bf16[128,1024]{1,0:T(8,128)(2,1)S(1)} %collective-permute-done.45.refs_11_), channel_id=1, source_target_pairs={{4,0},{8,4},{12,8},{14,12},{10,14},{6,10},{2,6},{0,2},{5,1},{9,5},... | collective-permute-start | bytes 786440 | tf_op jit(solution)/shard_map/ppermute | solution.py:347
  66.8 12.8 %collective-permute-start.39 = (bf16[128,1024]{1,0:T(8,128)(2,1)S(1)}, bf16[128,1024]{1,0:T(8,128)(2,1)S(1)}, u32[]{:S(2)}, u32[]{:S(2)}) collective-permute-start(bf16[128,1024]{1,0:T(8,128)(2,1)S(1)} %collective-permute-done.38.refs_3_), channel_id=1, source_target_pairs={{0,4},{4,8},{8,12},{12,14},{14,10},{10,6},{6,2},{2,0},{1,5},{5,9},... | collective-permute-start | bytes 786440 | tf_op jit(solution)/shard_map/ppermute | solution.py:347
  72.7 11.8 %collective-permute-start.10 = (bf16[128,1024]{1,0:T(8,128)(2,1)S(1)}, bf16[128,1024]{1,0:T(8,128)(2,1)S(1)}, u32[]{:S(2)}, u32[]{:S(2)}) collective-permute-start(bf16[128,1024]{1,0:T(8,128)(2,1)S(1)} %collective-permute-done.9.refs_11_), channel_id=1, source_target_pairs={{4,0},{8,4},{12,8},{14,12},{10,14},{6,10},{2,6},{0,2},{5,1},{9,5},... | collective-permute-start | bytes 786440 | tf_op jit(solution)/shard_map/ppermute | solution.py:347
  74.0 11.8 %collective-permute-start.3 = (bf16[128,1024]{1,0:T(8,128)(2,1)S(1)}, bf16[128,1024]{1,0:T(8,128)(2,1)}, u32[]{:S(2)}, u32[]{:S(2)}) collective-permute-start(bf16[128,1024]{1,0:T(8,128)(2,1)S(1)} %collective-permute-done.2.refs_3_), channel_id=1, source_target_pairs={{0,4},{4,8},{8,12},{12,14},{14,10},{10,6},{6,2},{2,0},{1,5},{5,9},... | collective-permute-start | bytes 786440 | tf_op jit(solution)/shard_map/ppermute | solution.py:347
  78.3 11.3 %collective-permute-start.47 = (bf16[128,1024]{1,0:T(8,128)(2,1)S(1)}, bf16[128,1024]{1,0:T(8,128)(2,1)}, u32[]{:S(2)}, u32[]{:S(2)}) collective-permute-start(bf16[128,1024]{1,0:T(8,128)(2,1)S(1)} %collective-permute-done.46.refs_12_), channel_id=1, source_target_pairs={{4,0},{8,4},{12,8},{14,12},{10,14},{6,10},{2,6},{0,2},{5,1},{9,5},... | collective-permute-start | bytes 786440 | tf_op jit(solution)/shard_map/ppermute | solution.py:347
  79.6 11.3 %collective-permute-start.40 = (bf16[128,1024]{1,0:T(8,128)(2,1)S(1)}, bf16[128,1024]{1,0:T(8,128)(2,1)}, u32[]{:S(2)}, u32[]{:S(2)}) collective-permute-start(bf16[128,1024]{1,0:T(8,128)(2,1)S(1)} %collective-permute-done.39.refs_4_), channel_id=1, source_target_pairs={{0,4},{4,8},{8,12},{12,14},{14,10},{10,6},{6,2},{2,0},{1,5},{5,9},... | collective-permute-start | bytes 786440 | tf_op jit(solution)/shard_map/ppermute | solution.py:347
  83.7 11.5 %collective-permute-start.20 = (bf16[256,256]{1,0:T(8,128)(2,1)}, bf16[256,256]{1,0:T(8,128)(2,1)S(1)}, u32[]{:S(2)}, u32[]{:S(2)}) collective-permute-start(bf16[256,256]{1,0:T(8,128)(2,1)} %add_part.42), channel_id=1, source_target_pairs={{0,4},{4,8},{8,12},{12,14},{14,10},{10,6},{6,2},{2,0},{1,5},{5,9},... | collective-permute-start | bytes 393224 | tf_op jit(solution)/shard_map/ppermute | solution.py:364
  84.5 19.4 %collective-permute-start.11 = (bf16[128,1024]{1,0:T(8,128)(2,1)S(1)}, bf16[128,1024]{1,0:T(8,128)(2,1)}, u32[]{:S(2)}, u32[]{:S(2)}) collective-permute-start(bf16[128,1024]{1,0:T(8,128)(2,1)S(1)} %collective-permute-done.10.refs_12_), channel_id=1, source_target_pairs={{4,0},{8,4},{12,8},{14,12},{10,14},{6,10},{2,6},{0,2},{5,1},{9,5},... | collective-permute-start | bytes 786440 | tf_op jit(solution)/shard_map/ppermute | solution.py:347
  85.8 18.5 %collective-permute-start.4 = (bf16[128,1024]{1,0:T(8,128)(2,1)}, bf16[128,1024]{1,0:T(8,128)(2,1)}, u32[]{:S(2)}, u32[]{:S(2)}) collective-permute-start(bf16[128,1024]{1,0:T(8,128)(2,1)} %collective-permute-done.3.refs_4_), channel_id=1, source_target_pairs={{0,4},{4,8},{8,12},{12,14},{14,10},{10,6},{6,2},{2,0},{1,5},{5,9},... | collective-permute-start | bytes 786440 | tf_op jit(solution)/shard_map/ppermute | solution.py:347
  89.6 16.3 %collective-permute-start.48 = (bf16[128,1024]{1,0:T(8,128)(2,1)}, bf16[128,1024]{1,0:T(8,128)(2,1)}, u32[]{:S(2)}, u32[]{:S(2)}) collective-permute-start(bf16[128,1024]{1,0:T(8,128)(2,1)} %collective-permute-done.47.refs_13_), channel_id=1, source_target_pairs={{4,0},{8,4},{12,8},{14,12},{10,14},{6,10},{2,6},{0,2},{5,1},{9,5},... | collective-permute-start | bytes 786440 | tf_op jit(solution)/shard_map/ppermute | solution.py:347
  91.0 15.4 %collective-permute-start.41 = (bf16[128,1024]{1,0:T(8,128)(2,1)}, bf16[128,1024]{1,0:T(8,128)(2,1)}, u32[]{:S(2)}, u32[]{:S(2)}) collective-permute-start(bf16[128,1024]{1,0:T(8,128)(2,1)} %collective-permute-done.40.refs_5_), channel_id=1, source_target_pairs={{0,4},{4,8},{8,12},{12,14},{14,10},{10,6},{6,2},{2,0},{1,5},{5,9},... | collective-permute-start | bytes 786440 | tf_op jit(solution)/shard_map/ppermute | solution.py:347
  105.9 17.3 %collective-permute-start.49 = (bf16[128,1024]{1,0:T(8,128)(2,1)}, bf16[128,1024]{1,0:T(8,128)(2,1)}, u32[]{:S(2)}, u32[]{:S(2)}) collective-permute-start(bf16[128,1024]{1,0:T(8,128)(2,1)} %collective-permute-done.48.refs_14_), channel_id=1, source_target_pairs={{4,0},{8,4},{12,8},{14,12},{10,14},{6,10},{2,6},{0,2},{5,1},{9,5},... | collective-permute-start | bytes 786440 | tf_op jit(solution)/shard_map/ppermute | solution.py:347
  106.4 16.9 %collective-permute-start.42 = (bf16[128,1024]{1,0:T(8,128)(2,1)}, bf16[128,1024]{1,0:T(8,128)(2,1)}, u32[]{:S(2)}, u32[]{:S(2)}) collective-permute-start(bf16[128,1024]{1,0:T(8,128)(2,1)} %collective-permute-done.41.refs_6_), channel_id=1, source_target_pairs={{0,4},{4,8},{8,12},{12,14},{14,10},{10,6},{6,2},{2,0},{1,5},{5,9},... | collective-permute-start | bytes 786440 | tf_op jit(solution)/shard_map/ppermute | solution.py:347
  108.7 13.5 %collective-permute-start.56 = (bf16[256,256]{1,0:T(8,128)(2,1)}, bf16[256,256]{1,0:T(8,128)(2,1)}, u32[]{:S(2)}, u32[]{:S(2)}) collective-permute-start(bf16[256,256]{1,0:T(8,128)(2,1)} %add_part.62), channel_id=1, source_target_pairs={{4,0},{8,4},{12,8},{14,12},{10,14},{6,10},{2,6},{0,2},{5,1},{9,5},... | collective-permute-start | bytes 393224 | tf_op jit(solution)/shard_map/ppermute | solution.py:364
  113.5 54.7 %collective-permute-start.13 = (bf16[128,1024]{1,0:T(8,128)(2,1)}, bf16[128,1024]{1,0:T(8,128)(2,1)}, u32[]{:S(2)}, u32[]{:S(2)}) collective-permute-start(bf16[128,1024]{1,0:T(8,128)(2,1)} %collective-permute-done.12.refs_14_), channel_id=1, source_target_pairs={{4,0},{8,4},{12,8},{14,12},{10,14},{6,10},{2,6},{0,2},{5,1},{9,5},... | collective-permute-start | bytes 786440 | tf_op jit(solution)/shard_map/ppermute | solution.py:347
  114.4 53.7 %collective-permute-start.6 = (bf16[128,1024]{1,0:T(8,128)(2,1)}, bf16[128,1024]{1,0:T(8,128)(2,1)}, u32[]{:S(2)}, u32[]{:S(2)}) collective-permute-start(bf16[128,1024]{1,0:T(8,128)(2,1)} %collective-permute-done.5.refs_6_), channel_id=1, source_target_pairs={{0,4},{4,8},{8,12},{12,14},{14,10},{10,6},{6,2},{2,0},{1,5},{5,9},... | collective-permute-start | bytes 786440 | tf_op jit(solution)/shard_map/ppermute | solution.py:347
  166.0 43.3 %collective-permute-start.57 = (bf16[128,1024]{1,0:T(8,128)(2,1)S(1)}, bf16[128,1024]{1,0:T(8,128)(2,1)S(1)}, u32[]{:S(2)}, u32[]{:S(2)}) collective-permute-start(bf16[128,1024]{1,0:T(8,128)(2,1)S(1)} %get-tuple-element.38), channel_id=1, source_target_pairs={{0,4},{4,8},{8,12},{12,14},{14,10},{10,6},{6,2},{2,0},{1,5},{5,9},... | collective-permute-start | bytes 786440 | tf_op jit(solution)/shard_map/ppermute | solution.py:364
  167.6 40.1 %collective-permute-start.64 = (bf16[128,1024]{1,0:T(8,128)(2,1)S(1)}, bf16[128,1024]{1,0:T(8,128)(2,1)S(1)}, u32[]{:S(2)}, u32[]{:S(2)}) collective-permute-start(bf16[128,1024]{1,0:T(8,128)(2,1)S(1)} %get-tuple-element.39), channel_id=1, source_target_pairs={{4,0},{8,4},{12,8},{14,12},{10,14},{6,10},{2,6},{0,2},{5,1},{9,5},... | collective-permute-start | bytes 786440 | tf_op jit(solution)/shard_map/ppermute | solution.py:364
  208.8 11.1 %collective-permute-start.65 = (bf16[128,1024]{1,0:T(8,128)(2,1)S(1)}, bf16[128,1024]{1,0:T(8,128)(2,1)S(1)}, u32[]{:S(2)}, u32[]{:S(2)}) collective-permute-start(bf16[128,1024]{1,0:T(8,128)(2,1)S(1)} %add_part.70), channel_id=1, source_target_pairs={{4,0},{8,4},{12,8},{14,12},{10,14},{6,10},{2,6},{0,2},{5,1},{9,5},... | collective-permute-start | bytes 786440 | tf_op jit(solution)/shard_map/ppermute | solution.py:364
  210.4 11.1 %collective-permute-start.58 = (bf16[128,1024]{1,0:T(8,128)(2,1)S(1)}, bf16[128,1024]{1,0:T(8,128)(2,1)S(1)}, u32[]{:S(2)}, u32[]{:S(2)}) collective-permute-start(bf16[128,1024]{1,0:T(8,128)(2,1)S(1)} %add_part.64), channel_id=1, source_target_pairs={{0,4},{4,8},{8,12},{12,14},{14,10},{10,6},{6,2},{2,0},{1,5},{5,9},... | collective-permute-start | bytes 786440 | tf_op jit(solution)/shard_map/ppermute | solution.py:364
  249.1 10.1 %collective-permute-start.33 = (bf16[128,1024]{1,0:T(8,128)(2,1)S(1)}, bf16[128,1024]{1,0:T(8,128)(2,1)S(1)}, u32[]{:S(2)}, u32[]{:S(2)}) collective-permute-start(bf16[128,1024]{1,0:T(8,128)(2,1)S(1)} %add_part.54), channel_id=1, source_target_pairs={{4,0},{8,4},{12,8},{14,12},{10,14},{6,10},{2,6},{0,2},{5,1},{9,5},... | collective-permute-start | bytes 786440 | tf_op jit(solution)/shard_map/ppermute | solution.py:364
  (91 other events, 851.4 us)

commit v2 on v1

v2 whole, which is shorter than its diff:
```python
import functools
import math

import jax
import jax.numpy as jnp
import numpy as np
from jax import lax
from jax.experimental import pallas as pl
from jax.experimental.pallas import tpu as pltpu
from jax.sharding import PartitionSpec as P

QUERY_HEADS = 64
KEY_VALUE_HEADS = 8
HEAD_SIZE = 128
EPS = 1e-06
THETA = 1000000.0
NEGATIVE = -1e30
FACTOR2 = math.log2(math.e) / math.sqrt(HEAD_SIZE)

ORDER = (0, 2, 4, 6, 7, 5, 3, 1)
RING = len(ORDER)
FORWARD = [(ORDER[i], ORDER[(i + 1) % RING]) for i in range(RING)]
BACKWARD = [(b, a) for a, b in FORWARD]

VMEM = pltpu.CompilerParams(vmem_limit_bytes=48 * 1024 * 1024)


def dot(left, right):
    return jnp.dot(left, right, preferred_element_type=jnp.float32)


def dot_t(left, right):
    return lax.dot_general(
        left, right, (((1,), (1,)), ((), ())), preferred_element_type=jnp.float32
    )


def turned(values, cosine, sine):
    return values * cosine + pltpu.roll(values, HEAD_SIZE // 2, 1) * sine


def span_layout(lengths, prefix, prefill, page_size):
    request_end = jnp.cumsum(lengths)
    request_start = request_end - lengths
    token_index = jnp.arange(prefill, dtype=jnp.int32)
    request = jnp.sum((token_index[:, None] >= request_end[None, :]).astype(jnp.int32), axis=1)
    onehot = (request[:, None] == jnp.arange(lengths.shape[0], dtype=jnp.int32)[None, :]).astype(
        jnp.int32
    )
    token_start = jnp.sum(onehot * request_start[None, :], axis=1)
    token_prefix = jnp.sum(onehot * prefix[None, :], axis=1)
    return (request, token_prefix * page_size + token_index - token_start)


def tables(positions):
    half_dim = HEAD_SIZE // 2
    frequency = jnp.exp(
        jnp.arange(half_dim, dtype=jnp.float32) * (-2.0 * math.log(THETA) / HEAD_SIZE)
    )
    angles = positions.astype(jnp.float32)[:, None] * frequency[None, :]
    cosine, sine = jnp.cos(angles), jnp.sin(angles)
    return (
        jnp.concatenate([cosine, cosine], axis=1),
        jnp.concatenate([-sine, sine], axis=1),
    )


def cost(flops, moved, transcendentals=0):
    return pl.CostEstimate(flops=flops, bytes_accessed=moved, transcendentals=transcendentals)


def shaped(shape, dtype):
    return jax.ShapeDtypeStruct(shape, dtype)


def pairs_kernel(blocks, x_ref, gain_ref, w_ref, out_ref, forward_ref, backward_ref, scaled):
    k = pl.program_id(0)

    @pl.when(k == 0)
    def _():
        gain = gain_ref[...].astype(jnp.float32)
        scaled[...] = (x_ref[...].astype(jnp.float32) * gain).astype(jnp.bfloat16)

    result = dot(scaled[...], w_ref[...]).astype(jnp.bfloat16)
    out_ref[0] = result
    half = forward_ref.shape[0]

    @pl.when(k == RING - 1)
    def _():
        forward_ref[...] = result[:half]

    @pl.when(k == 1)
    def _():
        backward_ref[...] = result[half:]


def pairs_partial(x, gain_row, matrix, blocks):
    rows, width = x.shape
    columns = matrix.shape[1] // RING
    first = pl.BlockSpec((rows // 2, columns), lambda k, b: (0, 0))
    return pl.pallas_call(
        pairs_kernel,
        grid_spec=pltpu.PrefetchScalarGridSpec(
            num_scalar_prefetch=1,
            grid=(RING,),
            in_specs=[
                pl.BlockSpec((rows, width), lambda k, b: (0, 0)),
                pl.BlockSpec((1, width), lambda k, b: (0, b[0])),
                pl.BlockSpec((width, columns), lambda k, b: (0, b[k])),
            ],
            out_specs=[pl.BlockSpec((1, rows, columns), lambda k, b: (k, 0, 0)), first, first],
            scratch_shapes=[pltpu.VMEM((rows, width), jnp.bfloat16)],
        ),
        out_shape=[
            shaped((RING, rows, columns), jnp.bfloat16),
            shaped((rows // 2, columns), jnp.bfloat16),
            shaped((rows // 2, columns), jnp.bfloat16),
        ],
        compiler_params=VMEM,
        cost_estimate=cost(2 * x.size * matrix.shape[1], 2 * (x.size + 2 * matrix.size)),
        name="pairs_partial",
    )(blocks, x, gain_row, matrix)


def add_pairs_kernel(a_ref, b_ref, pa_ref, pb_ref, oa_ref, ob_ref):
    for arrived, part, out in ((a_ref, pa_ref, oa_ref), (b_ref, pb_ref, ob_ref)):
        out[...] = (arrived[...].astype(jnp.float32) + part[0].astype(jnp.float32)).astype(
            out.dtype
        )


def add_pairs(ahead, back, parts, ka, kb, dtype):
    rows, columns = ahead.shape
    flat = pl.BlockSpec((rows, columns), lambda i: (0, 0))
    return pl.pallas_call(
        add_pairs_kernel,
        grid=(1,),
        in_specs=[
            flat,
            flat,
            pl.BlockSpec((1, rows, columns), lambda i: (ka, 0, 0)),
            pl.BlockSpec((1, rows, columns), lambda i: (kb, 1, 0)),
        ],
        out_specs=[flat, flat],
        out_shape=[shaped((rows, columns), dtype)] * 2,
        compiler_params=VMEM,
        cost_estimate=cost(2 * ahead.size, 16 * ahead.size),
        name="add_pairs",
    )(ahead, back, parts, parts)


def add_kernel(a_ref, b_ref, pa_ref, pb_ref, oa_ref, ob_ref):
    for arrived, part, out in ((a_ref, pa_ref, oa_ref), (b_ref, pb_ref, ob_ref)):
        out[...] = (arrived[...].astype(jnp.float32) + part[...].astype(jnp.float32)).astype(
            out.dtype
        )


def add_parts(ahead, back, part_ahead, part_back):
    rows, columns = ahead.shape
    flat = pl.BlockSpec((rows, columns), lambda i: (0, 0))
    return pl.pallas_call(
        add_kernel,
        grid=(1,),
        in_specs=[flat] * 4,
        out_specs=[flat, flat],
        out_shape=[shaped((rows, columns), ahead.dtype)] * 2,
        compiler_params=VMEM,
        cost_estimate=cost(2 * ahead.size, 16 * ahead.size),
        name="add_parts",
    )(ahead, back, part_ahead, part_back)


def last_kernel(x_ref, *refs):
    arrived, parts, (mixed_ref, hidden_ref, square_ref) = refs[:4], refs[4:8], refs[8:]
    rows = arrived[0].shape[0]
    sums = []
    for i in range(4):
        at = slice(i * rows, (i + 1) * rows)
        added = arrived[i][...].astype(jnp.float32) + parts[i][...].astype(jnp.float32)
        mixed = x_ref[at].astype(jnp.float32) + added
        mixed_ref[at] = mixed
        hidden_ref[at] = mixed.astype(jnp.bfloat16)
        sums.append(jnp.sum(mixed * mixed, axis=1, keepdims=True))
    column = jnp.broadcast_to(jnp.concatenate(sums, axis=0), (4 * rows, 128))
    square_ref[...] = column.T[: square_ref.shape[0]]


def last_parts(x, arrived, parts):
    rows, columns = x.shape
    flat = pl.BlockSpec((rows, columns), lambda i: (0, 0))
    quarter = pl.BlockSpec((rows // 4, columns), lambda i: (0, 0))
    return pl.pallas_call(
        last_kernel,
        grid=(1,),
        in_specs=[flat] + [quarter] * 8,
        out_specs=[flat, flat, pl.BlockSpec((8, rows), lambda i: (0, 0))],
        out_shape=[
            shaped((rows, columns), jnp.float32),
            shaped((rows, columns), jnp.bfloat16),
            shaped((8, rows), jnp.float32),
        ],
        compiler_params=VMEM,
        cost_estimate=cost(4 * x.size, 12 * x.size),
        name="last_parts",
    )(x, *arrived, *parts)


def norm_kernel(width, mixed_ref, square_ref, gain_ref, out_ref):
    inv = lax.rsqrt(square_ref[...].T[:, :1] / width + EPS)
    out_ref[...] = (mixed_ref[...] * inv * gain_ref[...]).astype(jnp.bfloat16)


def norm_out(mixed, squares, gain, width):
    rows, columns = mixed.shape
    return pl.pallas_call(
        functools.partial(norm_kernel, width),
        grid=(1,),
        in_specs=[pl.BlockSpec(a.shape, lambda i: (0, 0)) for a in (mixed, squares, gain)],
        out_specs=pl.BlockSpec((rows, columns), lambda i: (0, 0)),
        out_shape=shaped((rows, columns), jnp.bfloat16),
        compiler_params=VMEM,
        cost_estimate=cost(3 * mixed.size, 6 * mixed.size),
        name="norm_out",
    )(mixed, squares, gain)


def query_kernel(count, first, last, width, blocks, *refs):
    gain_ref, w_ref, *refs = refs
    if not first:
        total_in, squares_in, *refs = refs
    if last:
        cos_ref, sin_ref, *refs = refs
        *pieces, q_ref, inv_ref, scaled, total, squares = refs
    else:
        *pieces, total, squares, scaled = refs
    each = len(pieces) // count
    step = pl.program_id(0)
    rows_each = pieces[0].shape[0]
    gain = gain_ref[...].astype(jnp.float32)

    @pl.when(step == 0)
    def _():
        total[...] = jnp.zeros_like(total) if first else total_in[...]
        squares[...] = jnp.zeros_like(squares) if first else squares_in[...]

    for k in range(count):

        @pl.when(step == k)
        def _(k=k):
            for i in range(each):
                rows = slice(i * rows_each, (i + 1) * rows_each)
                values = pieces[each * k + i][...].astype(jnp.float32)
                squares[rows] += jnp.sum(values * values, axis=1, keepdims=True)
                scaled[rows] = (values * gain).astype(jnp.bfloat16)

    total[...] += dot(scaled[...], w_ref[...])

    if last:

        @pl.when(step == count - 1)
        def _():
            inv = lax.rsqrt(squares[...] / width + EPS)
            inv_ref[...] = inv
            for head in range(q_ref.shape[1] // HEAD_SIZE):
                at = slice(head * HEAD_SIZE, (head + 1) * HEAD_SIZE)
                q_ref[:, at] = turned(total[:, at] * inv, cos_ref[...], sin_ref[...]).astype(
                    jnp.bfloat16
                )


def pick(places, k, blocks):
    block = blocks[places[0]]
    for i, place in enumerate(places[1:], 1):
        block = jnp.where(k == i, blocks[place], block)
    return block


def query_part(places, pieces, gain_row, weight, blocks, sums=None, angles=None):
    count = len(places)
    rows_each, depth = pieces[0].shape
    rows, width = len(pieces) // count * rows_each, weight.shape[1]
    first, last = sums is None, angles is not None
    whole = lambda shape: pl.BlockSpec(shape, lambda k, b: (0, 0))
    sum_shapes = [(rows, width), (rows, 1)]
    in_specs = [
        pl.BlockSpec((1, depth), lambda k, b: (0, pick(places, k, b))),
        pl.BlockSpec((depth, width), lambda k, b: (pick(places, k, b), 0)),
    ]
    operands = [gain_row, weight]
    if not first:
        in_specs += [whole(s) for s in sum_shapes]
        operands += sums
    scratch = [pltpu.VMEM((rows, depth), jnp.bfloat16)]
    if last:
        in_specs += [whole((rows, HEAD_SIZE))] * 2
        operands += angles
        scratch += [pltpu.VMEM(s, jnp.float32) for s in sum_shapes]
        out_shape = [shaped((rows, width), jnp.bfloat16), shaped((rows, 1), jnp.float32)]
    else:
        out_shape = [shaped(s, jnp.float32) for s in sum_shapes]
    return pl.pallas_call(
        functools.partial(query_kernel, count, first, last, weight.shape[0]),
        grid_spec=pltpu.PrefetchScalarGridSpec(
            num_scalar_prefetch=1,
            grid=(count,),
            in_specs=in_specs + [whole((rows_each, depth))] * len(pieces),
            out_specs=[whole(s) for s in sum_shapes],
            scratch_shapes=scratch,
        ),
        out_shape=out_shape,
        compiler_params=VMEM,
        cost_estimate=cost(2 * count * rows * depth * width, count * depth * width * 4),
        name="query_part",
    )(blocks, *operands, *pieces)


def new_pairs(pairs_ref, inv_ref, cos_ref, sin_ref):
    pairs = (pairs_ref[...] * inv_ref[...]).astype(jnp.bfloat16)
    keys = turned(pairs[:, :HEAD_SIZE].astype(jnp.float32), cos_ref[...], sin_ref[...])
    return keys.astype(jnp.bfloat16), pairs[:, HEAD_SIZE:]


def decode_kernel(
    page_size, q_ref, cache_ref, pairs_ref, inv_ref, cos_ref, sin_ref, page_ref, pos_ref,
    out_ref, bias, new_key, new_value,
):
    @pl.when(pl.program_id(0) == 0)
    def _():
        token = lax.broadcasted_iota(jnp.int32, bias.shape, 1)
        page, offset = token // page_size, token % page_size
        times = jnp.zeros(bias.shape, jnp.float32)
        for j in range(page_ref.shape[1]):
            hit = (page == page_ref[:, j : j + 1]) & (offset + j * page_size < pos_ref[...])
            times += jnp.where(hit, 1.0, 0.0)
        bias[...] = jnp.where(times > 0, jnp.log2(jnp.maximum(times, 1.0)), NEGATIVE)
        keys, values = new_pairs(pairs_ref, inv_ref, cos_ref, sin_ref)
        new_key[...] = keys.astype(jnp.float32)
        new_value[...] = values.astype(jnp.float32)

    for head in range(q_ref.shape[1] // HEAD_SIZE):
        at = slice(head * HEAD_SIZE, (head + 1) * HEAD_SIZE)
        q = q_ref[:, at]
        score = dot_t(q, cache_ref[:, :HEAD_SIZE]) * FACTOR2 + bias[...]
        own = jnp.sum(q.astype(jnp.float32) * new_key[...], axis=1, keepdims=True) * FACTOR2
        peak = jnp.maximum(jnp.max(score, axis=1, keepdims=True), own)
        grown, grown_own = jnp.exp2(score - peak), jnp.exp2(own - peak)
        scale = 1.0 / (jnp.sum(grown, axis=1, keepdims=True) + grown_own)
        context = dot(grown.astype(jnp.bfloat16), cache_ref[:, HEAD_SIZE:])
        out_ref[:, at] = ((context + grown_own * new_value[...]) * scale).astype(jnp.bfloat16)


def decode_context(q, cache, pairs, inv, cosine, sine, page_table, positions, page_size):
    rows, width = positions.shape[0], q.shape[1]
    heads = min(4 * HEAD_SIZE, width)
    tokens = cache.shape[0]
    whole = lambda array: pl.BlockSpec(array.shape, lambda h: (0, 0))
    return pl.pallas_call(
        functools.partial(decode_kernel, page_size),
        grid=(width // heads,),
        in_specs=[pl.BlockSpec((rows, heads), lambda h: (0, h)), whole(cache), whole(pairs)]
        + [whole(inv), whole(cosine), whole(sine)]
        + [whole(page_table), whole(positions)],
        out_specs=pl.BlockSpec((rows, heads), lambda h: (0, h)),
        scratch_shapes=[
            pltpu.VMEM((rows, tokens), jnp.float32),
            pltpu.VMEM((rows, HEAD_SIZE), jnp.float32),
            pltpu.VMEM((rows, HEAD_SIZE), jnp.float32),
        ],
        out_shape=shaped((rows, width), jnp.bfloat16),
        compiler_params=VMEM,
        cost_estimate=cost(4 * rows * width * tokens, 8 * rows * width, 2 * width * tokens),
        name="decode_context",
    )(q, cache, pairs, inv, cosine, sine, page_table, positions)


def prefill_kernel(
    q_ref, prefix_ref, pairs_ref, inv_ref, cos_ref, sin_ref, request_ref, column_ref, owner_ref,
    out_ref, bias, keys, values,
):
    old = prefix_ref.shape[0]

    @pl.when(pl.program_id(0) == 0)
    def _():
        rows = request_ref.shape[0]
        request = request_ref[...]
        bias[:, :old] = jnp.where(request == owner_ref[...], 0.0, NEGATIVE)
        row = lax.broadcasted_iota(jnp.int32, (rows, rows), 0)
        column = lax.broadcasted_iota(jnp.int32, (rows, rows), 1)
        allowed = (request == column_ref[...]) & (column <= row)
        bias[:, old:] = jnp.where(allowed, 0.0, NEGATIVE)
        new_keys, new_values = new_pairs(pairs_ref, inv_ref, cos_ref, sin_ref)
        keys[:old] = prefix_ref[:, :HEAD_SIZE]
        keys[old:] = new_keys
        values[:old] = prefix_ref[:, HEAD_SIZE:]
        values[old:] = new_values

    for head in range(q_ref.shape[1] // HEAD_SIZE):
        at = slice(head * HEAD_SIZE, (head + 1) * HEAD_SIZE)
        score = dot_t(q_ref[:, at], keys[...]) * FACTOR2 + bias[...]
        grown = jnp.exp2(score - jnp.max(score, axis=1, keepdims=True))
        scale = 1.0 / jnp.sum(grown, axis=1, keepdims=True)
        context = dot(grown.astype(jnp.bfloat16), values[...]) * scale
        out_ref[:, at] = context.astype(jnp.bfloat16)


def prefill_context(q, prefix, pairs, inv, cosine, sine, request, owner):
    rows, width = request.shape[0], q.shape[1]
    heads = min(4 * HEAD_SIZE, width)
    tokens = prefix.shape[0] + rows
    whole = lambda array: pl.BlockSpec(array.shape, lambda h: (0, 0))
    maps = (request[:, None], request[None, :], owner[None, :])
    return pl.pallas_call(
        prefill_kernel,
        grid=(width // heads,),
        in_specs=[pl.BlockSpec((rows, heads), lambda h: (0, h)), whole(prefix), whole(pairs)]
        + [whole(inv), whole(cosine), whole(sine)]
        + [whole(a) for a in maps],
        out_specs=pl.BlockSpec((rows, heads), lambda h: (0, h)),
        scratch_shapes=[
            pltpu.VMEM((rows, tokens), jnp.float32),
            pltpu.VMEM((tokens, HEAD_SIZE), jnp.bfloat16),
            pltpu.VMEM((tokens, HEAD_SIZE), jnp.bfloat16),
        ],
        out_shape=shaped((rows, width), jnp.bfloat16),
        compiler_params=VMEM,
        cost_estimate=cost(4 * rows * width * tokens, 8 * rows * width, 2 * width * tokens),
        name="prefill_context",
    )(q, prefix, pairs, inv, cosine, sine, *maps)


def output_kernel(count, blocks, *refs):
    contexts, (wa_ref, wb_ref), outs = refs[:count], refs[count : count + 2], refs[count + 2 :]
    quarter = outs[0].shape[0]
    for w_ref, results in ((wa_ref, outs[: 2 * count]), (wb_ref, outs[2 * count :])):
        for i, context_ref in enumerate(contexts):
            result = dot(context_ref[...], w_ref[...]).astype(jnp.bfloat16)
            results[2 * i][...] = result[:quarter]
            results[2 * i + 1][...] = result[quarter:]


def output_part(contexts, weight, places, blocks, tiles=4):
    rows, depth = contexts[0].shape
    columns = weight.shape[1] // RING
    tile = columns // tiles
    count = len(contexts)
    pa, pb = places
    outs = pl.pallas_call(
        functools.partial(output_kernel, count),
        grid_spec=pltpu.PrefetchScalarGridSpec(
            num_scalar_prefetch=1,
            grid=(tiles,),
            in_specs=[pl.BlockSpec((rows, depth), lambda t, b: (0, 0))] * count
            + [
                pl.BlockSpec((depth, tile), lambda t, b: (0, b[pa] * tiles + t)),
                pl.BlockSpec((depth, tile), lambda t, b: (0, b[pb] * tiles + t)),
            ],
            out_specs=[pl.BlockSpec((rows // 2, tile), lambda t, b: (0, t))] * (4 * count),
        ),
        out_shape=[shaped((rows // 2, columns), jnp.bfloat16)] * (4 * count),
        compiler_params=VMEM,
        cost_estimate=cost(4 * count * rows * depth * columns, 8 * depth * columns),
        name="output_part",
    )(blocks, *contexts, weight, weight)
    return {pa: outs[: 2 * count], pb: outs[2 * count :]}


def after(array, *others):
    return lax.optimization_barrier((array, *others))[0]


def hop(ahead, back):
    return lax.ppermute(ahead, "tensor", FORWARD), lax.ppermute(back, "tensor", BACKWARD)


def sum_squares(squares):
    for low in (1, 2, 4):
        squares = squares + lax.ppermute(
            squares, "tensor", [(t, t ^ low) for t in range(RING)]
        )
    return squares


def body(
    inputs,
    entry_gain,
    exit_gain,
    query_weight,
    key_value_matrix,
    output_weight,
    page_pool,
    page_table,
    positions,
    request_lengths,
    prefix_pages,
    source_pages,
    target_pages,
):
    decode = page_table.shape[0]
    prefill = inputs.shape[0] - decode
    page_count, page_size, _ = page_pool.shape
    me = lax.axis_index("tensor")
    width = inputs.shape[1]
    per_device = query_weight.shape[1] // HEAD_SIZE
    group = me * per_device // (QUERY_HEADS // KEY_VALUE_HEADS)
    pair = 2 * HEAD_SIZE

    ring = lax.axis_size("tensor") == RING
    if ring:
        gathered = [[inputs[:prefill]], [inputs[prefill:]]]

        def gather_hop(*others):
            sent = [pieces[-1] for pieces in gathered]
            if others:
                sent = lax.optimization_barrier((*sent, *others))[:2]
            for pieces, arrived in zip(gathered, hop(*sent)):
                pieces.append(arrived)

        gather_hop()
        token = lax.ppermute(inputs[:16, :HEAD_SIZE], "replica", [(0, 1), (1, 0)])
        local = after(inputs, token)
        page_pool, positions, request_lengths, prefix_pages = lax.optimization_barrier(
            (page_pool, positions, request_lengths, prefix_pages, gathered[0][1])
        )[:4]

    own_pool = lax.dynamic_slice_in_dim(page_pool, group * pair, pair, 2)
    peer_pool = lax.ppermute(own_pool, "replica", [(0, 1), (1, 0)])
    prefix = prefix_pages[0]
    page_max = target_pages.shape[2]
    arrived = peer_pool[source_pages.reshape(-1)]
    usable = jnp.arange(page_max, dtype=jnp.int32)[None, :] < prefix[:, None]
    target = jnp.where(usable.reshape(-1), target_pages.reshape(-1), page_count)
    cache = own_pool.at[target].set(arrived, mode="drop").reshape(-1, pair)
    prefix_rows = arrived.reshape(-1, pair)
    slots = jnp.where(usable, jnp.arange(prefix.shape[0], dtype=jnp.int32)[:, None], -1)
    owner = jnp.repeat(slots.reshape(-1), page_size)

    request, span = span_layout(request_lengths[0], prefix, prefill, page_size)
    cosine, sine = tables(jnp.concatenate([span, positions]))
    angles = ((cosine[:prefill], sine[:prefill]), (cosine[prefill:], sine[prefill:]))
    gain_row = entry_gain[None, :]

    def attend_prefill(q, pairs, inv):
        return prefill_context(q, prefix_rows, pairs, inv, *angles[0], request, owner)

    def attend_decode(q, pairs, inv):
        return decode_context(
            q, cache, pairs, inv, *angles[1], page_table, positions[:, None], page_size
        )

    exit_row = lax.dynamic_slice_in_dim(exit_gain, me * width, width, 0)
    exit_row = exit_row.astype(jnp.float32)[None, :]

    if ring:
        place = jnp.where(me % 2 == 0, me // 2, RING - 1 - me // 2)
        places = (place + jnp.arange(RING, dtype=jnp.int32)) % RING
        blocks = jnp.where(places < RING // 2, 2 * places, 2 * (RING - places) - 1)
        parts, *moving = pairs_partial(local, gain_row, key_value_matrix, blocks)

        def pairs_hop(moving, s):
            moving = lax.optimization_barrier((*moving, gathered[0][s], gathered[1][s]))[:2]
            dtype = jnp.float32 if s == RING - 1 else jnp.bfloat16
            return add_pairs(*hop(*moving), parts, RING - 1 - s, (1 + s) % RING, dtype)

        def query(side, hops, sums=None, angles=None):
            places = [(-s if side == 0 else s) % RING for s in hops]
            pieces = [gathered[side][s] for s in hops]
            return query_part(
                places, pieces, gain_row, query_weight, blocks, sums, angles
            )

        gather_hop(*moving)
        moving = pairs_hop(moving, 1)
        gather_hop(*moving)
        moving = pairs_hop(moving, 2)
        gather_hop(*moving)
        moving = pairs_hop(moving, 3)
        sums = [query(0, (0, 1, 2, 3)), None]
        gather_hop(*moving, sums[0][1])
        moving = pairs_hop(moving, 4)
        sums[1] = query(1, (0, 1, 2, 3, 4))
        gather_hop(*moving, sums[1][1], cache, *angles[0], *angles[1])
        moving = pairs_hop(moving, 5)
        sums[0] = query(0, (4, 5), sums[0])
        gather_hop(*moving, sums[0][1])
        moving = pairs_hop(moving, 6)
        sums[1] = query(1, (5, 6), sums[1])
        sums[0] = query(0, (6,), sums[0])
        moving = lax.optimization_barrier((*moving, sums[0][1], sums[1][1]))[:2]
        pairs = pairs_hop(moving, 7)
        q, inv = query(0, (7,), sums[0], angles[0])
        prefilled = attend_prefill(q, pairs[0], inv)
        parts = [output_part([prefilled], output_weight, (7, 1), blocks), None]
        first = hop(parts[0][7][0], parts[0][1][1])
        parts[0] |= output_part([prefilled], output_weight, (6, 2), blocks)
        q, inv = query(1, (7,), sums[1], angles[1])
        second = hop(*add_parts(*first, parts[0][6][0], parts[0][2][1]))
        decoded = attend_decode(after(q, first[0]), pairs[1], inv)
        decoded_late = after(decoded, second[0])
        parts[1] = output_part([decoded_late], output_weight, (7, 1), blocks)
        parts[1] |= output_part([decoded_late], output_weight, (6, 2), blocks)
        for places in ((5, 3), (4, 0)):
            both = output_part([prefilled, decoded], output_weight, places, blocks)
            for i in range(2):
                parts[i] |= {k: both[k][2 * i : 2 * i + 2] for k in places}
        running = [second, (parts[1][7][0], parts[1][1][1])]
        for s in range(1, RING):
            for i in range(2):
                if i == 0 and s <= 2:
                    moved = second
                else:
                    moved = hop(*running[i])
                if s < RING - 1 and not (i == 0 and s == 1):
                    moved = add_parts(*moved, parts[i][RING - 1 - s][0], parts[i][1 + s][1])
                running[i] = moved
        mixed, hidden, squares = last_parts(
            inputs, [*running[0], *running[1]], [*parts[0][0], *parts[1][0]]
        )
        return hidden, norm_out(mixed, sum_squares(squares), exit_row, exit_gain.shape[0])

    rows = lax.all_gather(inputs, "tensor", axis=1, tiled=True).astype(jnp.float32)
    inv = lax.rsqrt(jnp.mean(rows * rows, axis=1, keepdims=True) + EPS)
    scaled = (rows * inv * entry_gain.astype(jnp.float32)).astype(jnp.bfloat16)
    own = lax.dynamic_slice_in_dim(scaled, me * width, width, 1)
    pairs = lax.psum(dot(own, key_value_matrix), "tensor")
    pairs = lax.dynamic_slice_in_dim(pairs, group * pair, pair, 1)
    q = dot(scaled, query_weight).reshape(-1, per_device, HEAD_SIZE)
    swapped = jnp.roll(q, HEAD_SIZE // 2, 2)
    q = (q * cosine[:, None] + swapped * sine[:, None]).astype(jnp.bfloat16)
    q = q.reshape(-1, per_device * HEAD_SIZE)
    one = jnp.ones_like(inv)
    context = [
        attend_prefill(q[:prefill], pairs[:prefill], one[:prefill]),
        attend_decode(q[prefill:], pairs[prefill:], one[prefill:]),
    ]
    context = jnp.concatenate(context, axis=0)
    summed = lax.psum_scatter(
        dot(context, output_weight), "tensor", scatter_dimension=1, tiled=True
    )
    mixed = inputs.astype(jnp.float32) + summed
    squares = lax.psum(jnp.sum(mixed * mixed, axis=1), "tensor")[:, None]
    out = mixed * lax.rsqrt(squares / exit_gain.shape[0] + EPS) * exit_row
    return mixed.astype(jnp.bfloat16), out.astype(jnp.bfloat16)


def solution(mesh):
    rows = ("groups", "replica")
    return jax.shard_map(
        body,
        mesh=mesh,
        in_specs=(
            P(rows, "tensor"),
            P(),
            P(),
            P(None, "tensor"),
            P("tensor", None),
            P("tensor", None),
            P(rows, None, None),
            P(rows, None),
            P(rows),
            P(rows, None),
            P(rows, None),
            P(rows, None, None),
            P(rows, None, None),
        ),
        out_specs=(P(rows, "tensor"), P(rows, "tensor")),
        check_vma=False,
    )
```

time: 300 us -> 253 us (0.84)
  Pallas kernels: 112 us -> 91 us
  other arithmetic: 15.7 us -> 2.45 us
  starting transfers between devices: 80.2 us -> 67.4 us
  local copies, waits for them, and re-layouts: 21.7 us -> 24.8 us
    pallas_call x47 -> x35, Pallas kernels: 94 us -> 74.3 us  [the longest x7 33.4 us: query_part(): pl.pallas_call(functools.partial(query_kernel, count, first, last, weight...]
    ppermute x70 -> x56, starting transfers between devices: 72.8 us -> 61.4 us  [the longest x28 33.5 us: hop(): lax.ppermute(ahead, 'tensor', FORWARD)]
    another operation x4 -> x1, other arithmetic: 8.59 us -> 0.18 us
    ppermute x70 -> x56, waiting for transfers between devices: 62.2 us -> 58.8 us  [the longest x28 44.5 us: hop(): lax.ppermute(ahead, 'tensor', FORWARD)]
    concatenate x4 -> x0, other arithmetic: 3.04 us -> none  [the longest x2 3.03 us: body(): return (jnp.concatenate(hidden, axis=0), jnp.concatenate(out, axis=0))]
    ppermute x6 -> x3, starting transfers between devices: 7.4 us -> 5.95 us  [sum_squares(): lax.ppermute(squares, 'tensor', [(t, t ^ low) for t in range(RING)])]
    unnamed x95 -> x73, local copies, waits for them, and re-layouts: 12.9 us -> 13.1 us
  transfers between devices with their start and end apart: 77 -> 60, of which waited for: 31 -> 31; matrix products, arithmetic and copies ran while one was open for 7% -> 6% of each run, Pallas kernels for 35% -> 29%
where the time goes in v2:
time: 253 us; the launch traced here: 252 us
  Pallas kernels  91 us (36%)
  starting transfers between devices  67.4 us (27%)
  waiting for transfers between devices  64.6 us (26%)
  local copies, waits for them, and re-layouts  24.8 us (10%)
    ppermute x28, waiting for transfers between devices, hop(): lax.ppermute(ahead, 'tensor', FORWARD)  44.5 us
    ppermute x28, starting transfers between devices, hop(): lax.ppermute(ahead, 'tensor', FORWARD)  33.5 us
    pallas_call x7, Pallas kernels, query_part(): pl.pallas_call(functools.partial(query_kernel, count, first, last, weight...  33.4 us
    pallas_call x6, Pallas kernels, output_part(): pl.pallas_call(functools.partial(output_kernel, count), grid_spec=pltpu.P...  29.1 us
    ppermute x28, starting transfers between devices, hop(): lax.ppermute(back, 'tensor', BACKWARD)  27.9 us
    ppermute x28, waiting for transfers between devices, hop(): lax.ppermute(back, 'tensor', BACKWARD)  14.3 us
    unnamed x73, local copies, waits for them, and re-layouts  13.1 us
    pallas_call x1, Pallas kernels, decode_context(): pl.pallas_call(functools.partial(decode_kernel, page_size), grid=(width /...  8.77 us
  transfers between devices with their start and end apart: 60, of which 31 were waited for; matrix products, arithmetic and copies ran while one was open for 6% of the time, Pallas kernels for 29%

profile of v2, /device:TPU:0, one launch (start us, length us, event | category | flops | bytes accessed | tf_op | source)
XLA Modules:
  0.0 251.5 jit_solution(13897224696005231765)
XLA Ops:
  1.9 3.1 %collective-permute-start = (bf16[256,1024]{1,0:T(8,128)(2,1)S(1)}, bf16[256,1024]{1,0:T(8,128)(2,1)}, u32[]{:S(2)}, u32[]{:S(2)}) collective-permute-start(bf16[256,1024]{1,0:T(8,128)(2,1)S(1)} %get-tuple-element.253.refs_2_), channel_id=1, source_target_pairs={{0,4},{4,8},{8,12},{12,14},{14,10},{10,6},{6,2},{2,0},{1,5},{5,9},... | collective-permute-start | bytes 1572872 | tf_op jit(solution)/shard_map/ppermute | solution.py:473
  7.9 7.9 %pairs_partial.1 = (bf16[8,512,256]{2,1,0:T(8,128)(2,1)S(1)}, bf16[256,256]{1,0:T(8,128)(2,1)}, bf16[256,256]{1,0:T(8,128)(2,1)S(1)}) custom-call(s32[8]{0:T(128)S(1)} %compare_select_fusion.4.blocks, bf16[512,1024]{1,0:T(8,128)(2,1)S(1)} %copy-done, bf16[1,8192]{1,0:T(2,128)(2,1)S(1)} %broadcast_in_dim.45.gain_ref.refs_0_, bf16[1024,2048]{1,0:T(8,128)(2,1)} %w_ref.1), custom_call_target="tpu_custom_call" | custom-call | flops 2147483648 | bytes 9437184 | tf_op jit(solution)/shard_map/pairs_partial/pallas_call | solution.py:101
  25.1 8.9 %collective-permute-done.4.a_ref = bf16[256,256]{1,0:T(8,128)(2,1)S(1)} collective-permute-done((bf16[256,256]{1,0:T(8,128)(2,1)}, bf16[256,256]{1,0:T(8,128)(2,1)S(1)}, u32[]{:S(2)}, u32[]{:S(2)}) %collective-permute-start.4) | collective-permute-done | bytes 131104 | tf_op jit(solution)/shard_map/ppermute | solution.py:473
  39.7 10.1 %collective-permute-done.8.a_ref = bf16[256,256]{1,0:T(8,128)(2,1)S(1)} collective-permute-done((bf16[256,256]{1,0:T(8,128)(2,1)S(1)}, bf16[256,256]{1,0:T(8,128)(2,1)S(1)}, u32[]{:S(2)}, u32[]{:S(2)}) %collective-permute-start.8) | collective-permute-done | bytes 131104 | tf_op jit(solution)/shard_map/ppermute | solution.py:473
  56.4 7.1 %query_part.7 = (f32[256,1024]{1,0:T(8,128)S(1)}, f32[256,1]{1,0:T(8,128)S(1)}) custom-call(s32[8]{0:T(128)S(1)} %compare_select_fusion.4.blocks, bf16[1,8192]{1,0:T(2,128)(2,1)S(1)} %broadcast_in_dim.45.gain_ref.refs_0_, bf16[8192,1024]{1,0:T(8,128)(2,1)} %refs_1_.19, bf16[256,1024]{1,0:T(8,128)(2,1)S(1)} %get-tuple-element.253.refs_2_, ...), custom_call_target="tpu_custom_call" | custom-call | flops 2147483648 | bytes 16777216 | tf_op jit(solution)/shard_map/query_part/pallas_call | solution.py:302
  70.4 3.9 %scatter_fusion = bf16[96,16,256]{2,1,0:T(8,128)(2,1)} fusion(bf16[96,16,256]{2,1,0:T(8,128)(2,1)} %constant_dynamic-slice_fusion, s32[32]{0:T(128)S(1)} %fusion.4, bf16[32,16,256]{2,1,0:T(8,128)(2,1)S(1)} %gather_fusion), kind=kCustom, calls=%fused_computation.1 | custom fusion | bytes 786560 | tf_op jit(solution)/shard_map/scatter | solution.py:533
  77.4 8.7 %query_part.9 = (f32[256,1024]{1,0:T(8,128)S(1)}, f32[256,1]{1,0:T(8,128)S(1)}) custom-call(s32[8]{0:T(128)S(1)} %compare_select_fusion.4.blocks, bf16[1,8192]{1,0:T(2,128)(2,1)S(1)} %broadcast_in_dim.45.gain_ref.refs_0_, bf16[8192,1024]{1,0:T(8,128)(2,1)} %refs_1_.19, bf16[256,1024]{1,0:T(8,128)(2,1)S(1)} %get-tuple-element.252.refs_2_, ...), custom_call_target="tpu_custom_call" | custom-call | flops 2684354560 | bytes 20971520 | tf_op jit(solution)/shard_map/query_part/pallas_call | solution.py:302
  90.3 4.3 %query_part.8 = (f32[256,1024]{1,0:T(8,128)S(1)}, f32[256,1]{1,0:T(8,128)S(1)}) custom-call(s32[8]{0:T(128)S(1)} %compare_select_fusion.4.blocks, bf16[1,8192]{1,0:T(2,128)(2,1)S(1)} %broadcast_in_dim.45.gain_ref.refs_0_, bf16[8192,1024]{1,0:T(8,128)(2,1)} %refs_1_.19, f32[256,1024]{1,0:T(8,128)S(1)} %copy-done.3, f32[256,1]{1,0:T(8,128)S(1)} %copy-done.17, ...), custom_call_target="tpu_custom_call" | custom-call | flops 1073741824 | bytes 8388608 | tf_op jit(solution)/shard_map/query_part/pallas_call | solution.py:302
  94.7 6.0 %collective-permute-done.21.a_ref = bf16[256,256]{1,0:T(8,128)(2,1)S(1)} collective-permute-done((bf16[256,256]{1,0:T(8,128)(2,1)S(1)}, bf16[256,256]{1,0:T(8,128)(2,1)S(1)}, u32[]{:S(2)}, u32[]{:S(2)}) %collective-permute-start.21) | collective-permute-done | bytes 131104 | tf_op jit(solution)/shard_map/ppermute | solution.py:473
  100.6 2.2 collective-permute-done.22.b_ref
  107.0 2.9 %query_part.10 = (f32[256,1024]{1,0:T(8,128)S(1)}, f32[256,1]{1,0:T(8,128)S(1)}) custom-call(s32[8]{0:T(128)S(1)} %compare_select_fusion.4.blocks, bf16[1,8192]{1,0:T(2,128)(2,1)S(1)} %broadcast_in_dim.45.gain_ref.refs_0_, bf16[8192,1024]{1,0:T(8,128)(2,1)} %refs_1_.19, f32[256,1024]{1,0:T(8,128)S(1)} %get-tuple-element.150.refs_2_, ...), custom_call_target="tpu_custom_call" | custom-call | flops 536870912 | bytes 4194304 | tf_op jit(solution)/shard_map/query_part/pallas_call | solution.py:302
  111.5 4.2 %query_part.12 = (f32[256,1024]{1,0:T(8,128)S(1)}, f32[256,1]{1,0:T(8,128)S(1)}) custom-call(s32[8]{0:T(128)S(1)} %compare_select_fusion.4.blocks, bf16[1,8192]{1,0:T(2,128)(2,1)S(1)} %broadcast_in_dim.45.gain_ref.refs_0_, bf16[8192,1024]{1,0:T(8,128)(2,1)} %refs_1_.19, f32[256,1024]{1,0:T(8,128)S(1)} %get-tuple-element.176.refs_2_, ...), custom_call_target="tpu_custom_call" | custom-call | flops 1073741824 | bytes 8388608 | tf_op jit(solution)/shard_map/query_part/pallas_call | solution.py:302
  124.5 3.1 %query_part.11 = (bf16[256,1024]{1,0:T(8,128)(2,1)S(1)}, f32[256,1]{1,0:T(8,128)S(1)}) custom-call(s32[8]{0:T(128)S(1)} %compare_select_fusion.4.blocks, bf16[1,8192]{1,0:T(2,128)(2,1)S(1)} %broadcast_in_dim.45.gain_ref.refs_0_, bf16[8192,1024]{1,0:T(8,128)(2,1)} %refs_1_.19, f32[256,1024]{1,0:T(8,128)S(1)} %copy-done.7, f32[256,1]{1,0:T(8,128)S(1)} %copy-done.19, ...), custom_call_target="tpu_custom_call" | custom-call | flops 536870912 | bytes 4194304 | tf_op jit(solution)/shard_map/query_part/pallas_call | solution.py:302
  128.7 3.8 %prefill_context.1.refs_0_ = bf16[256,1024]{1,0:T(8,128)(2,1)S(1)} custom-call(bf16[256,1024]{1,0:T(8,128)(2,1)S(1)} %get-tuple-element.171.q_ref, bf16[512,256]{1,0:T(8,128)(2,1)S(1)} %bitcast.19, f32[256,256]{1,0:T(8,128)S(1)} %get-tuple-element.183.pairs_ref, f32[256,1]{1,0:T(8,128)S(1)} %get-tuple-element.184.inv_ref, ...), custom_call_target="tpu_custom_call" | custom-call | flops 805306368 | bytes 2097152 | tf_op jit(solution)/shard_map/prefill_context/pallas_call | solution.py:413
  132.6 4.5 %output_part.6 = (bf16[128,1024]{1,0:T(8,128)(2,1)S(1)}, bf16[128,1024]{1,0:T(8,128)(2,1)S(1)}, bf16[128,1024]{1,0:T(8,128)(2,1)S(1)}, bf16[128,1024]{1,0:T(8,128)(2,1)S(1)}) custom-call(s32[8]{0:T(128)S(1)} %compare_select_fusion.4.blocks, bf16[256,1024]{1,0:T(8,128)(2,1)S(1)} %prefill_context.1.refs_0_, bf16[1024,8192]{1,0:T(8,128)(2,1)} %refs_2_.11, ...), custom_call_target="tpu_custom_call" | custom-call | flops 1073741824 | bytes 8388608 | tf_op jit(solution)/shard_map/output_part/pallas_call | solution.py:448
  139.2 4.5 %output_part.7 = (bf16[128,1024]{1,0:T(8,128)(2,1)S(1)}, bf16[128,1024]{1,0:T(8,128)(2,1)S(1)}, bf16[128,1024]{1,0:T(8,128)(2,1)S(1)}, bf16[128,1024]{1,0:T(8,128)(2,1)S(1)}) custom-call(s32[8]{0:T(128)S(1)} %compare_select_fusion.4.blocks, bf16[256,1024]{1,0:T(8,128)(2,1)S(1)} %prefill_context.1.refs_0_, bf16[1024,8192]{1,0:T(8,128)(2,1)} %refs_2_.11, ...), custom_call_target="tpu_custom_call" | custom-call | flops 1073741824 | bytes 8388608 | tf_op jit(solution)/shard_map/output_part/pallas_call | solution.py:448
  149.0 3.1 %query_part.13 = (bf16[256,1024]{1,0:T(8,128)(2,1)S(1)}, f32[256,1]{1,0:T(8,128)S(1)}) custom-call(s32[8]{0:T(128)S(1)} %compare_select_fusion.4.blocks, bf16[1,8192]{1,0:T(2,128)(2,1)S(1)} %broadcast_in_dim.45.gain_ref.refs_0_, bf16[8192,1024]{1,0:T(8,128)(2,1)} %refs_1_.19, f32[256,1024]{1,0:T(8,128)S(1)} %copy-done.5, f32[256,1]{1,0:T(8,128)S(1)} %copy-done.15, ...), custom_call_target="tpu_custom_call" | custom-call | flops 536870912 | bytes 4194304 | tf_op jit(solution)/shard_map/query_part/pallas_call | solution.py:302
  152.1 8.8 %decode_context.1.refs_1_.refs_0_ = bf16[256,1024]{1,0:T(8,128)(2,1)S(1)} custom-call(bf16[256,1024]{1,0:T(8,128)(2,1)S(1)} %get-tuple-element.193.q_ref, bf16[1536,256]{1,0:T(8,128)(2,1)} %bitcast.3.cache_ref, f32[256,256]{1,0:T(8,128)S(1)} %copy-done.26, f32[256,1]{1,0:T(8,128)S(1)} %get-tuple-element.195.inv_ref, ...), custom_call_target="tpu_custom_call" | custom-call | flops 1610612736 | bytes 2097152 | tf_op jit(solution)/shard_map/decode_context/pallas_call | solution.py:358
  160.9 4.5 %output_part.10 = (bf16[128,1024]{1,0:T(8,128)(2,1)S(1)}, bf16[128,1024]{1,0:T(8,128)(2,1)S(1)}, bf16[128,1024]{1,0:T(8,128)(2,1)S(1)}, bf16[128,1024]{1,0:T(8,128)(2,1)S(1)}) custom-call(s32[8]{0:T(128)S(1)} %compare_select_fusion.4.blocks, bf16[256,1024]{1,0:T(8,128)(2,1)S(1)} %decode_context.1.refs_1_.refs_0_, bf16[1024,8192]{1,0:T(8,128)(2,1)} %refs_2_.11, ...), custom_call_target="tpu_custom_call" | custom-call | flops 1073741824 | bytes 8388608 | tf_op jit(solution)/shard_map/output_part/pallas_call | solution.py:448
  169.3 4.5 %output_part.11 = (bf16[128,1024]{1,0:T(8,128)(2,1)S(1)}, bf16[128,1024]{1,0:T(8,128)(2,1)S(1)}, bf16[128,1024]{1,0:T(8,128)(2,1)S(1)}, bf16[128,1024]{1,0:T(8,128)(2,1)S(1)}) custom-call(s32[8]{0:T(128)S(1)} %compare_select_fusion.4.blocks, bf16[256,1024]{1,0:T(8,128)(2,1)S(1)} %decode_context.1.refs_1_.refs_0_, bf16[1024,8192]{1,0:T(8,128)(2,1)} %refs_2_.11, ...), custom_call_target="tpu_custom_call" | custom-call | flops 1073741824 | bytes 8388608 | tf_op jit(solution)/shard_map/output_part/pallas_call | solution.py:448
  174.3 2.2 collective-permute-start.46
  176.5 5.5 %output_part.8 = (bf16[128,1024]{1,0:T(8,128)(2,1)S(1)}, bf16[128,1024]{1,0:T(8,128)(2,1)S(1)}, bf16[128,1024]{1,0:T(8,128)(2,1)S(1)}, bf16[128,1024]{1,0:T(8,12...) custom-call(s32[8]{0:T(128)S(1)} %compare_select_fusion.4.blocks, ...), custom_call_target="tpu_custom_call" | custom-call | flops 2147483648 | bytes 8388608 | tf_op jit(solution)/shard_map/output_part/pallas_call | solution.py:448
  183.2 2.3 collective-permute-start.34
  185.7 2.2 collective-permute-start.48
  187.9 5.5 %output_part.9 = (bf16[128,1024]{1,0:T(8,128)(2,1)S(1)}, bf16[128,1024]{1,0:T(8,128)(2,1)S(1)}, bf16[128,1024]{1,0:T(8,128)(2,1)S(1)}, bf16[128,1024]{1,0:T(8,12...) custom-call(s32[8]{0:T(128)S(1)} %compare_select_fusion.4.blocks, ...), custom_call_target="tpu_custom_call" | custom-call | flops 2147483648 | bytes 8388608 | tf_op jit(solution)/shard_map/output_part/pallas_call | solution.py:448
  200.6 2.7 %collective-permute-done.35.a_ref = bf16[128,1024]{1,0:T(8,128)(2,1)S(1)} collective-permute-done((bf16[128,1024]{1,0:T(8,128)(2,1)S(1)}, bf16[128,1024]{1,0:T(8,128)(2,1)S(1)}, u32[]{:S(2)}, u32[]{:S(2)}) %collective-permute-start.35) | collective-permute-done | bytes 262176 | tf_op jit(solution)/shard_map/ppermute | solution.py:473
  206.2 2.7 %collective-permute-done.49.a_ref = bf16[128,1024]{1,0:T(8,128)(2,1)S(1)} collective-permute-done((bf16[128,1024]{1,0:T(8,128)(2,1)S(1)}, bf16[128,1024]{1,0:T(8,128)(2,1)S(1)}, u32[]{:S(2)}, u32[]{:S(2)}) %collective-permute-start.49) | collective-permute-done | bytes 262176 | tf_op jit(solution)/shard_map/ppermute | solution.py:473
  211.8 2.7 %collective-permute-done.37.a_ref = bf16[128,1024]{1,0:T(8,128)(2,1)S(1)} collective-permute-done((bf16[128,1024]{1,0:T(8,128)(2,1)S(1)}, bf16[128,1024]{1,0:T(8,128)(2,1)S(1)}, u32[]{:S(2)}, u32[]{:S(2)}) %collective-permute-start.37) | collective-permute-done | bytes 262176 | tf_op jit(solution)/shard_map/ppermute | solution.py:473
  217.4 2.7 %collective-permute-done.51.a_ref = bf16[128,1024]{1,0:T(8,128)(2,1)S(1)} collective-permute-done((bf16[128,1024]{1,0:T(8,128)(2,1)S(1)}, bf16[128,1024]{1,0:T(8,128)(2,1)S(1)}, u32[]{:S(2)}, u32[]{:S(2)}) %collective-permute-start.51) | collective-permute-done | bytes 262176 | tf_op jit(solution)/shard_map/ppermute | solution.py:473
  232.3 2.7 %collective-permute-done.55.refs_2_ = bf16[128,1024]{1,0:T(8,128)(2,1)S(1)} collective-permute-done((bf16[128,1024]{1,0:T(8,128)(2,1)S(1)}, bf16[128,1024]{1,0:T(8,128)(2,1)S(1)}, u32[]{:S(2)}, u32[]{:S(2)}) %collective-permute-start.55) | collective-permute-done | bytes 262176 | tf_op jit(solution)/shard_map/ppermute | solution.py:473
  238.5 3.0 %collective-permute-done.57 = f32[8,512]{1,0:T(8,128)S(1)} collective-permute-done((f32[8,512]{1,0:T(8,128)S(1)}, f32[8,512]{1,0:T(8,128)S(1)}, u32[]{:S(2)}, u32[]{:S(2)}) %collective-permute-start.57) | collective-permute-done | bytes 16416 | tf_op jit(solution)/shard_map/ppermute | solution.py:478
  245.3 3.2 %collective-permute-start.59 = (f32[8,512]{1,0:T(8,128)S(1)}, f32[8,512]{1,0:T(8,128)S(1)}, u32[]{:S(2)}, u32[]{:S(2)}) collective-permute-start(f32[8,512]{1,0:T(8,128)S(1)} %add.68), channel_id=1, source_target_pairs={{0,8},{2,10},{4,12},{6,14},{8,0},{10,2},{12,4},{14,6},{1,9},{3,11}... | collective-permute-start | bytes 49160 | tf_op jit(solution)/shard_map/ppermute | solution.py:478
  (230 shorter events, 106.6 us)
Async XLA Ops:
  1.9 15.0 %collective-permute-start = (bf16[256,1024]{1,0:T(8,128)(2,1)S(1)}, bf16[256,1024]{1,0:T(8,128)(2,1)}, u32[]{:S(2)}, u32[]{:S(2)}) collective-permute-start(bf16[256,1024]{1,0:T(8,128)(2,1)S(1)} %get-tuple-element.253.refs_2_), channel_id=1, source_target_pairs={{0,4},{4,8},{8,12},{12,14},{14,10},{10,6},{6,2},{2,0},{1,5},{5,9},... | collective-permute-start | bytes 1572872 | tf_op jit(solution)/shard_map/ppermute | solution.py:473
  5.0 13.5 %collective-permute-start.1 = (bf16[256,1024]{1,0:T(8,128)(2,1)S(1)}, bf16[256,1024]{1,0:T(8,128)(2,1)}, u32[]{:S(2)}, u32[]{:S(2)}) collective-permute-start(bf16[256,1024]{1,0:T(8,128)(2,1)S(1)} %get-tuple-element.252.refs_2_), channel_id=1, source_target_pairs={{4,0},{8,4},{12,8},{14,12},{10,14},{6,10},{2,6},{0,2},{5,1},{9,5},... | collective-permute-start | bytes 1572872 | tf_op jit(solution)/shard_map/ppermute | solution.py:473
  18.5 16.9 %collective-permute-start.2 = (bf16[256,1024]{1,0:T(8,128)(2,1)}, bf16[256,1024]{1,0:T(8,128)(2,1)}, u32[]{:S(2)}, u32[]{:S(2)}) collective-permute-start(bf16[256,1024]{1,0:T(8,128)(2,1)} %collective-permute-done.refs_3_), channel_id=1, source_target_pairs={{0,4},{4,8},{8,12},{12,14},{14,10},{10,6},{6,2},{2,0},{1,5},{5,9},... | collective-permute-start | bytes 1572872 | tf_op jit(solution)/shard_map/ppermute | solution.py:473
  20.1 15.3 %collective-permute-start.3 = (bf16[256,1024]{1,0:T(8,128)(2,1)}, bf16[256,1024]{1,0:T(8,128)(2,1)}, u32[]{:S(2)}, u32[]{:S(2)}) collective-permute-start(bf16[256,1024]{1,0:T(8,128)(2,1)} %collective-permute-done.1.refs_3_), channel_id=1, source_target_pairs={{4,0},{8,4},{12,8},{14,12},{10,14},{6,10},{2,6},{0,2},{5,1},{9,5},... | collective-permute-start | bytes 1572872 | tf_op jit(solution)/shard_map/ppermute | solution.py:473
  20.7 13.3 %collective-permute-start.4 = (bf16[256,256]{1,0:T(8,128)(2,1)}, bf16[256,256]{1,0:T(8,128)(2,1)S(1)}, u32[]{:S(2)}, u32[]{:S(2)}) collective-permute-start(bf16[256,256]{1,0:T(8,128)(2,1)} %get-tuple-element.130), channel_id=1, source_target_pairs={{0,4},{4,8},{8,12},{12,14},{14,10},{10,6},{6,2},{2,0},{1,5},{5,9},... | collective-permute-start | bytes 393224 | tf_op jit(solution)/shard_map/ppermute | solution.py:473
  22.3 13.0 %collective-permute-start.5 = (bf16[256,256]{1,0:T(8,128)(2,1)}, bf16[256,256]{1,0:T(8,128)(2,1)S(1)}, u32[]{:S(2)}, u32[]{:S(2)}) collective-permute-start(bf16[256,256]{1,0:T(8,128)(2,1)} %copy-done.27), channel_id=1, source_target_pairs={{4,0},{8,4},{12,8},{14,12},{10,14},{6,10},{2,6},{0,2},{5,1},{9,5},... | collective-permute-start | bytes 393224 | tf_op jit(solution)/shard_map/ppermute | solution.py:473
  24.8 43.8 %collective-permute-start.18 = (bf16[96,16,256]{2,1,0:T(8,128)(2,1)}, bf16[96,16,256]{2,1,0:T(8,128)(2,1)}, u32[]{:S(2)}, u32[]{:S(2)}) collective-permute-start(bf16[96,16,256]{2,1,0:T(8,128)(2,1)} %constant_dynamic-slice_fusion), channel_id=1, source_target_pairs={{0,1},{1,0},{2,3},{3,2},{4,5},{5,4},{6,7},{7,6},{8,9},{9,8},{10,11... | collective-permute-start | bytes 2359304 | tf_op jit(solution)/shard_map/ppermute | solution.py:527
  35.4 15.8 %collective-permute-start.6 = (bf16[256,1024]{1,0:T(8,128)(2,1)}, bf16[256,1024]{1,0:T(8,128)(2,1)S(1)}, u32[]{:S(2)}, u32[]{:S(2)}) collective-permute-start(bf16[256,1024]{1,0:T(8,128)(2,1)} %collective-permute-done.2.refs_4_), channel_id=1, source_target_pairs={{0,4},{4,8},{8,12},{12,14},{14,10},{10,6},{6,2},{2,0},{1,5},{5,9},... | collective-permute-start | bytes 1572872 | tf_op jit(solution)/shard_map/ppermute | solution.py:473
  37.0 14.2 %collective-permute-start.7 = (bf16[256,1024]{1,0:T(8,128)(2,1)}, bf16[256,1024]{1,0:T(8,128)(2,1)S(1)}, u32[]{:S(2)}, u32[]{:S(2)}) collective-permute-start(bf16[256,1024]{1,0:T(8,128)(2,1)} %collective-permute-done.3.refs_4_), channel_id=1, source_target_pairs={{4,0},{8,4},{12,8},{14,12},{10,14},{6,10},{2,6},{0,2},{5,1},{9,5},... | collective-permute-start | bytes 1572872 | tf_op jit(solution)/shard_map/ppermute | solution.py:473
  37.6 12.3 %collective-permute-start.8 = (bf16[256,256]{1,0:T(8,128)(2,1)S(1)}, bf16[256,256]{1,0:T(8,128)(2,1)S(1)}, u32[]{:S(2)}, u32[]{:S(2)}) collective-permute-start(bf16[256,256]{1,0:T(8,128)(2,1)S(1)} %get-tuple-element.139), channel_id=1, source_target_pairs={{0,4},{4,8},{8,12},{12,14},{14,10},{10,6},{6,2},{2,0},{1,5},{5,9},... | collective-permute-start | bytes 393224 | tf_op jit(solution)/shard_map/ppermute | solution.py:473
  39.2 11.9 %collective-permute-start.9 = (bf16[256,256]{1,0:T(8,128)(2,1)S(1)}, bf16[256,256]{1,0:T(8,128)(2,1)S(1)}, u32[]{:S(2)}, u32[]{:S(2)}) collective-permute-start(bf16[256,256]{1,0:T(8,128)(2,1)S(1)} %get-tuple-element.140), channel_id=1, source_target_pairs={{4,0},{8,4},{12,8},{14,12},{10,14},{6,10},{2,6},{0,2},{5,1},{9,5},... | collective-permute-start | bytes 393224 | tf_op jit(solution)/shard_map/ppermute | solution.py:473
  51.2 15.0 %collective-permute-start.10 = (bf16[256,1024]{1,0:T(8,128)(2,1)S(1)}, bf16[256,1024]{1,0:T(8,128)(2,1)}, u32[]{:S(2)}, u32[]{:S(2)}) collective-permute-start(bf16[256,1024]{1,0:T(8,128)(2,1)S(1)} %collective-permute-done.6.refs_5_), channel_id=1, source_target_pairs={{0,4},{4,8},{8,12},{12,14},{14,10},{10,6},{6,2},{2,0},{1,5},{5,9},... | collective-permute-start | bytes 1572872 | tf_op jit(solution)/shard_map/ppermute | solution.py:473
  53.0 13.3 %collective-permute-start.11 = (bf16[256,1024]{1,0:T(8,128)(2,1)S(1)}, bf16[256,1024]{1,0:T(8,128)(2,1)}, u32[]{:S(2)}, u32[]{:S(2)}) collective-permute-start(bf16[256,1024]{1,0:T(8,128)(2,1)S(1)} %collective-permute-done.7.refs_5_), channel_id=1, source_target_pairs={{4,0},{8,4},{12,8},{14,12},{10,14},{6,10},{2,6},{0,2},{5,1},{9,5},... | collective-permute-start | bytes 1572872 | tf_op jit(solution)/shard_map/ppermute | solution.py:473
  66.3 19.9 %collective-permute-start.14 = (bf16[256,1024]{1,0:T(8,128)(2,1)}, bf16[256,1024]{1,0:T(8,128)(2,1)}, u32[]{:S(2)}, u32[]{:S(2)}) collective-permute-start(bf16[256,1024]{1,0:T(8,128)(2,1)} %collective-permute-done.10.refs_4_), channel_id=1, source_target_pairs={{0,4},{4,8},{8,12},{12,14},{14,10},{10,6},{6,2},{2,0},{1,5},{5,9},... | collective-permute-start | bytes 1572872 | tf_op jit(solution)/shard_map/ppermute | solution.py:473
  67.8 18.4 %collective-permute-start.15 = (bf16[256,1024]{1,0:T(8,128)(2,1)}, bf16[256,1024]{1,0:T(8,128)(2,1)}, u32[]{:S(2)}, u32[]{:S(2)}) collective-permute-start(bf16[256,1024]{1,0:T(8,128)(2,1)} %collective-permute-done.11.refs_6_), channel_id=1, source_target_pairs={{4,0},{8,4},{12,8},{14,12},{10,14},{6,10},{2,6},{0,2},{5,1},{9,5},... | collective-permute-start | bytes 1572872 | tf_op jit(solution)/shard_map/ppermute | solution.py:473
  74.3 11.8 %collective-permute-start.16 = (bf16[256,256]{1,0:T(8,128)(2,1)}, bf16[256,256]{1,0:T(8,128)(2,1)S(1)}, u32[]{:S(2)}, u32[]{:S(2)}) collective-permute-start(bf16[256,256]{1,0:T(8,128)(2,1)} %copy-done.29), channel_id=1, source_target_pairs={{0,4},{4,8},{8,12},{12,14},{14,10},{10,6},{6,2},{2,0},{1,5},{5,9},... | collective-permute-start | bytes 393224 | tf_op jit(solution)/shard_map/ppermute | solution.py:473
  86.2 16.7 %collective-permute-start.19 = (bf16[256,1024]{1,0:T(8,128)(2,1)}, bf16[256,1024]{1,0:T(8,128)(2,1)S(1)}, u32[]{:S(2)}, u32[]{:S(2)}) collective-permute-start(bf16[256,1024]{1,0:T(8,128)(2,1)} %collective-permute-done.14.refs_5_), channel_id=1, source_target_pairs={{0,4},{4,8},{8,12},{12,14},{14,10},{10,6},{6,2},{2,0},{1,5},{5,9},... | collective-permute-start | bytes 1572872 | tf_op jit(solution)/shard_map/ppermute | solution.py:473
  87.7 15.2 %collective-permute-start.20 = (bf16[256,1024]{1,0:T(8,128)(2,1)}, bf16[256,1024]{1,0:T(8,128)(2,1)S(1)}, u32[]{:S(2)}, u32[]{:S(2)}) collective-permute-start(bf16[256,1024]{1,0:T(8,128)(2,1)} %collective-permute-done.15.refs_4_), channel_id=1, source_target_pairs={{4,0},{8,4},{12,8},{14,12},{10,14},{6,10},{2,6},{0,2},{5,1},{9,5},... | collective-permute-start | bytes 1572872 | tf_op jit(solution)/shard_map/ppermute | solution.py:473
  88.3 12.4 %collective-permute-start.21 = (bf16[256,256]{1,0:T(8,128)(2,1)S(1)}, bf16[256,256]{1,0:T(8,128)(2,1)S(1)}, u32[]{:S(2)}, u32[]{:S(2)}) collective-permute-start(bf16[256,256]{1,0:T(8,128)(2,1)S(1)} %get-tuple-element.166), channel_id=1, source_target_pairs={{0,4},{4,8},{8,12},{12,14},{14,10},{10,6},{6,2},{2,0},{1,5},{5,9},... | collective-permute-start | bytes 393224 | tf_op jit(solution)/shard_map/ppermute | solution.py:473
  89.7 13.1 %collective-permute-start.22 = (bf16[256,256]{1,0:T(8,128)(2,1)S(1)}, bf16[256,256]{1,0:T(8,128)(2,1)S(1)}, u32[]{:S(2)}, u32[]{:S(2)}) collective-permute-start(bf16[256,256]{1,0:T(8,128)(2,1)S(1)} %get-tuple-element.167), channel_id=1, source_target_pairs={{4,0},{8,4},{12,8},{14,12},{10,14},{6,10},{2,6},{0,2},{5,1},{9,5},... | collective-permute-start | bytes 393224 | tf_op jit(solution)/shard_map/ppermute | solution.py:473
  102.9 14.5 %collective-permute-start.23 = (bf16[256,1024]{1,0:T(8,128)(2,1)S(1)}, bf16[256,1024]{1,0:T(8,128)(2,1)S(1)}, u32[]{:S(2)}, u32[]{:S(2)}) collective-permute-start(bf16[256,1024]{1,0:T(8,128)(2,1)S(1)} %collective-permute-done.19.refs_4_), channel_id=1, source_target_pairs={{0,4},{4,8},{8,12},{12,14},{14,10},{10,6},{6,2},{2,0},{1,5},{5,9},... | collective-permute-start | bytes 1572872 | tf_op jit(solution)/shard_map/ppermute | solution.py:473
  104.2 14.0 %collective-permute-start.26 = (bf16[256,1024]{1,0:T(8,128)(2,1)S(1)}, bf16[256,1024]{1,0:T(8,128)(2,1)S(1)}, u32[]{:S(2)}, u32[]{:S(2)}) collective-permute-start(bf16[256,1024]{1,0:T(8,128)(2,1)S(1)} %collective-permute-done.20.refs_5_), channel_id=1, source_target_pairs={{4,0},{8,4},{12,8},{14,12},{10,14},{6,10},{2,6},{0,2},{5,1},{9,5},... | collective-permute-start | bytes 1572872 | tf_op jit(solution)/shard_map/ppermute | solution.py:473
  105.0 11.7 %collective-permute-start.24 = (bf16[256,256]{1,0:T(8,128)(2,1)S(1)}, bf16[256,256]{1,0:T(8,128)(2,1)S(1)}, u32[]{:S(2)}, u32[]{:S(2)}) collective-permute-start(bf16[256,256]{1,0:T(8,128)(2,1)S(1)} %get-tuple-element.172), channel_id=1, source_target_pairs={{0,4},{4,8},{8,12},{12,14},{14,10},{10,6},{6,2},{2,0},{1,5},{5,9},... | collective-permute-start | bytes 393224 | tf_op jit(solution)/shard_map/ppermute | solution.py:473
  146.2 14.7 %collective-permute-start.31 = (bf16[128,1024]{1,0:T(8,128)(2,1)}, bf16[128,1024]{1,0:T(8,128)(2,1)}, u32[]{:S(2)}, u32[]{:S(2)}) collective-permute-start(bf16[128,1024]{1,0:T(8,128)(2,1)} %get-tuple-element.189), channel_id=1, source_target_pairs={{0,4},{4,8},{8,12},{12,14},{14,10},{10,6},{6,2},{2,0},{1,5},{5,9},... | collective-permute-start | bytes 786440 | tf_op jit(solution)/shard_map/ppermute | solution.py:473
  167.6 14.5 %collective-permute-start.32 = (bf16[128,1024]{1,0:T(8,128)(2,1)S(1)}, bf16[128,1024]{1,0:T(8,128)(2,1)S(1)}, u32[]{:S(2)}, u32[]{:S(2)}) collective-permute-start(bf16[128,1024]{1,0:T(8,128)(2,1)S(1)} %copy-done.24), channel_id=1, source_target_pairs={{4,0},{8,4},{12,8},{14,12},{10,14},{6,10},{2,6},{0,2},{5,1},{9,5},... | collective-permute-start | bytes 786440 | tf_op jit(solution)/shard_map/ppermute | solution.py:473
  174.0 11.4 %collective-permute-start.45 = (bf16[128,1024]{1,0:T(8,128)(2,1)S(1)}, bf16[128,1024]{1,0:T(8,128)(2,1)S(1)}, u32[]{:S(2)}, u32[]{:S(2)}) collective-permute-start(bf16[128,1024]{1,0:T(8,128)(2,1)S(1)} %get-tuple-element.221), channel_id=1, source_target_pairs={{0,4},{4,8},{8,12},{12,14},{14,10},{10,6},{6,2},{2,0},{1,5},{5,9},... | collective-permute-start | bytes 786440 | tf_op jit(solution)/shard_map/ppermute | solution.py:473
  174.3 11.1 %collective-permute-start.46 = (bf16[128,1024]{1,0:T(8,128)(2,1)S(1)}, bf16[128,1024]{1,0:T(8,128)(2,1)S(1)}, u32[]{:S(2)}, u32[]{:S(2)}) collective-permute-start(bf16[128,1024]{1,0:T(8,128)(2,1)S(1)} %get-tuple-element.222), channel_id=1, source_target_pairs={{4,0},{8,4},{12,8},{14,12},{10,14},{6,10},{2,6},{0,2},{5,1},{9,5},... | collective-permute-start | bytes 786440 | tf_op jit(solution)/shard_map/ppermute | solution.py:473
  185.6 12.1 %collective-permute-start.47 = (bf16[128,1024]{1,0:T(8,128)(2,1)S(1)}, bf16[128,1024]{1,0:T(8,128)(2,1)S(1)}, u32[]{:S(2)}, u32[]{:S(2)}) collective-permute-start(bf16[128,1024]{1,0:T(8,128)(2,1)S(1)} %get-tuple-element.225), channel_id=1, source_target_pairs={{0,4},{4,8},{8,12},{12,14},{14,10},{10,6},{6,2},{2,0},{1,5},{5,9},... | collective-permute-start | bytes 786440 | tf_op jit(solution)/shard_map/ppermute | solution.py:473
  185.7 12.4 %collective-permute-start.48 = (bf16[128,1024]{1,0:T(8,128)(2,1)S(1)}, bf16[128,1024]{1,0:T(8,128)(2,1)S(1)}, u32[]{:S(2)}, u32[]{:S(2)}) collective-permute-start(bf16[128,1024]{1,0:T(8,128)(2,1)S(1)} %get-tuple-element.226), channel_id=1, source_target_pairs={{4,0},{8,4},{12,8},{14,12},{10,14},{6,10},{2,6},{0,2},{5,1},{9,5},... | collective-permute-start | bytes 786440 | tf_op jit(solution)/shard_map/ppermute | solution.py:473
  198.2 10.7 %collective-permute-start.49 = (bf16[128,1024]{1,0:T(8,128)(2,1)S(1)}, bf16[128,1024]{1,0:T(8,128)(2,1)S(1)}, u32[]{:S(2)}, u32[]{:S(2)}) collective-permute-start(bf16[128,1024]{1,0:T(8,128)(2,1)S(1)} %get-tuple-element.229), channel_id=1, source_target_pairs={{0,4},{4,8},{8,12},{12,14},{14,10},{10,6},{6,2},{2,0},{1,5},{5,9},... | collective-permute-start | bytes 786440 | tf_op jit(solution)/shard_map/ppermute | solution.py:473
  203.8 10.7 %collective-permute-start.37 = (bf16[128,1024]{1,0:T(8,128)(2,1)S(1)}, bf16[128,1024]{1,0:T(8,128)(2,1)S(1)}, u32[]{:S(2)}, u32[]{:S(2)}) collective-permute-start(bf16[128,1024]{1,0:T(8,128)(2,1)S(1)} %get-tuple-element.206), channel_id=1, source_target_pairs={{0,4},{4,8},{8,12},{12,14},{14,10},{10,6},{6,2},{2,0},{1,5},{5,9},... | collective-permute-start | bytes 786440 | tf_op jit(solution)/shard_map/ppermute | solution.py:473
  209.5 10.7 %collective-permute-start.51 = (bf16[128,1024]{1,0:T(8,128)(2,1)S(1)}, bf16[128,1024]{1,0:T(8,128)(2,1)S(1)}, u32[]{:S(2)}, u32[]{:S(2)}) collective-permute-start(bf16[128,1024]{1,0:T(8,128)(2,1)S(1)} %get-tuple-element.233), channel_id=1, source_target_pairs={{0,4},{4,8},{8,12},{12,14},{14,10},{10,6},{6,2},{2,0},{1,5},{5,9},... | collective-permute-start | bytes 786440 | tf_op jit(solution)/shard_map/ppermute | solution.py:473
  (63 other events, 533.4 us)

commit v3 on v2

--- a/solution.py
+++ b/solution.py
@@ -19,6 +19,7 @@
 
 ORDER = (0, 2, 4, 6, 7, 5, 3, 1)
 RING = len(ORDER)
+FAR = RING // 2
 FORWARD = [(ORDER[i], ORDER[(i + 1) % RING]) for i in range(RING)]
 BACKWARD = [(b, a) for a, b in FORWARD]
 
@@ -85,12 +86,9 @@
     out_ref[0] = result
     half = forward_ref.shape[0]
 
-    @pl.when(k == RING - 1)
+    @pl.when(k == FAR)
     def _():
         forward_ref[...] = result[:half]
-
-    @pl.when(k == 1)
-    def _():
         backward_ref[...] = result[half:]
 
 
@@ -123,77 +121,112 @@
 
 
 def add_pairs_kernel(a_ref, b_ref, pa_ref, pb_ref, oa_ref, ob_ref):
-    for arrived, part, out in ((a_ref, pa_ref, oa_ref), (b_ref, pb_ref, ob_ref)):
-        out[...] = (arrived[...].astype(jnp.float32) + part[0].astype(jnp.float32)).astype(
-            out.dtype
-        )
-
-
-def add_pairs(ahead, back, parts, ka, kb, dtype):
-    rows, columns = ahead.shape
+    rows, half = oa_ref.shape[0], oa_ref.shape[0] // 2
+    sides = ((a_ref, pa_ref, oa_ref, 0), (b_ref, pb_ref, ob_ref, half))
+    for arrived, part, out, low in sides:
+        if arrived.shape[0] == rows:
+            total = arrived[...].astype(jnp.float32) + part[0].astype(jnp.float32)
+            out[...] = total.astype(out.dtype)
+        else:
+            out[...] = part[0]
+            at = slice(low, low + half)
+            total = arrived[...].astype(jnp.float32) + part[0, at].astype(jnp.float32)
+            out[at] = total.astype(out.dtype)
+
+
+def add_pairs(ahead, back, parts, ka, kb):
+    _, rows, columns = parts.shape
+    whole = lambda array: pl.BlockSpec(array.shape, lambda i: (0, 0))
     flat = pl.BlockSpec((rows, columns), lambda i: (0, 0))
     return pl.pallas_call(
         add_pairs_kernel,
         grid=(1,),
         in_specs=[
-            flat,
-            flat,
+            whole(ahead),
+            whole(back),
             pl.BlockSpec((1, rows, columns), lambda i: (ka, 0, 0)),
-            pl.BlockSpec((1, rows, columns), lambda i: (kb, 1, 0)),
+            pl.BlockSpec((1, rows, columns), lambda i: (kb, 0, 0)),
         ],
         out_specs=[flat, flat],
-        out_shape=[shaped((rows, columns), dtype)] * 2,
-        compiler_params=VMEM,
-        cost_estimate=cost(2 * ahead.size, 16 * ahead.size),
+        out_shape=[shaped((rows, columns), jnp.bfloat16)] * 2,
+        compiler_params=VMEM,
+        cost_estimate=cost(2 * rows * columns, 12 * rows * columns),
         name="add_pairs",
     )(ahead, back, parts, parts)
 
 
-def add_kernel(a_ref, b_ref, pa_ref, pb_ref, oa_ref, ob_ref):
-    for arrived, part, out in ((a_ref, pa_ref, oa_ref), (b_ref, pb_ref, ob_ref)):
+def end_pairs_kernel(a_ref, b_ref, part_ref, prefill_ref, decode_ref):
+    half = prefill_ref.shape[0]
+    total = a_ref[...].astype(jnp.float32) + b_ref[...].astype(jnp.float32)
+    total += part_ref[0].astype(jnp.float32)
+    prefill_ref[...] = total[:half]
+    decode_ref[...] = total[half:]
+
+
+def end_pairs(ahead, back, parts):
+    _, rows, columns = parts.shape
+    flat = pl.BlockSpec((rows, columns), lambda i: (0, 0))
+    half = pl.BlockSpec((rows // 2, columns), lambda i: (0, 0))
+    return pl.pallas_call(
+        end_pairs_kernel,
+        grid=(1,),
+        in_specs=[flat, flat, pl.BlockSpec((1, rows, columns), lambda i: (0, 0, 0))],
+        out_specs=[half, half],
+        out_shape=[shaped((rows // 2, columns), jnp.float32)] * 2,
+        compiler_params=VMEM,
+        cost_estimate=cost(2 * rows * columns, 10 * rows * columns),
+        name="end_pairs",
+    )(ahead, back, parts)
+
+
+def add_kernel(*refs):
+    count = len(refs) // 3
+    for arrived, part, out in zip(refs[:count], refs[count : 2 * count], refs[2 * count :]):
         out[...] = (arrived[...].astype(jnp.float32) + part[...].astype(jnp.float32)).astype(
             out.dtype
         )
 
 
-def add_parts(ahead, back, part_ahead, part_back):
-    rows, columns = ahead.shape
+def add_parts(arrived, parts):
+    rows, columns = arrived[0].shape
+    count = len(arrived)
     flat = pl.BlockSpec((rows, columns), lambda i: (0, 0))
     return pl.pallas_call(
         add_kernel,
         grid=(1,),
-        in_specs=[flat] * 4,
-        out_specs=[flat, flat],
-        out_shape=[shaped((rows, columns), ahead.dtype)] * 2,
-        compiler_params=VMEM,
-        cost_estimate=cost(2 * ahead.size, 16 * ahead.size),
+        in_specs=[flat] * (2 * count),
+        out_specs=[flat] * count,
+        out_shape=[shaped((rows, columns), jnp.bfloat16)] * count,
+        compiler_params=VMEM,
+        cost_estimate=cost(count * rows * columns, 6 * count * rows * columns),
         name="add_parts",
-    )(ahead, back, part_ahead, part_back)
+    )(*arrived, *parts)
 
 
 def last_kernel(x_ref, *refs):
-    arrived, parts, (mixed_ref, hidden_ref, square_ref) = refs[:4], refs[4:8], refs[8:]
-    rows = arrived[0].shape[0]
+    terms, (mixed_ref, hidden_ref, square_ref) = (refs[:3], refs[3:6]), refs[6:]
+    rows = refs[0].shape[0]
     sums = []
-    for i in range(4):
+    for i in range(2):
         at = slice(i * rows, (i + 1) * rows)
-        added = arrived[i][...].astype(jnp.float32) + parts[i][...].astype(jnp.float32)
-        mixed = x_ref[at].astype(jnp.float32) + added
+        mixed = x_ref[at].astype(jnp.float32)
+        for term in terms[i]:
+            mixed += term[...].astype(jnp.float32)
         mixed_ref[at] = mixed
         hidden_ref[at] = mixed.astype(jnp.bfloat16)
         sums.append(jnp.sum(mixed * mixed, axis=1, keepdims=True))
-    column = jnp.broadcast_to(jnp.concatenate(sums, axis=0), (4 * rows, 128))
+    column = jnp.broadcast_to(jnp.concatenate(sums, axis=0), (2 * rows, 128))
     square_ref[...] = column.T[: square_ref.shape[0]]
 
 
-def last_parts(x, arrived, parts):
+def last_parts(x, prefill, decode):
     rows, columns = x.shape
     flat = pl.BlockSpec((rows, columns), lambda i: (0, 0))
-    quarter = pl.BlockSpec((rows // 4, columns), lambda i: (0, 0))
+    half = pl.BlockSpec((rows // 2, columns), lambda i: (0, 0))
     return pl.pallas_call(
         last_kernel,
         grid=(1,),
-        in_specs=[flat] + [quarter] * 8,
+        in_specs=[flat] + [half] * 6,
         out_specs=[flat, flat, pl.BlockSpec((8, rows), lambda i: (0, 0))],
         out_shape=[
             shaped((rows, columns), jnp.float32),
@@ -203,7 +236,7 @@
         compiler_params=VMEM,
         cost_estimate=cost(4 * x.size, 12 * x.size),
         name="last_parts",
-    )(x, *arrived, *parts)
+    )(x, *prefill, *decode)
 
 
 def norm_kernel(width, mixed_ref, square_ref, gain_ref, out_ref):
@@ -276,12 +309,12 @@
     return block
 
 
-def query_part(places, pieces, gain_row, weight, blocks, sums=None, angles=None):
+def query_part(places, pieces, gain_row, weight, blocks, sums=None, angles=None, at=0):
     count = len(places)
     rows_each, depth = pieces[0].shape
     rows, width = len(pieces) // count * rows_each, weight.shape[1]
     first, last = sums is None, angles is not None
-    whole = lambda shape: pl.BlockSpec(shape, lambda k, b: (0, 0))
+    whole = lambda shape, at=0: pl.BlockSpec(shape, lambda k, b: (at, 0))
     sum_shapes = [(rows, width), (rows, 1)]
     in_specs = [
         pl.BlockSpec((1, depth), lambda k, b: (0, pick(places, k, b))),
@@ -289,7 +322,7 @@
     ]
     operands = [gain_row, weight]
     if not first:
-        in_specs += [whole(s) for s in sum_shapes]
+        in_specs += [whole(s, at) for s in sum_shapes]
         operands += sums
     scratch = [pltpu.VMEM((rows, depth), jnp.bfloat16)]
     if last:
@@ -322,18 +355,10 @@
 
 
 def decode_kernel(
-    page_size, q_ref, cache_ref, pairs_ref, inv_ref, cos_ref, sin_ref, page_ref, pos_ref,
-    out_ref, bias, new_key, new_value,
+    q_ref, cache_ref, bias_ref, pairs_ref, inv_ref, cos_ref, sin_ref, out_ref, new_key, new_value
 ):
     @pl.when(pl.program_id(0) == 0)
     def _():
-        token = lax.broadcasted_iota(jnp.int32, bias.shape, 1)
-        page, offset = token // page_size, token % page_size
-        times = jnp.zeros(bias.shape, jnp.float32)
-        for j in range(page_ref.shape[1]):
-            hit = (page == page_ref[:, j : j + 1]) & (offset + j * page_size < pos_ref[...])
-            times += jnp.where(hit, 1.0, 0.0)
-        bias[...] = jnp.where(times > 0, jnp.log2(jnp.maximum(times, 1.0)), NEGATIVE)
         keys, values = new_pairs(pairs_ref, inv_ref, cos_ref, sin_ref)
         new_key[...] = keys.astype(jnp.float32)
         new_value[...] = values.astype(jnp.float32)
@@ -341,7 +366,7 @@
     for head in range(q_ref.shape[1] // HEAD_SIZE):
         at = slice(head * HEAD_SIZE, (head + 1) * HEAD_SIZE)
         q = q_ref[:, at]
-        score = dot_t(q, cache_ref[:, :HEAD_SIZE]) * FACTOR2 + bias[...]
+        score = dot_t(q, cache_ref[:, :HEAD_SIZE]) * FACTOR2 + bias_ref[...]
         own = jnp.sum(q.astype(jnp.float32) * new_key[...], axis=1, keepdims=True) * FACTOR2
         peak = jnp.maximum(jnp.max(score, axis=1, keepdims=True), own)
         grown, grown_own = jnp.exp2(score - peak), jnp.exp2(own - peak)
@@ -350,20 +375,18 @@
         out_ref[:, at] = ((context + grown_own * new_value[...]) * scale).astype(jnp.bfloat16)
 
 
-def decode_context(q, cache, pairs, inv, cosine, sine, page_table, positions, page_size):
-    rows, width = positions.shape[0], q.shape[1]
+def decode_context(q, cache, bias, pairs, inv, cosine, sine):
+    rows, width = q.shape
     heads = min(4 * HEAD_SIZE, width)
     tokens = cache.shape[0]
     whole = lambda array: pl.BlockSpec(array.shape, lambda h: (0, 0))
     return pl.pallas_call(
-        functools.partial(decode_kernel, page_size),
+        decode_kernel,
         grid=(width // heads,),
-        in_specs=[pl.BlockSpec((rows, heads), lambda h: (0, h)), whole(cache), whole(pairs)]
-        + [whole(inv), whole(cosine), whole(sine)]
-        + [whole(page_table), whole(positions)],
+        in_specs=[pl.BlockSpec((rows, heads), lambda h: (0, h))]
+        + [whole(a) for a in (cache, bias, pairs, inv, cosine, sine)],
         out_specs=pl.BlockSpec((rows, heads), lambda h: (0, h)),
         scratch_shapes=[
-            pltpu.VMEM((rows, tokens), jnp.float32),
             pltpu.VMEM((rows, HEAD_SIZE), jnp.float32),
             pltpu.VMEM((rows, HEAD_SIZE), jnp.float32),
         ],
@@ -371,24 +394,16 @@
         compiler_params=VMEM,
         cost_estimate=cost(4 * rows * width * tokens, 8 * rows * width, 2 * width * tokens),
         name="decode_context",
-    )(q, cache, pairs, inv, cosine, sine, page_table, positions)
+    )(q, cache, bias, pairs, inv, cosine, sine)
 
 
 def prefill_kernel(
-    q_ref, prefix_ref, pairs_ref, inv_ref, cos_ref, sin_ref, request_ref, column_ref, owner_ref,
-    out_ref, bias, keys, values,
+    q_ref, prefix_ref, bias_ref, pairs_ref, inv_ref, cos_ref, sin_ref, out_ref, keys, values
 ):
     old = prefix_ref.shape[0]
 
     @pl.when(pl.program_id(0) == 0)
     def _():
-        rows = request_ref.shape[0]
-        request = request_ref[...]
-        bias[:, :old] = jnp.where(request == owner_ref[...], 0.0, NEGATIVE)
-        row = lax.broadcasted_iota(jnp.int32, (rows, rows), 0)
-        column = lax.broadcasted_iota(jnp.int32, (rows, rows), 1)
-        allowed = (request == column_ref[...]) & (column <= row)
-        bias[:, old:] = jnp.where(allowed, 0.0, NEGATIVE)
         new_keys, new_values = new_pairs(pairs_ref, inv_ref, cos_ref, sin_ref)
         keys[:old] = prefix_ref[:, :HEAD_SIZE]
         keys[old:] = new_keys
@@ -397,28 +412,25 @@
 
     for head in range(q_ref.shape[1] // HEAD_SIZE):
         at = slice(head * HEAD_SIZE, (head + 1) * HEAD_SIZE)
-        score = dot_t(q_ref[:, at], keys[...]) * FACTOR2 + bias[...]
+        score = dot_t(q_ref[:, at], keys[...]) * FACTOR2 + bias_ref[...]
         grown = jnp.exp2(score - jnp.max(score, axis=1, keepdims=True))
         scale = 1.0 / jnp.sum(grown, axis=1, keepdims=True)
         context = dot(grown.astype(jnp.bfloat16), values[...]) * scale
         out_ref[:, at] = context.astype(jnp.bfloat16)
 
 
-def prefill_context(q, prefix, pairs, inv, cosine, sine, request, owner):
-    rows, width = request.shape[0], q.shape[1]
+def prefill_context(q, prefix, bias, pairs, inv, cosine, sine):
+    rows, width = q.shape
     heads = min(4 * HEAD_SIZE, width)
     tokens = prefix.shape[0] + rows
     whole = lambda array: pl.BlockSpec(array.shape, lambda h: (0, 0))
-    maps = (request[:, None], request[None, :], owner[None, :])
     return pl.pallas_call(
         prefill_kernel,
         grid=(width // heads,),
-        in_specs=[pl.BlockSpec((rows, heads), lambda h: (0, h)), whole(prefix), whole(pairs)]
-        + [whole(inv), whole(cosine), whole(sine)]
-        + [whole(a) for a in maps],
+        in_specs=[pl.BlockSpec((rows, heads), lambda h: (0, h))]
+        + [whole(a) for a in (prefix, bias, pairs, inv, cosine, sine)],
         out_specs=pl.BlockSpec((rows, heads), lambda h: (0, h)),
         scratch_shapes=[
-            pltpu.VMEM((rows, tokens), jnp.float32),
             pltpu.VMEM((tokens, HEAD_SIZE), jnp.bfloat16),
             pltpu.VMEM((tokens, HEAD_SIZE), jnp.bfloat16),
         ],
@@ -426,43 +438,76 @@
         compiler_params=VMEM,
         cost_estimate=cost(4 * rows * width * tokens, 8 * rows * width, 2 * width * tokens),
         name="prefill_context",
-    )(q, prefix, pairs, inv, cosine, sine, *maps)
-
-
-def output_kernel(count, blocks, *refs):
-    contexts, (wa_ref, wb_ref), outs = refs[:count], refs[count : count + 2], refs[count + 2 :]
-    quarter = outs[0].shape[0]
-    for w_ref, results in ((wa_ref, outs[: 2 * count]), (wb_ref, outs[2 * count :])):
-        for i, context_ref in enumerate(contexts):
-            result = dot(context_ref[...], w_ref[...]).astype(jnp.bfloat16)
-            results[2 * i][...] = result[:quarter]
-            results[2 * i + 1][...] = result[quarter:]
-
-
-def output_part(contexts, weight, places, blocks, tiles=4):
+    )(q, prefix, bias, pairs, inv, cosine, sine)
+
+
+def masks_kernel(
+    page_size, request_ref, column_ref, owner_ref, page_ref, pos_ref, prefill_ref, decode_ref
+):
+    old = owner_ref.shape[1]
+    rows = request_ref.shape[0]
+    request = request_ref[...]
+    prefill_ref[:, :old] = jnp.where(request == owner_ref[...], 0.0, NEGATIVE)
+    row = lax.broadcasted_iota(jnp.int32, (rows, rows), 0)
+    column = lax.broadcasted_iota(jnp.int32, (rows, rows), 1)
+    allowed = (request == column_ref[...]) & (column <= row)
+    prefill_ref[:, old:] = jnp.where(allowed, 0.0, NEGATIVE)
+
+    token = lax.broadcasted_iota(jnp.int32, decode_ref.shape, 1)
+    page, offset = token // page_size, token % page_size
+    times = jnp.zeros(decode_ref.shape, jnp.float32)
+    for j in range(page_ref.shape[1]):
+        hit = (page == page_ref[:, j : j + 1]) & (offset + j * page_size < pos_ref[...])
+        times += jnp.where(hit, 1.0, 0.0)
+    decode_ref[...] = jnp.where(times > 0, jnp.log2(jnp.maximum(times, 1.0)), NEGATIVE)
+
+
+def masks(request, owner, page_table, positions, tokens, page_size):
+    rows, decode = request.shape[0], positions.shape[0]
+    operands = (
+        request[:, None], request[None, :], owner[None, :], page_table, positions[:, None]
+    )
+    outs = [(rows, owner.shape[0] + rows), (decode, tokens)]
+    return pl.pallas_call(
+        functools.partial(masks_kernel, page_size),
+        grid=(1,),
+        in_specs=[pl.BlockSpec(a.shape, lambda i: (0, 0)) for a in operands],
+        out_specs=[pl.BlockSpec(a, lambda i: (0, 0)) for a in outs],
+        out_shape=[shaped(a, jnp.float32) for a in outs],
+        compiler_params=VMEM,
+        cost_estimate=cost(20 * decode * tokens, 4 * decode * tokens),
+        name="masks",
+    )(*operands)
+
+
+def output_kernel(count, jobs, blocks, *refs):
+    contexts, weights, outs = refs[:count], refs[count : -len(jobs)], refs[-len(jobs) :]
+    for (c, w), out in zip(jobs, outs):
+        out[...] = dot(contexts[c][...], weights[w][...]).astype(jnp.bfloat16)
+
+
+def output_part(contexts, weight, places, blocks, jobs=None, tiles=4):
     rows, depth = contexts[0].shape
     columns = weight.shape[1] // RING
     tile = columns // tiles
     count = len(contexts)
-    pa, pb = places
-    outs = pl.pallas_call(
-        functools.partial(output_kernel, count),
+    jobs = jobs or [(c, w) for w in range(len(places)) for c in range(count)]
+    return pl.pallas_call(
+        functools.partial(output_kernel, count, tuple(jobs)),
         grid_spec=pltpu.PrefetchScalarGridSpec(
             num_scalar_prefetch=1,
             grid=(tiles,),
             in_specs=[pl.BlockSpec((rows, depth), lambda t, b: (0, 0))] * count
-            + [
-                pl.BlockSpec((depth, tile), lambda t, b: (0, b[pa] * tiles + t)),
-                pl.BlockSpec((depth, tile), lambda t, b: (0, b[pb] * tiles + t)),
-            ],
-            out_specs=[pl.BlockSpec((rows // 2, tile), lambda t, b: (0, t))] * (4 * count),
+            + [pl.BlockSpec((depth, tile), lambda t, b, p=p: (0, b[p] * tiles + t)) for p in places],
+            out_specs=[pl.BlockSpec((rows, tile), lambda t, b: (0, t))] * len(jobs),
         ),
-        out_shape=[shaped((rows // 2, columns), jnp.bfloat16)] * (4 * count),
-        compiler_params=VMEM,
-        cost_estimate=cost(4 * count * rows * depth * columns, 8 * depth * columns),
+        out_shape=[shaped((rows, columns), jnp.bfloat16)] * len(jobs),
+        compiler_params=VMEM,
+        cost_estimate=cost(
+            2 * len(jobs) * rows * depth * columns, 2 * len(places) * depth * columns
+        ),
         name="output_part",
-    )(blocks, *contexts, weight, weight)
-    return {pa: outs[: 2 * count], pb: outs[2 * count :]}
+    )(blocks, *contexts, *([weight] * len(places)))
 
 
 def after(array, *others):
@@ -474,11 +519,11 @@
 
 
 def sum_squares(squares):
-    for low in (1, 2, 4):
-        squares = squares + lax.ppermute(
-            squares, "tensor", [(t, t ^ low) for t in range(RING)]
-        )
-    return squares
+    def partner(other):
+        return lax.ppermute(squares, "tensor", [(t, t ^ other) for t in range(RING)])
+
+    squares = squares + partner(1)
+    return squares + partner(2) + partner(4) + partner(6)
 
 
 def body(
@@ -507,20 +552,22 @@
 
     ring = lax.axis_size("tensor") == RING
     if ring:
-        gathered = [[inputs[:prefill]], [inputs[prefill:]]]
+        ahead, back = [inputs], [inputs]
 
         def gather_hop(*others):
-            sent = [pieces[-1] for pieces in gathered]
+            sent = ahead[-1], back[-1]
+            if len(ahead) == FAR:
+                sent = sent[0][:prefill], sent[1][prefill:]
             if others:
                 sent = lax.optimization_barrier((*sent, *others))[:2]
-            for pieces, arrived in zip(gathered, hop(*sent)):
+            for pieces, arrived in zip((ahead, back), hop(*sent)):
                 pieces.append(arrived)
 
         gather_hop()
         token = lax.ppermute(inputs[:16, :HEAD_SIZE], "replica", [(0, 1), (1, 0)])
         local = after(inputs, token)
         page_pool, positions, request_lengths, prefix_pages = lax.optimization_barrier(
-            (page_pool, positions, request_lengths, prefix_pages, gathered[0][1])
+            (page_pool, positions, request_lengths, prefix_pages, token)
         )[:4]
 
     own_pool = lax.dynamic_slice_in_dim(page_pool, group * pair, pair, 2)
@@ -538,15 +585,14 @@
     request, span = span_layout(request_lengths[0], prefix, prefill, page_size)
     cosine, sine = tables(jnp.concatenate([span, positions]))
     angles = ((cosine[:prefill], sine[:prefill]), (cosine[prefill:], sine[prefill:]))
+    bias = masks(request, owner, page_table, positions, cache.shape[0], page_size)
     gain_row = entry_gain[None, :]
 
     def attend_prefill(q, pairs, inv):
-        return prefill_context(q, prefix_rows, pairs, inv, *angles[0], request, owner)
+        return prefill_context(q, prefix_rows, bias[0], pairs, inv, *angles[0])
 
     def attend_decode(q, pairs, inv):
-        return decode_context(
-            q, cache, pairs, inv, *angles[1], page_table, positions[:, None], page_size
-        )
+        return decode_context(q, cache, bias[1], pairs, inv, *angles[1])
 
     exit_row = lax.dynamic_slice_in_dim(exit_gain, me * width, width, 0)
     exit_row = exit_row.astype(jnp.float32)[None, :]
@@ -557,65 +603,52 @@
         blocks = jnp.where(places < RING // 2, 2 * places, 2 * (RING - places) - 1)
         parts, *moving = pairs_partial(local, gain_row, key_value_matrix, blocks)
 
-        def pairs_hop(moving, s):
-            moving = lax.optimization_barrier((*moving, gathered[0][s], gathered[1][s]))[:2]
-            dtype = jnp.float32 if s == RING - 1 else jnp.bfloat16
-            return add_pairs(*hop(*moving), parts, RING - 1 - s, (1 + s) % RING, dtype)
-
-        def query(side, hops, sums=None, angles=None):
-            places = [(-s if side == 0 else s) % RING for s in hops]
-            pieces = [gathered[side][s] for s in hops]
+        def query(places, sums=None, **more):
+            pieces = [back[k] if k < FAR else ahead[RING - k] for k in places]
+            return query_part(places, pieces, gain_row, query_weight, blocks, sums, **more)
+
+        def query_end(pieces, which, sums):
             return query_part(
-                places, pieces, gain_row, query_weight, blocks, sums, angles
+                (FAR,), pieces, gain_row, query_weight, blocks, sums, angles[which], which
             )
 
+        def pairs_hop(moving, *others):
+            return lax.optimization_barrier((*hop(*moving), *others))[:2]
+
+        moving = add_pairs(*hop(*moving), parts, 3, 5)
         gather_hop(*moving)
-        moving = pairs_hop(moving, 1)
+        sums = query((0, 1, 7))
+        moving = add_pairs(*pairs_hop(moving, sums[1]), parts, 2, 6)
         gather_hop(*moving)
-        moving = pairs_hop(moving, 2)
+        sums = query((2, 6), sums)
+        moving = pairs_hop(moving, sums[1], cache, *bias, *angles[0], *angles[1])
+        moving = add_pairs(*moving, parts, 1, 7)
         gather_hop(*moving)
-        moving = pairs_hop(moving, 3)
-        sums = [query(0, (0, 1, 2, 3)), None]
-        gather_hop(*moving, sums[0][1])
-        moving = pairs_hop(moving, 4)
-        sums[1] = query(1, (0, 1, 2, 3, 4))
-        gather_hop(*moving, sums[1][1], cache, *angles[0], *angles[1])
-        moving = pairs_hop(moving, 5)
-        sums[0] = query(0, (4, 5), sums[0])
-        gather_hop(*moving, sums[0][1])
-        moving = pairs_hop(moving, 6)
-        sums[1] = query(1, (5, 6), sums[1])
-        sums[0] = query(0, (6,), sums[0])
-        moving = lax.optimization_barrier((*moving, sums[0][1], sums[1][1]))[:2]
-        pairs = pairs_hop(moving, 7)
-        q, inv = query(0, (7,), sums[0], angles[0])
+        sums = query((3, 5), sums)
+        pairs = end_pairs(*pairs_hop(moving, sums[1]), parts)
+
+        q, inv = query_end([ahead[FAR]], 0, sums)
         prefilled = attend_prefill(q, pairs[0], inv)
-        parts = [output_part([prefilled], output_weight, (7, 1), blocks), None]
-        first = hop(parts[0][7][0], parts[0][1][1])
-        parts[0] |= output_part([prefilled], output_weight, (6, 2), blocks)
-        q, inv = query(1, (7,), sums[1], angles[1])
-        second = hop(*add_parts(*first, parts[0][6][0], parts[0][2][1]))
-        decoded = attend_decode(after(q, first[0]), pairs[1], inv)
-        decoded_late = after(decoded, second[0])
-        parts[1] = output_part([decoded_late], output_weight, (7, 1), blocks)
-        parts[1] |= output_part([decoded_late], output_weight, (6, 2), blocks)
-        for places in ((5, 3), (4, 0)):
-            both = output_part([prefilled, decoded], output_weight, places, blocks)
-            for i in range(2):
-                parts[i] |= {k: both[k][2 * i : 2 * i + 2] for k in places}
-        running = [second, (parts[1][7][0], parts[1][1][1])]
-        for s in range(1, RING):
-            for i in range(2):
-                if i == 0 and s <= 2:
-                    moved = second
-                else:
-                    moved = hop(*running[i])
-                if s < RING - 1 and not (i == 0 and s == 1):
-                    moved = add_parts(*moved, parts[i][RING - 1 - s][0], parts[i][1 + s][1])
-                running[i] = moved
-        mixed, hidden, squares = last_parts(
-            inputs, [*running[0], *running[1]], [*parts[0][0], *parts[1][0]]
+        p4, p5 = output_part([prefilled], output_weight, (4, 5), blocks)
+        p_ahead, p_back = hop(p4, p5)
+        q, inv = query_end([back[FAR]], 1, sums)
+        decoded = attend_decode(q, pairs[1], inv)
+        d4, d3 = output_part(
+            [lax.optimization_barrier((decoded, p_ahead, p_back))[0]], output_weight, (4, 3), blocks
         )
+        d_ahead, d_back = hop(d3, d4)
+        both = [prefilled, decoded]
+        p3, d5 = output_part(both, output_weight, (3, 5), blocks, [(0, 0), (1, 1)])
+        p6, d6, p2, d2 = output_part(both, output_weight, (6, 2), blocks)
+        p_ahead, p_back = hop(*add_parts((p_ahead, p_back), (p3, p6)))
+        d_ahead, d_back = hop(*add_parts((d_ahead, d_back), (d2, d5)))
+        p7, d7, p1, d1 = output_part(both, output_weight, (7, 1), blocks)
+        p_ahead, p_back = hop(*add_parts((p_ahead, p_back), (p2, p7)))
+        d_ahead, d_back = hop(*add_parts((d_ahead, d_back), (d1, d6)))
+        p0, d0 = output_part(both, output_weight, (0,), blocks)
+        p_ahead = lax.ppermute(add_parts((p_ahead,), (p1,))[0], "tensor", FORWARD)
+        d_back = lax.ppermute(add_parts((d_back,), (d7,))[0], "tensor", BACKWARD)
+        mixed, hidden, squares = last_parts(inputs, (p_ahead, p_back, p0), (d_ahead, d_back, d0))
         return hidden, norm_out(mixed, sum_squares(squares), exit_row, exit_gain.shape[0])
 
     rows = lax.all_gather(inputs, "tensor", axis=1, tiled=True).astype(jnp.float32)

time: 253 us -> 228 us (0.901)
  starting transfers between devices: 67.4 us -> 35.7 us
  waiting for transfers between devices: 64.6 us -> 76.3 us
  Pallas kernels: 91 us -> 83.8 us
    ppermute x28 -> x14, starting transfers between devices: 33.5 us -> 7.79 us  [hop(): lax.ppermute(ahead, 'tensor', FORWARD)]
    ppermute x28 -> x14, waiting for transfers between devices: 44.5 us -> 65.6 us  [hop(): lax.ppermute(ahead, 'tensor', FORWARD)]
    ppermute x28 -> x14, starting transfers between devices: 27.9 us -> 20.4 us  [hop(): lax.ppermute(back, 'tensor', BACKWARD)]
    ppermute x28 -> x14, waiting for transfers between devices: 14.3 us -> 7.43 us  [hop(): lax.ppermute(back, 'tensor', BACKWARD)]
    pallas_call x7 -> x5, Pallas kernels: 33.4 us -> 27.8 us  [query_part(): pl.pallas_call(functools.partial(query_kernel, count, first, last, weight...]
    ppermute x3 -> x7, waiting for transfers between devices: 5.76 us -> 3.29 us  [the longest x4 3.02 us: partner(): lax.ppermute(squares, 'tensor', [(t, t ^ other) for t in range(RING)])]
    pallas_call x27 -> x19, Pallas kernels: 44.6 us -> 42.8 us  [the longest x6 28.7 us: output_part(): pl.pallas_call(functools.partial(output_kernel, count, tuple(jobs)), grid...]
    ppermute x3 -> x7, starting transfers between devices: 5.95 us -> 7.37 us  [the longest x4 6.14 us: partner(): lax.ppermute(squares, 'tensor', [(t, t ^ other) for t in range(RING)])]
  transfers between devices with their start and end apart: 60 -> 36, of which waited for: 31 -> 15; matrix products, arithmetic and copies ran while one was open for 6% -> 8% of each run, Pallas kernels for 29% -> 33%
where the time goes in v3:
time: 228 us; the launch traced here: 226 us
  Pallas kernels  83.8 us (37%)
  waiting for transfers between devices  76.3 us (33%)
  starting transfers between devices  35.7 us (16%)
  local copies, waits for them, and re-layouts  26.1 us (11%)
  other arithmetic  3.21 us (1%)
    ppermute x14, waiting for transfers between devices, hop(): lax.ppermute(ahead, 'tensor', FORWARD)  65.6 us
    pallas_call x6, Pallas kernels, output_part(): pl.pallas_call(functools.partial(output_kernel, count, tuple(jobs)), grid...  28.7 us
    pallas_call x5, Pallas kernels, query_part(): pl.pallas_call(functools.partial(query_kernel, count, first, last, weight...  27.8 us
    ppermute x14, starting transfers between devices, hop(): lax.ppermute(back, 'tensor', BACKWARD)  20.4 us
    unnamed x49, local copies, waits for them, and re-layouts  13.3 us
    pallas_call x1, Pallas kernels, pairs_partial(): pl.pallas_call(pairs_kernel, grid_spec=pltpu.PrefetchScalarGridSpec(num_s...  7.98 us
    ppermute x14, starting transfers between devices, hop(): lax.ppermute(ahead, 'tensor', FORWARD)  7.79 us
    pallas_call x1, Pallas kernels, decode_context(): pl.pallas_call(decode_kernel, grid=(width // heads,), in_specs=[pl.BlockS...  7.64 us
  transfers between devices with their start and end apart: 36, of which 15 were waited for; matrix products, arithmetic and copies ran while one was open for 8% of the time, Pallas kernels for 33%

profile of v3, /device:TPU:0, one launch (start us, length us, event | category | flops | bytes accessed | tf_op | source)
XLA Modules:
  0.0 226.3 jit_solution(9728646232135972390)
XLA Ops:
  0.6 3.0 %collective-permute-start = (bf16[512,1024]{1,0:T(8,128)(2,1)}, bf16[512,1024]{1,0:T(8,128)(2,1)}, u32[]{:S(2)}, u32[]{:S(2)}) collective-permute-start(bf16[512,1024]{1,0:T(8,128)(2,1)} %x_ref.2), channel_id=1, source_target_pairs={{4,0},{8,4},{12,8},{14,12},{10,14},{6,10},{2,6},{0,2},{5,1},{9,5},... | collective-permute-start | bytes 3145736 | tf_op jit(solution)/shard_map/ppermute | solution.py:518
  9.1 8.0 %pairs_partial.1 = (bf16[8,512,256]{2,1,0:T(8,128)(2,1)S(1)}, bf16[256,256]{1,0:T(8,128)(2,1)}, bf16[256,256]{1,0:T(8,128)(2,1)}) custom-call(s32[8]{0:T(128)S(1)} %compare_select_fusion.4.blocks, bf16[512,1024]{1,0:T(8,128)(2,1)S(1)} %copy-done, bf16[1,8192]{1,0:T(2,128)(2,1)S(1)} %broadcast_in_dim.45.refs_0_.gain_ref, bf16[1024,2048]{1,0:T(8,128)(2,1)} %w_ref.1), custom_call_target="tpu_custom_call" | custom-call | flops 2147483648 | bytes 9437184 | tf_op jit(solution)/shard_map/pairs_partial/pallas_call | solution.py:99
  17.0 2.0 collective-permute-start.3
  19.1 2.1 constant_dynamic-slice_fusion
  21.6 9.7 %collective-permute-done.3.a_ref = bf16[256,256]{1,0:T(8,128)(2,1)S(1)} collective-permute-done((bf16[256,256]{1,0:T(8,128)(2,1)}, bf16[256,256]{1,0:T(8,128)(2,1)S(1)}, u32[]{:S(2)}, u32[]{:S(2)}) %collective-permute-start.3) | collective-permute-done | bytes 131104 | tf_op jit(solution)/shard_map/ppermute | solution.py:518
  37.2 7.8 %query_part.5 = (f32[512,1024]{1,0:T(8,128)S(1)}, f32[512,1]{1,0:T(8,128)S(1)}) custom-call(s32[8]{0:T(128)S(1)} %compare_select_fusion.4.blocks, bf16[1,8192]{1,0:T(2,128)(2,1)S(1)} %broadcast_in_dim.45.refs_0_.gain_ref, bf16[8192,1024]{1,0:T(8,128)(2,1)} %refs_1_.12, bf16[512,1024]{1,0:T(8,128)(2,1)S(1)} %copy-done.1, ...), custom_call_target="tpu_custom_call" | custom-call | flops 3221225472 | bytes 12582912 | tf_op jit(solution)/shard_map/query_part/pallas_call | solution.py:335
  45.1 18.8 %collective-permute-done.7.a_ref = bf16[512,256]{1,0:T(8,128)(2,1)S(1)} collective-permute-done((bf16[512,256]{1,0:T(8,128)(2,1)S(1)}, bf16[512,256]{1,0:T(8,128)(2,1)S(1)}, u32[]{:S(2)}, u32[]{:S(2)}) %collective-permute-start.7) | collective-permute-done | bytes 262176 | tf_op jit(solution)/shard_map/ppermute | solution.py:518
  79.1 4.0 %scatter_fusion = bf16[96,16,256]{2,1,0:T(8,128)(2,1)} fusion(bf16[96,16,256]{2,1,0:T(8,128)(2,1)} %constant_dynamic-slice_fusion, s32[32]{0:T(128)S(1)} %fusion.4, bf16[32,16,256]{2,1,0:T(8,128)(2,1)S(1)} %gather_fusion), kind=kCustom, calls=%fused_computation.1 | custom fusion | bytes 786560 | tf_op jit(solution)/shard_map/scatter | solution.py:580
  84.1 6.9 %query_part.6 = (f32[512,1024]{1,0:T(8,128)S(1)}, f32[512,1]{1,0:T(8,128)S(1)}) custom-call(s32[8]{0:T(128)S(1)} %compare_select_fusion.4.blocks, bf16[1,8192]{1,0:T(2,128)(2,1)S(1)} %broadcast_in_dim.45.refs_0_.gain_ref, bf16[8192,1024]{1,0:T(8,128)(2,1)} %refs_1_.12, f32[512,1024]{1,0:T(8,128)} %copy-done.2, f32[512,1]{1,0:T(8,128)S(1)} %copy-done.11, ...), custom_call_target="tpu_custom_call" | custom-call | flops 2147483648 | bytes 8388608 | tf_op jit(solution)/shard_map/query_part/pallas_call | solution.py:335
  92.3 3.1 %collective-permute-done.11.a_ref = bf16[512,256]{1,0:T(8,128)(2,1)} collective-permute-done((bf16[512,256]{1,0:T(8,128)(2,1)}, bf16[512,256]{1,0:T(8,128)(2,1)}, u32[]{:S(2)}, u32[]{:S(2)}) %collective-permute-start.11) | collective-permute-done | bytes 262176 | tf_op jit(solution)/shard_map/ppermute | solution.py:518
  101.3 6.9 %query_part.7 = (f32[512,1024]{1,0:T(8,128)S(1)}, f32[512,1]{1,0:T(8,128)S(1)}) custom-call(s32[8]{0:T(128)S(1)} %compare_select_fusion.4.blocks, bf16[1,8192]{1,0:T(2,128)(2,1)S(1)} %broadcast_in_dim.45.refs_0_.gain_ref, bf16[8192,1024]{1,0:T(8,128)(2,1)} %refs_1_.12, f32[512,1024]{1,0:T(8,128)} %copy-done.3, f32[512,1]{1,0:T(8,128)S(1)} %get-tuple-element.81.refs_3_, ...), custom_call_target="tpu_custom_call" | custom-call | flops 2147483648 | bytes 8388608 | tf_op jit(solution)/shard_map/query_part/pallas_call | solution.py:335
  108.1 6.4 %collective-permute-done.15.a_ref = bf16[512,256]{1,0:T(8,128)(2,1)S(1)} collective-permute-done((bf16[512,256]{1,0:T(8,128)(2,1)S(1)}, bf16[512,256]{1,0:T(8,128)(2,1)S(1)}, u32[]{:S(2)}, u32[]{:S(2)}) %collective-permute-start.15) | collective-permute-done | bytes 262176 | tf_op jit(solution)/shard_map/ppermute | solution.py:518
  116.3 3.1 %query_part.8 = (bf16[256,1024]{1,0:T(8,128)(2,1)S(1)}, f32[256,1]{1,0:T(8,128)S(1)}) custom-call(s32[8]{0:T(128)S(1)} %compare_select_fusion.4.blocks, bf16[1,8192]{1,0:T(2,128)(2,1)S(1)} %broadcast_in_dim.45.refs_0_.gain_ref, bf16[8192,1024]{1,0:T(8,128)(2,1)} %refs_1_.12, f32[512,1024]{1,0:T(8,128)S(1)} %get-tuple-element.88.refs_2_, ...), custom_call_target="tpu_custom_call" | custom-call | flops 536870912 | bytes 4194304 | tf_op jit(solution)/shard_map/query_part/pallas_call | solution.py:335
  119.4 3.9 %prefill_context.1.refs_0_ = bf16[256,1024]{1,0:T(8,128)(2,1)S(1)} custom-call(bf16[256,1024]{1,0:T(8,128)(2,1)S(1)} %get-tuple-element.101.q_ref, bf16[512,256]{1,0:T(8,128)(2,1)S(1)} %bitcast.19, f32[256,768]{1,0:T(8,128)S(1)} %copy-done.17, f32[256,256]{1,0:T(8,128)S(1)} %get-tuple-element.104.pairs_ref, f32[256,1]{1,0:T(8,128)S(1)} %get-tuple-element.105.inv_ref, ...), custom_call_target="tpu_custom_call" | custom-call | flops 805306368 | bytes 2097152 | tf_op jit(solution)/shard_map/prefill_context/pallas_call | solution.py:427
  123.3 4.6 %output_part.6 = (bf16[256,1024]{1,0:T(8,128)(2,1)S(1)}, bf16[256,1024]{1,0:T(8,128)(2,1)S(1)}) custom-call(s32[8]{0:T(128)S(1)} %compare_select_fusion.4.blocks, bf16[256,1024]{1,0:T(8,128)(2,1)S(1)} %prefill_context.1.refs_0_, bf16[1024,8192]{1,0:T(8,128)(2,1)} %refs_2_.13, bf16[1024,8192]{1,0:T(8,128)(2,1)} %refs_2_.13), custom_call_target="tpu_custom_call" | custom-call | flops 1073741824 | bytes 4194304 | tf_op jit(solution)/shard_map/output_part/pallas_call | solution.py:495
  130.0 3.1 %query_part.9 = (bf16[256,1024]{1,0:T(8,128)(2,1)S(1)}, f32[256,1]{1,0:T(8,128)S(1)}) custom-call(s32[8]{0:T(128)S(1)} %compare_select_fusion.4.blocks, bf16[1,8192]{1,0:T(2,128)(2,1)S(1)} %broadcast_in_dim.45.refs_0_.gain_ref, bf16[8192,1024]{1,0:T(8,128)(2,1)} %refs_1_.12, f32[512,1024]{1,0:T(8,128)S(1)} %get-tuple-element.88.refs_2_, ...), custom_call_target="tpu_custom_call" | custom-call | flops 536870912 | bytes 4194304 | tf_op jit(solution)/shard_map/query_part/pallas_call | solution.py:335
  133.1 7.6 %decode_context.1.refs_1_.refs_0_ = bf16[256,1024]{1,0:T(8,128)(2,1)S(1)} custom-call(bf16[256,1024]{1,0:T(8,128)(2,1)S(1)} %get-tuple-element.109.q_ref, bf16[1536,256]{1,0:T(8,128)(2,1)} %bitcast.7.cache_ref, f32[256,1536]{1,0:T(8,128)S(1)} %copy-done.15, f32[256,256]{1,0:T(8,128)S(1)} %get-tuple-element.110.pairs_ref, ...), custom_call_target="tpu_custom_call" | custom-call | flops 1610612736 | bytes 2097152 | tf_op jit(solution)/shard_map/decode_context/pallas_call | solution.py:383
  140.8 4.6 %output_part.11 = (bf16[256,1024]{1,0:T(8,128)(2,1)S(1)}, bf16[256,1024]{1,0:T(8,128)(2,1)S(1)}) custom-call(s32[8]{0:T(128)S(1)} %compare_select_fusion.4.blocks, bf16[256,1024]{1,0:T(8,128)(2,1)S(1)} %decode_context.1.refs_1_.refs_0_, bf16[1024,8192]{1,0:T(8,128)(2,1)} %refs_2_.13, bf16[1024,8192]{1,0:T(8,128)(2,1)} %refs_2_.13), custom_call_target="tpu_custom_call" | custom-call | flops 1073741824 | bytes 4194304 | tf_op jit(solution)/shard_map/output_part/pallas_call | solution.py:495
  147.4 4.6 %output_part.7 = (bf16[256,1024]{1,0:T(8,128)(2,1)S(1)}, bf16[256,1024]{1,0:T(8,128)(2,1)S(1)}) custom-call(s32[8]{0:T(128)S(1)} %compare_select_fusion.4.blocks, bf16[256,1024]{1,0:T(8,128)(2,1)S(1)} %prefill_context.1.refs_0_, bf16[256,1024]{1,0:T(8,128)(2,1)S(1)} %decode_context.1.refs_1_.refs_0_, bf16[1024,8192]{1,0:T(8,128)(2,1)} %refs_2_.13, ...), custom_call_target="tpu_custom_call" | custom-call | flops 1073741824 | bytes 4194304 | tf_op jit(solution)/shard_map/output_part/pallas_call | solution.py:495
  152.0 5.5 %output_part.8 = (bf16[256,1024]{1,0:T(8,128)(2,1)S(1)}, bf16[256,1024]{1,0:T(8,128)(2,1)S(1)}, bf16[256,1024]{1,0:T(8,128)(2,1)S(1)}, bf16[256,1024]{1,0:T(8,128)(2,1)S(1)}) custom-call(s32[8]{0:T(128)S(1)} %compare_select_fusion.4.blocks, bf16[256,1024]{1,0:T(8,128)(2,1)S(1)} %prefill_context.1.refs_0_, ...), custom_call_target="tpu_custom_call" | custom-call | flops 2147483648 | bytes 4194304 | tf_op jit(solution)/shard_map/output_part/pallas_call | solution.py:495
  162.1 5.5 %output_part.9 = (bf16[256,1024]{1,0:T(8,128)(2,1)S(1)}, bf16[256,1024]{1,0:T(8,128)(2,1)S(1)}, bf16[256,1024]{1,0:T(8,128)(2,1)S(1)}, bf16[256,1024]{1,0:T(8,128)(2,1)S(1)}) custom-call(s32[8]{0:T(128)S(1)} %compare_select_fusion.4.blocks, bf16[256,1024]{1,0:T(8,128)(2,1)S(1)} %prefill_context.1.refs_0_, ...), custom_call_target="tpu_custom_call" | custom-call | flops 2147483648 | bytes 4194304 | tf_op jit(solution)/shard_map/output_part/pallas_call | solution.py:495
  167.6 5.0 %collective-permute-done.20.refs_0_ = bf16[256,1024]{1,0:T(8,128)(2,1)S(1)} collective-permute-done((bf16[256,1024]{1,0:T(8,128)(2,1)S(1)}, bf16[256,1024]{1,0:T(8,128)(2,1)S(1)}, u32[]{:S(2)}, u32[]{:S(2)}) %collective-permute-start.20) | collective-permute-done | bytes 524320 | tf_op jit(solution)/shard_map/ppermute | solution.py:518
  173.4 9.3 %collective-permute-done.27.refs_0_ = bf16[256,1024]{1,0:T(8,128)(2,1)S(1)} collective-permute-done((bf16[256,1024]{1,0:T(8,128)(2,1)S(1)}, bf16[256,1024]{1,0:T(8,128)(2,1)S(1)}, u32[]{:S(2)}, u32[]{:S(2)}) %collective-permute-start.27) | collective-permute-done | bytes 524320 | tf_op jit(solution)/shard_map/ppermute | solution.py:518
  184.3 7.8 %collective-permute-done.22.refs_0_ = bf16[256,1024]{1,0:T(8,128)(2,1)S(1)} collective-permute-done((bf16[256,1024]{1,0:T(8,128)(2,1)S(1)}, bf16[256,1024]{1,0:T(8,128)(2,1)S(1)}, u32[]{:S(2)}, u32[]{:S(2)}) %collective-permute-start.22) | collective-permute-done | bytes 524320 | tf_op jit(solution)/shard_map/ppermute | solution.py:518
  193.2 4.6 %collective-permute-done.30.refs_0_ = bf16[256,1024]{1,0:T(8,128)(2,1)S(1)} collective-permute-done((bf16[256,1024]{1,0:T(8,128)(2,1)S(1)}, bf16[256,1024]{1,0:T(8,128)(2,1)S(1)}, u32[]{:S(2)}, u32[]{:S(2)}) %collective-permute-start.30) | collective-permute-done | bytes 524320 | tf_op jit(solution)/shard_map/ppermute | solution.py:518
  198.7 4.1 %output_part.10 = (bf16[256,1024]{1,0:T(8,128)(2,1)S(1)}, bf16[256,1024]{1,0:T(8,128)(2,1)S(1)}) custom-call(s32[8]{0:T(128)S(1)} %compare_select_fusion.4.blocks, bf16[256,1024]{1,0:T(8,128)(2,1)S(1)} %prefill_context.1.refs_0_, bf16[256,1024]{1,0:T(8,128)(2,1)S(1)} %decode_context.1.refs_1_.refs_0_, bf16[1024,8192]{1,0:T(8,128)(2,1)} %refs_2_.13), custom_call_target="tpu_custom_call" | custom-call | flops 1073741824 | bytes 2097152 | tf_op jit(solution)/shard_map/output_part/pallas_call | solution.py:495
  202.8 2.8 %collective-permute-done.24.refs_1_ = bf16[256,1024]{1,0:T(8,128)(2,1)S(1)} collective-permute-done((bf16[256,1024]{1,0:T(8,128)(2,1)S(1)}, bf16[256,1024]{1,0:T(8,128)(2,1)S(1)}, u32[]{:S(2)}, u32[]{:S(2)}) %collective-permute-start.24) | collective-permute-done | bytes 524320 | tf_op jit(solution)/shard_map/ppermute | solution.py:518
  205.6 5.3 %collective-permute-done.29.refs_3_ = bf16[256,1024]{1,0:T(8,128)(2,1)S(1)} collective-permute-done((bf16[256,1024]{1,0:T(8,128)(2,1)S(1)}, bf16[256,1024]{1,0:T(8,128)(2,1)S(1)}, u32[]{:S(2)}, u32[]{:S(2)}) %collective-permute-start.29) | collective-permute-done | bytes 524320 | tf_op jit(solution)/shard_map/ppermute | solution.py:518
  211.2 2.3 %last_parts.1 = (f32[512,1024]{1,0:T(8,128)}, bf16[512,1024]{1,0:T(8,128)(2,1)}, f32[8,512]{1,0:T(8,128)S(1)}) custom-call(bf16[512,1024]{1,0:T(8,128)(2,1)S(1)} %copy-done.1, bf16[256,1024]{1,0:T(8,128)(2,1)S(1)} %collective-permute-done.23.refs_0_, bf16[256,1024]{1,0:T(8,128)(2,1)S(1)} %collective-permute-done.24.refs_1_, ...), custom_call_target="tpu_custom_call" | custom-call | flops 2097152 | bytes 6291456 | tf_op jit(solution)/shard_map/last_parts/pallas_call | solution.py:226
  213.5 1.8 collective-permute-start.32
  215.3 2.0 collective-permute-done.32
  219.3 2.3 %collective-permute-start.33 = (f32[8,512]{1,0:T(8,128)S(1)}, f32[8,512]{1,0:T(8,128)S(1)}, u32[]{:S(2)}, u32[]{:S(2)}) collective-permute-start(f32[8,512]{1,0:T(8,128)S(1)} %add.70), channel_id=1, source_target_pairs={{0,4},{2,6},{4,0},{6,2},{8,12},{10,14},{12,8},{14,10},{1,5},{3,7},... | collective-permute-start | bytes 49160 | tf_op jit(solution)/shard_map/ppermute | solution.py:523
  (149 shorter events, 56.8 us)
Async XLA Ops:
  0.6 32.3 %collective-permute-start = (bf16[512,1024]{1,0:T(8,128)(2,1)}, bf16[512,1024]{1,0:T(8,128)(2,1)}, u32[]{:S(2)}, u32[]{:S(2)}) collective-permute-start(bf16[512,1024]{1,0:T(8,128)(2,1)} %x_ref.2), channel_id=1, source_target_pairs={{4,0},{8,4},{12,8},{14,12},{10,14},{6,10},{2,6},{0,2},{5,1},{9,5},... | collective-permute-start | bytes 3145736 | tf_op jit(solution)/shard_map/ppermute | solution.py:518
  3.6 29.3 %collective-permute-start.1 = (bf16[512,1024]{1,0:T(8,128)(2,1)}, bf16[512,1024]{1,0:T(8,128)(2,1)}, u32[]{:S(2)}, u32[]{:S(2)}) collective-permute-start(bf16[512,1024]{1,0:T(8,128)(2,1)} %x_ref.2), channel_id=1, source_target_pairs={{0,4},{4,8},{8,12},{12,14},{14,10},{10,6},{6,2},{2,0},{1,5},{5,9},... | collective-permute-start | bytes 3145736 | tf_op jit(solution)/shard_map/ppermute | solution.py:518
  17.0 14.2 %collective-permute-start.3 = (bf16[256,256]{1,0:T(8,128)(2,1)}, bf16[256,256]{1,0:T(8,128)(2,1)S(1)}, u32[]{:S(2)}, u32[]{:S(2)}) collective-permute-start(bf16[256,256]{1,0:T(8,128)(2,1)} %get-tuple-element.73), channel_id=1, source_target_pairs={{0,4},{4,8},{8,12},{12,14},{14,10},{10,6},{6,2},{2,0},{1,5},{5,9},... | collective-permute-start | bytes 393224 | tf_op jit(solution)/shard_map/ppermute | solution.py:518
  19.0 12.3 %collective-permute-start.4 = (bf16[256,256]{1,0:T(8,128)(2,1)}, bf16[256,256]{1,0:T(8,128)(2,1)S(1)}, u32[]{:S(2)}, u32[]{:S(2)}) collective-permute-start(bf16[256,256]{1,0:T(8,128)(2,1)} %get-tuple-element.74), channel_id=1, source_target_pairs={{4,0},{8,4},{12,8},{14,12},{10,14},{6,10},{2,6},{0,2},{5,1},{9,5},... | collective-permute-start | bytes 393224 | tf_op jit(solution)/shard_map/ppermute | solution.py:518
  21.3 56.1 %collective-permute-start.13 = (bf16[96,16,256]{2,1,0:T(8,128)(2,1)}, bf16[96,16,256]{2,1,0:T(8,128)(2,1)}, u32[]{:S(2)}, u32[]{:S(2)}) collective-permute-start(bf16[96,16,256]{2,1,0:T(8,128)(2,1)} %constant_dynamic-slice_fusion), channel_id=1, source_target_pairs={{0,1},{1,0},{2,3},{3,2},{4,5},{5,4},{6,7},{7,6},{8,9},{9,8},{10,11... | collective-permute-start | bytes 2359304 | tf_op jit(solution)/shard_map/ppermute | solution.py:574
  33.0 32.5 %collective-permute-start.5 = (bf16[512,1024]{1,0:T(8,128)(2,1)}, bf16[512,1024]{1,0:T(8,128)(2,1)}, u32[]{:S(2)}, u32[]{:S(2)}) collective-permute-start(bf16[512,1024]{1,0:T(8,128)(2,1)} %collective-permute-done.refs_3_), channel_id=1, source_target_pairs={{4,0},{8,4},{12,8},{14,12},{10,14},{6,10},{2,6},{0,2},{5,1},{9,5},... | collective-permute-start | bytes 3145736 | tf_op jit(solution)/shard_map/ppermute | solution.py:518
  34.6 30.9 %collective-permute-start.6 = (bf16[512,1024]{1,0:T(8,128)(2,1)}, bf16[512,1024]{1,0:T(8,128)(2,1)}, u32[]{:S(2)}, u32[]{:S(2)}) collective-permute-start(bf16[512,1024]{1,0:T(8,128)(2,1)} %collective-permute-done.1.refs_4_), channel_id=1, source_target_pairs={{0,4},{4,8},{8,12},{12,14},{14,10},{10,6},{6,2},{2,0},{1,5},{5,9},... | collective-permute-start | bytes 3145736 | tf_op jit(solution)/shard_map/ppermute | solution.py:518
  35.2 28.7 %collective-permute-start.7 = (bf16[512,256]{1,0:T(8,128)(2,1)S(1)}, bf16[512,256]{1,0:T(8,128)(2,1)S(1)}, u32[]{:S(2)}, u32[]{:S(2)}) collective-permute-start(bf16[512,256]{1,0:T(8,128)(2,1)S(1)} %get-tuple-element.76), channel_id=1, source_target_pairs={{0,4},{4,8},{8,12},{12,14},{14,10},{10,6},{6,2},{2,0},{1,5},{5,9},... | collective-permute-start | bytes 786440 | tf_op jit(solution)/shard_map/ppermute | solution.py:518
  35.6 28.3 %collective-permute-start.8 = (bf16[512,256]{1,0:T(8,128)(2,1)S(1)}, bf16[512,256]{1,0:T(8,128)(2,1)S(1)}, u32[]{:S(2)}, u32[]{:S(2)}) collective-permute-start(bf16[512,256]{1,0:T(8,128)(2,1)S(1)} %get-tuple-element.77), channel_id=1, source_target_pairs={{4,0},{8,4},{12,8},{14,12},{10,14},{6,10},{2,6},{0,2},{5,1},{9,5},... | collective-permute-start | bytes 786440 | tf_op jit(solution)/shard_map/ppermute | solution.py:518
  65.5 32.1 %collective-permute-start.9 = (bf16[512,1024]{1,0:T(8,128)(2,1)}, bf16[512,1024]{1,0:T(8,128)(2,1)}, u32[]{:S(2)}, u32[]{:S(2)}) collective-permute-start(bf16[512,1024]{1,0:T(8,128)(2,1)} %collective-permute-done.5.refs_4_), channel_id=1, source_target_pairs={{4,0},{8,4},{12,8},{14,12},{10,14},{6,10},{2,6},{0,2},{5,1},{9,5},... | collective-permute-start | bytes 3145736 | tf_op jit(solution)/shard_map/ppermute | solution.py:518
  67.1 29.5 %collective-permute-start.10 = (bf16[512,1024]{1,0:T(8,128)(2,1)}, bf16[512,1024]{1,0:T(8,128)(2,1)}, u32[]{:S(2)}, u32[]{:S(2)}) collective-permute-start(bf16[512,1024]{1,0:T(8,128)(2,1)} %collective-permute-done.6.refs_5_), channel_id=1, source_target_pairs={{0,4},{4,8},{8,12},{12,14},{14,10},{10,6},{6,2},{2,0},{1,5},{5,9},... | collective-permute-start | bytes 3145736 | tf_op jit(solution)/shard_map/ppermute | solution.py:518
  68.7 26.6 %collective-permute-start.11 = (bf16[512,256]{1,0:T(8,128)(2,1)}, bf16[512,256]{1,0:T(8,128)(2,1)}, u32[]{:S(2)}, u32[]{:S(2)}) collective-permute-start(bf16[512,256]{1,0:T(8,128)(2,1)} %copy-done.19), channel_id=1, source_target_pairs={{0,4},{4,8},{8,12},{12,14},{14,10},{10,6},{6,2},{2,0},{1,5},{5,9},... | collective-permute-start | bytes 786440 | tf_op jit(solution)/shard_map/ppermute | solution.py:518
  69.2 26.1 %collective-permute-start.12 = (bf16[512,256]{1,0:T(8,128)(2,1)}, bf16[512,256]{1,0:T(8,128)(2,1)}, u32[]{:S(2)}, u32[]{:S(2)}) collective-permute-start(bf16[512,256]{1,0:T(8,128)(2,1)} %copy-done.18), channel_id=1, source_target_pairs={{4,0},{8,4},{12,8},{14,12},{10,14},{6,10},{2,6},{0,2},{5,1},{9,5},... | collective-permute-start | bytes 786440 | tf_op jit(solution)/shard_map/ppermute | solution.py:518
  98.7 17.5 %collective-permute-start.14 = (bf16[256,1024]{1,0:T(8,128)(2,1)S(1)}, bf16[256,1024]{1,0:T(8,128)(2,1)S(1)}, u32[]{:S(2)}, u32[]{:S(2)}) collective-permute-start(bf16[256,1024]{1,0:T(8,128)(2,1)S(1)} %slice.34), channel_id=1, source_target_pairs={{0,4},{4,8},{8,12},{12,14},{14,10},{10,6},{6,2},{2,0},{1,5},{5,9},... | collective-permute-start | bytes 1572872 | tf_op jit(solution)/shard_map/ppermute | solution.py:518
  99.2 15.3 %collective-permute-start.15 = (bf16[512,256]{1,0:T(8,128)(2,1)S(1)}, bf16[512,256]{1,0:T(8,128)(2,1)S(1)}, u32[]{:S(2)}, u32[]{:S(2)}) collective-permute-start(bf16[512,256]{1,0:T(8,128)(2,1)S(1)} %get-tuple-element.98), channel_id=1, source_target_pairs={{0,4},{4,8},{8,12},{12,14},{14,10},{10,6},{6,2},{2,0},{1,5},{5,9},... | collective-permute-start | bytes 786440 | tf_op jit(solution)/shard_map/ppermute | solution.py:518
  99.7 14.9 %collective-permute-start.16 = (bf16[512,256]{1,0:T(8,128)(2,1)S(1)}, bf16[512,256]{1,0:T(8,128)(2,1)S(1)}, u32[]{:S(2)}, u32[]{:S(2)}) collective-permute-start(bf16[512,256]{1,0:T(8,128)(2,1)S(1)} %get-tuple-element.99), channel_id=1, source_target_pairs={{4,0},{8,4},{12,8},{14,12},{10,14},{6,10},{2,6},{0,2},{5,1},{9,5},... | collective-permute-start | bytes 786440 | tf_op jit(solution)/shard_map/ppermute | solution.py:518
  114.6 15.4 %collective-permute-start.19 = (bf16[256,1024]{1,0:T(8,128)(2,1)S(1)}, bf16[256,1024]{1,0:T(8,128)(2,1)S(1)}, u32[]{:S(2)}, u32[]{:S(2)}) collective-permute-start(bf16[256,1024]{1,0:T(8,128)(2,1)S(1)} %slice.35), channel_id=1, source_target_pairs={{4,0},{8,4},{12,8},{14,12},{10,14},{6,10},{2,6},{0,2},{5,1},{9,5},... | collective-permute-start | bytes 1572872 | tf_op jit(solution)/shard_map/ppermute | solution.py:518
  127.9 12.9 %collective-permute-start.17 = (bf16[256,1024]{1,0:T(8,128)(2,1)S(1)}, bf16[256,1024]{1,0:T(8,128)(2,1)S(1)}, u32[]{:S(2)}, u32[]{:S(2)}) collective-permute-start(bf16[256,1024]{1,0:T(8,128)(2,1)S(1)} %get-tuple-element.106), channel_id=1, source_target_pairs={{0,4},{4,8},{8,12},{12,14},{14,10},{10,6},{6,2},{2,0},{1,5},{5,9},... | collective-permute-start | bytes 1572872 | tf_op jit(solution)/shard_map/ppermute | solution.py:518
  128.4 12.4 %collective-permute-start.18 = (bf16[256,1024]{1,0:T(8,128)(2,1)S(1)}, bf16[256,1024]{1,0:T(8,128)(2,1)S(1)}, u32[]{:S(2)}, u32[]{:S(2)}) collective-permute-start(bf16[256,1024]{1,0:T(8,128)(2,1)S(1)} %get-tuple-element.107), channel_id=1, source_target_pairs={{4,0},{8,4},{12,8},{14,12},{10,14},{6,10},{2,6},{0,2},{5,1},{9,5},... | collective-permute-start | bytes 1572872 | tf_op jit(solution)/shard_map/ppermute | solution.py:518
  145.4 14.4 %collective-permute-start.25 = (bf16[256,1024]{1,0:T(8,128)(2,1)S(1)}, bf16[256,1024]{1,0:T(8,128)(2,1)S(1)}, u32[]{:S(2)}, u32[]{:S(2)}) collective-permute-start(bf16[256,1024]{1,0:T(8,128)(2,1)S(1)} %get-tuple-element.123), channel_id=1, source_target_pairs={{0,4},{4,8},{8,12},{12,14},{14,10},{10,6},{6,2},{2,0},{1,5},{5,9},... | collective-permute-start | bytes 1572872 | tf_op jit(solution)/shard_map/ppermute | solution.py:518
  145.9 13.9 %collective-permute-start.26 = (bf16[256,1024]{1,0:T(8,128)(2,1)S(1)}, bf16[256,1024]{1,0:T(8,128)(2,1)S(1)}, u32[]{:S(2)}, u32[]{:S(2)}) collective-permute-start(bf16[256,1024]{1,0:T(8,128)(2,1)S(1)} %get-tuple-element.124), channel_id=1, source_target_pairs={{4,0},{8,4},{12,8},{14,12},{10,14},{6,10},{2,6},{0,2},{5,1},{9,5},... | collective-permute-start | bytes 1572872 | tf_op jit(solution)/shard_map/ppermute | solution.py:518
  157.7 14.9 %collective-permute-start.20 = (bf16[256,1024]{1,0:T(8,128)(2,1)S(1)}, bf16[256,1024]{1,0:T(8,128)(2,1)S(1)}, u32[]{:S(2)}, u32[]{:S(2)}) collective-permute-start(bf16[256,1024]{1,0:T(8,128)(2,1)S(1)} %get-tuple-element.114), channel_id=1, source_target_pairs={{0,4},{4,8},{8,12},{12,14},{14,10},{10,6},{6,2},{2,0},{1,5},{5,9},... | collective-permute-start | bytes 1572872 | tf_op jit(solution)/shard_map/ppermute | solution.py:518
  158.2 14.4 %collective-permute-start.21 = (bf16[256,1024]{1,0:T(8,128)(2,1)S(1)}, bf16[256,1024]{1,0:T(8,128)(2,1)S(1)}, u32[]{:S(2)}, u32[]{:S(2)}) collective-permute-start(bf16[256,1024]{1,0:T(8,128)(2,1)S(1)} %get-tuple-element.115), channel_id=1, source_target_pairs={{4,0},{8,4},{12,8},{14,12},{10,14},{6,10},{2,6},{0,2},{5,1},{9,5},... | collective-permute-start | bytes 1572872 | tf_op jit(solution)/shard_map/ppermute | solution.py:518
  160.0 22.6 %collective-permute-start.27 = (bf16[256,1024]{1,0:T(8,128)(2,1)S(1)}, bf16[256,1024]{1,0:T(8,128)(2,1)S(1)}, u32[]{:S(2)}, u32[]{:S(2)}) collective-permute-start(bf16[256,1024]{1,0:T(8,128)(2,1)S(1)} %get-tuple-element.127), channel_id=1, source_target_pairs={{0,4},{4,8},{8,12},{12,14},{14,10},{10,6},{6,2},{2,0},{1,5},{5,9},... | collective-permute-start | bytes 1572872 | tf_op jit(solution)/shard_map/ppermute | solution.py:518
  160.5 22.1 %collective-permute-start.28 = (bf16[256,1024]{1,0:T(8,128)(2,1)S(1)}, bf16[256,1024]{1,0:T(8,128)(2,1)S(1)}, u32[]{:S(2)}, u32[]{:S(2)}) collective-permute-start(bf16[256,1024]{1,0:T(8,128)(2,1)S(1)} %get-tuple-element.128), channel_id=1, source_target_pairs={{4,0},{8,4},{12,8},{14,12},{10,14},{6,10},{2,6},{0,2},{5,1},{9,5},... | collective-permute-start | bytes 1572872 | tf_op jit(solution)/shard_map/ppermute | solution.py:518
  172.9 19.3 %collective-permute-start.22 = (bf16[256,1024]{1,0:T(8,128)(2,1)S(1)}, bf16[256,1024]{1,0:T(8,128)(2,1)S(1)}, u32[]{:S(2)}, u32[]{:S(2)}) collective-permute-start(bf16[256,1024]{1,0:T(8,128)(2,1)S(1)} %get-tuple-element.118), channel_id=1, source_target_pairs={{0,4},{4,8},{8,12},{12,14},{14,10},{10,6},{6,2},{2,0},{1,5},{5,9},... | collective-permute-start | bytes 1572872 | tf_op jit(solution)/shard_map/ppermute | solution.py:518
  182.9 14.9 %collective-permute-start.30 = (bf16[256,1024]{1,0:T(8,128)(2,1)S(1)}, bf16[256,1024]{1,0:T(8,128)(2,1)S(1)}, u32[]{:S(2)}, u32[]{:S(2)}) collective-permute-start(bf16[256,1024]{1,0:T(8,128)(2,1)S(1)} %get-tuple-element.132), channel_id=1, source_target_pairs={{4,0},{8,4},{12,8},{14,12},{10,14},{6,10},{2,6},{0,2},{5,1},{9,5},... | collective-permute-start | bytes 1572872 | tf_op jit(solution)/shard_map/ppermute | solution.py:518
  183.7 21.9 %collective-permute-start.24 = (bf16[256,1024]{1,0:T(8,128)(2,1)S(1)}, bf16[256,1024]{1,0:T(8,128)(2,1)S(1)}, u32[]{:S(2)}, u32[]{:S(2)}) collective-permute-start(bf16[256,1024]{1,0:T(8,128)(2,1)S(1)} %get-tuple-element.120), channel_id=1, source_target_pairs={{4,0},{8,4},{12,8},{14,12},{10,14},{6,10},{2,6},{0,2},{5,1},{9,5},... | collective-permute-start | bytes 1572872 | tf_op jit(solution)/shard_map/ppermute | solution.py:518
  192.3 13.3 %collective-permute-start.23 = (bf16[256,1024]{1,0:T(8,128)(2,1)S(1)}, bf16[256,1024]{1,0:T(8,128)(2,1)S(1)}, u32[]{:S(2)}, u32[]{:S(2)}) collective-permute-start(bf16[256,1024]{1,0:T(8,128)(2,1)S(1)} %add_parts.8), channel_id=1, source_target_pairs={{0,4},{4,8},{8,12},{12,14},{14,10},{10,6},{6,2},{2,0},{1,5},{5,9},... | collective-permute-start | bytes 1572872 | tf_op jit(solution)/shard_map/ppermute | solution.py:649
  192.8 18.2 %collective-permute-start.29 = (bf16[256,1024]{1,0:T(8,128)(2,1)S(1)}, bf16[256,1024]{1,0:T(8,128)(2,1)S(1)}, u32[]{:S(2)}, u32[]{:S(2)}) collective-permute-start(bf16[256,1024]{1,0:T(8,128)(2,1)S(1)} %get-tuple-element.131), channel_id=1, source_target_pairs={{0,4},{4,8},{8,12},{12,14},{14,10},{10,6},{6,2},{2,0},{1,5},{5,9},... | collective-permute-start | bytes 1572872 | tf_op jit(solution)/shard_map/ppermute | solution.py:518
  198.0 13.2 %collective-permute-start.31 = (bf16[256,1024]{1,0:T(8,128)(2,1)S(1)}, bf16[256,1024]{1,0:T(8,128)(2,1)S(1)}, u32[]{:S(2)}, u32[]{:S(2)}) collective-permute-start(bf16[256,1024]{1,0:T(8,128)(2,1)S(1)} %add_parts.11), channel_id=1, source_target_pairs={{4,0},{8,4},{12,8},{14,12},{10,14},{6,10},{2,6},{0,2},{5,1},{9,5},... | collective-permute-start | bytes 1572872 | tf_op jit(solution)/shard_map/ppermute | solution.py:650
  217.3 5.5 %collective-permute-start.35 = (f32[8,512]{1,0:T(8,128)S(1)}, f32[8,512]{1,0:T(8,128)S(1)}, u32[]{:S(2)}, u32[]{:S(2)}) collective-permute-start(f32[8,512]{1,0:T(8,128)S(1)} %add.70), channel_id=1, source_target_pairs={{0,12},{2,14},{4,8},{6,10},{8,4},{10,6},{12,0},{14,2},{1,13},{3,15... | collective-permute-start | bytes 49160 | tf_op jit(solution)/shard_map/ppermute | solution.py:523
  (27 other events, 124.7 us)

commit v4 on v3

--- a/solution.py
+++ b/solution.py
@@ -246,11 +246,16 @@
 
 def norm_out(mixed, squares, gain, width):
     rows, columns = mixed.shape
+    block = pl.BlockSpec((128, columns), lambda i: (i, 0))
     return pl.pallas_call(
         functools.partial(norm_kernel, width),
-        grid=(1,),
-        in_specs=[pl.BlockSpec(a.shape, lambda i: (0, 0)) for a in (mixed, squares, gain)],
-        out_specs=pl.BlockSpec((rows, columns), lambda i: (0, 0)),
+        grid=(rows // 128,),
+        in_specs=[
+            block,
+            pl.BlockSpec((8, 128), lambda i: (0, i)),
+            pl.BlockSpec((1, columns), lambda i: (0, 0)),
+        ],
+        out_specs=block,
         out_shape=shaped((rows, columns), jnp.bfloat16),
         compiler_params=VMEM,
         cost_estimate=cost(3 * mixed.size, 6 * mixed.size),
@@ -354,91 +359,96 @@
     return keys.astype(jnp.bfloat16), pairs[:, HEAD_SIZE:]
 
 
-def decode_kernel(
-    q_ref, cache_ref, bias_ref, pairs_ref, inv_ref, cos_ref, sin_ref, out_ref, new_key, new_value
-):
-    @pl.when(pl.program_id(0) == 0)
-    def _():
-        keys, values = new_pairs(pairs_ref, inv_ref, cos_ref, sin_ref)
-        new_key[...] = keys.astype(jnp.float32)
-        new_value[...] = values.astype(jnp.float32)
-
-    for head in range(q_ref.shape[1] // HEAD_SIZE):
-        at = slice(head * HEAD_SIZE, (head + 1) * HEAD_SIZE)
+def weight_copies(places, blocks, weight, held, sems):
+    columns = held.shape[2]
+    return [
+        pltpu.make_async_copy(
+            weight.at[:, pl.ds(pl.multiple_of(blocks[place] * columns, columns), columns)],
+            held.at[i],
+            sems.at[i],
+        )
+        for i, place in enumerate(places)
+    ]
+
+
+def head_columns(ref):
+    return [slice(low, low + HEAD_SIZE) for low in range(0, ref.shape[1], HEAD_SIZE)]
+
+
+def decode_heads(refs, out_ref):
+    q_ref, cache_ref, bias_ref, *rest = refs
+    keys, values = new_pairs(*rest)
+    keys, values = keys.astype(jnp.float32), values.astype(jnp.float32)
+    for at in head_columns(out_ref):
         q = q_ref[:, at]
         score = dot_t(q, cache_ref[:, :HEAD_SIZE]) * FACTOR2 + bias_ref[...]
-        own = jnp.sum(q.astype(jnp.float32) * new_key[...], axis=1, keepdims=True) * FACTOR2
+        own = jnp.sum(q.astype(jnp.float32) * keys, axis=1, keepdims=True) * FACTOR2
         peak = jnp.maximum(jnp.max(score, axis=1, keepdims=True), own)
         grown, grown_own = jnp.exp2(score - peak), jnp.exp2(own - peak)
         scale = 1.0 / (jnp.sum(grown, axis=1, keepdims=True) + grown_own)
         context = dot(grown.astype(jnp.bfloat16), cache_ref[:, HEAD_SIZE:])
-        out_ref[:, at] = ((context + grown_own * new_value[...]) * scale).astype(jnp.bfloat16)
-
-
-def decode_context(q, cache, bias, pairs, inv, cosine, sine):
-    rows, width = q.shape
-    heads = min(4 * HEAD_SIZE, width)
-    tokens = cache.shape[0]
-    whole = lambda array: pl.BlockSpec(array.shape, lambda h: (0, 0))
-    return pl.pallas_call(
-        decode_kernel,
-        grid=(width // heads,),
-        in_specs=[pl.BlockSpec((rows, heads), lambda h: (0, h))]
-        + [whole(a) for a in (cache, bias, pairs, inv, cosine, sine)],
-        out_specs=pl.BlockSpec((rows, heads), lambda h: (0, h)),
-        scratch_shapes=[
-            pltpu.VMEM((rows, HEAD_SIZE), jnp.float32),
-            pltpu.VMEM((rows, HEAD_SIZE), jnp.float32),
-        ],
-        out_shape=shaped((rows, width), jnp.bfloat16),
-        compiler_params=VMEM,
-        cost_estimate=cost(4 * rows * width * tokens, 8 * rows * width, 2 * width * tokens),
-        name="decode_context",
-    )(q, cache, bias, pairs, inv, cosine, sine)
-
-
-def prefill_kernel(
-    q_ref, prefix_ref, bias_ref, pairs_ref, inv_ref, cos_ref, sin_ref, out_ref, keys, values
-):
-    old = prefix_ref.shape[0]
-
-    @pl.when(pl.program_id(0) == 0)
-    def _():
-        new_keys, new_values = new_pairs(pairs_ref, inv_ref, cos_ref, sin_ref)
-        keys[:old] = prefix_ref[:, :HEAD_SIZE]
-        keys[old:] = new_keys
-        values[:old] = prefix_ref[:, HEAD_SIZE:]
-        values[old:] = new_values
-
-    for head in range(q_ref.shape[1] // HEAD_SIZE):
-        at = slice(head * HEAD_SIZE, (head + 1) * HEAD_SIZE)
-        score = dot_t(q_ref[:, at], keys[...]) * FACTOR2 + bias_ref[...]
+        out_ref[:, at] = ((context + grown_own * values) * scale).astype(jnp.bfloat16)
+
+
+def prefill_heads(refs, out_ref):
+    q_ref, prefix_ref, bias_ref, *rest = refs
+    new_keys, new_values = new_pairs(*rest)
+    keys = jnp.concatenate([prefix_ref[:, :HEAD_SIZE], new_keys], axis=0)
+    values = jnp.concatenate([prefix_ref[:, HEAD_SIZE:], new_values], axis=0)
+    for at in head_columns(out_ref):
+        score = dot_t(q_ref[:, at], keys) * FACTOR2 + bias_ref[...]
         grown = jnp.exp2(score - jnp.max(score, axis=1, keepdims=True))
         scale = 1.0 / jnp.sum(grown, axis=1, keepdims=True)
-        context = dot(grown.astype(jnp.bfloat16), values[...]) * scale
+        context = dot(grown.astype(jnp.bfloat16), values) * scale
         out_ref[:, at] = context.astype(jnp.bfloat16)
 
 
-def prefill_context(q, prefix, bias, pairs, inv, cosine, sine):
+def context_kernel(heads, places, blocks, *refs):
+    if not places:
+        heads(refs[:-1], refs[-1])
+        return
+    *refs, weight, out_ref, first, second, held, sems = refs
+    copies = weight_copies(places, blocks, weight, held, sems)
+    for copy in copies:
+        copy.start()
+    heads(refs, out_ref)
+    tile = first.shape[1] // 4
+    for i, (copy, product) in enumerate(zip(copies, (first, second))):
+        copy.wait()
+        for low in range(0, product.shape[1], tile):
+            at = slice(low, low + tile)
+            product[:, at] = dot(out_ref[...], held[i, :, at]).astype(jnp.bfloat16)
+
+
+def contexts(heads, q, pages, bias, pairs, inv, angles, blocks, weight=None, places=()):
     rows, width = q.shape
-    heads = min(4 * HEAD_SIZE, width)
-    tokens = prefix.shape[0] + rows
-    whole = lambda array: pl.BlockSpec(array.shape, lambda h: (0, 0))
-    return pl.pallas_call(
-        prefill_kernel,
-        grid=(width // heads,),
-        in_specs=[pl.BlockSpec((rows, heads), lambda h: (0, h))]
-        + [whole(a) for a in (prefix, bias, pairs, inv, cosine, sine)],
-        out_specs=pl.BlockSpec((rows, heads), lambda h: (0, h)),
-        scratch_shapes=[
-            pltpu.VMEM((tokens, HEAD_SIZE), jnp.bfloat16),
-            pltpu.VMEM((tokens, HEAD_SIZE), jnp.bfloat16),
-        ],
-        out_shape=shaped((rows, width), jnp.bfloat16),
-        compiler_params=VMEM,
-        cost_estimate=cost(4 * rows * width * tokens, 8 * rows * width, 2 * width * tokens),
-        name="prefill_context",
-    )(q, prefix, bias, pairs, inv, cosine, sine)
+    operands = [q, pages, bias, pairs, inv, *angles]
+    in_specs = [pl.BlockSpec(a.shape, lambda i, b: (0, 0)) for a in operands]
+    out_shape = [shaped((rows, width), jnp.bfloat16)]
+    scratch = []
+    if places:
+        operands.append(weight)
+        in_specs.append(pl.BlockSpec(memory_space=pl.ANY))
+        columns = weight.shape[1] // RING
+        out_shape += [shaped((rows, columns), jnp.bfloat16)] * 2
+        scratch = [
+            pltpu.VMEM((2, width, columns), jnp.bfloat16),
+            pltpu.SemaphoreType.DMA((2,)),
+        ]
+    return pl.pallas_call(
+        functools.partial(context_kernel, heads, places),
+        grid_spec=pltpu.PrefetchScalarGridSpec(
+            num_scalar_prefetch=1,
+            grid=(1,),
+            in_specs=in_specs,
+            out_specs=[pl.BlockSpec(a.shape, lambda i, b: (0, 0)) for a in out_shape],
+            scratch_shapes=scratch,
+        ),
+        out_shape=out_shape,
+        compiler_params=VMEM,
+        cost_estimate=cost(8 * rows * width * bias.shape[1], 16 * rows * width),
+        name="contexts",
+    )(blocks, *operands)
 
 
 def masks_kernel(
@@ -588,11 +598,9 @@
     bias = masks(request, owner, page_table, positions, cache.shape[0], page_size)
     gain_row = entry_gain[None, :]
 
-    def attend_prefill(q, pairs, inv):
-        return prefill_context(q, prefix_rows, bias[0], pairs, inv, *angles[0])
-
-    def attend_decode(q, pairs, inv):
-        return decode_context(q, cache, bias[1], pairs, inv, *angles[1])
+    def attend(which, q, pairs, inv, blocks, *product):
+        heads, pages = ((prefill_heads, prefix_rows), (decode_heads, cache))[which]
+        return contexts(heads, q, pages, bias[which], pairs, inv, angles[which], blocks, *product)
 
     exit_row = lax.dynamic_slice_in_dim(exit_gain, me * width, width, 0)
     exit_row = exit_row.astype(jnp.float32)[None, :]
@@ -612,30 +620,32 @@
                 (FAR,), pieces, gain_row, query_weight, blocks, sums, angles[which], which
             )
 
-        def pairs_hop(moving, *others):
-            return lax.optimization_barrier((*hop(*moving), *others))[:2]
-
-        moving = add_pairs(*hop(*moving), parts, 3, 5)
+        def settled(arrived, *others):
+            return lax.optimization_barrier((*arrived, *others))[:2]
+
+        arrived = hop(*moving)
+        gather_hop()
+        moving = add_pairs(*settled(arrived, ahead[1], back[1]), parts, 3, 5)
+        sums = query((0, 1, 7))
+        arrived = hop(*moving)
+        gather_hop(*moving, sums[1])
+        sums = query((2, 6), sums)
+        moving = add_pairs(
+            *settled(arrived, sums[1], cache, *bias, *angles[0], *angles[1]), parts, 2, 6
+        )
+        arrived = hop(*moving)
         gather_hop(*moving)
-        sums = query((0, 1, 7))
-        moving = add_pairs(*pairs_hop(moving, sums[1]), parts, 2, 6)
-        gather_hop(*moving)
-        sums = query((2, 6), sums)
-        moving = pairs_hop(moving, sums[1], cache, *bias, *angles[0], *angles[1])
-        moving = add_pairs(*moving, parts, 1, 7)
-        gather_hop(*moving)
+        moving = add_pairs(*settled(arrived, ahead[3], back[3]), parts, 1, 7)
         sums = query((3, 5), sums)
-        pairs = end_pairs(*pairs_hop(moving, sums[1]), parts)
+        pairs = end_pairs(*settled(hop(*moving), sums[1]), parts)
 
         q, inv = query_end([ahead[FAR]], 0, sums)
-        prefilled = attend_prefill(q, pairs[0], inv)
-        p4, p5 = output_part([prefilled], output_weight, (4, 5), blocks)
+        prefilled, p4, p5 = attend(0, q, pairs[0], inv, blocks, output_weight, (4, 5))
         p_ahead, p_back = hop(p4, p5)
         q, inv = query_end([back[FAR]], 1, sums)
-        decoded = attend_decode(q, pairs[1], inv)
-        d4, d3 = output_part(
-            [lax.optimization_barrier((decoded, p_ahead, p_back))[0]], output_weight, (4, 3), blocks
-        )
+        q = after(q, p4)
+        decoded, d4, d3 = attend(1, q, pairs[1], inv, blocks, output_weight, (4, 3))
+        decoded, p_ahead, p_back = lax.optimization_barrier((decoded, p_ahead, p_back))
         d_ahead, d_back = hop(d3, d4)
         both = [prefilled, decoded]
         p3, d5 = output_part(both, output_weight, (3, 5), blocks, [(0, 0), (1, 1)])
@@ -662,9 +672,10 @@
     q = (q * cosine[:, None] + swapped * sine[:, None]).astype(jnp.bfloat16)
     q = q.reshape(-1, per_device * HEAD_SIZE)
     one = jnp.ones_like(inv)
+    none = jnp.zeros((1,), jnp.int32)
     context = [
-        attend_prefill(q[:prefill], pairs[:prefill], one[:prefill]),
-        attend_decode(q[prefill:], pairs[prefill:], one[prefill:]),
+        attend(0, q[:prefill], pairs[:prefill], one[:prefill], none)[0],
+        attend(1, q[prefill:], pairs[prefill:], one[prefill:], none)[0],
     ]
     context = jnp.concatenate(context, axis=0)
     summed = lax.psum_scatter(

time: 228 us -> 217 us (0.952)
  waiting for transfers between devices: 76.3 us -> 69.8 us
  Pallas kernels: 83.8 us -> 79.6 us
  starting transfers between devices: 35.7 us -> 39.5 us
  local copies, waits for them, and re-layouts: 26.1 us -> 23.2 us
    ppermute x14, waiting for transfers between devices: 65.6 us -> 36.7 us  [hop(): lax.ppermute(ahead, 'tensor', FORWARD)]
    ppermute x14, waiting for transfers between devices: 7.43 us -> 22.2 us  [hop(): lax.ppermute(back, 'tensor', BACKWARD)]
    pallas_call x6 -> x4, Pallas kernels: 28.7 us -> 19.6 us  [output_part(): pl.pallas_call(functools.partial(output_kernel, count, tuple(jobs)), grid...]
    ppermute x1, waiting for transfers between devices: 0.01 us -> 5.06 us  [body(): p_ahead = lax.ppermute(add_parts((p_ahead,), (p1,))[0], 'tensor', FORWARD)]
    pallas_call x3, Pallas kernels: 12.8 us -> 17.8 us  [the longest x2 15.8 us: contexts(): pl.pallas_call(functools.partial(context_kernel, heads, places), grid_spe...]
    ppermute x14, starting transfers between devices: 7.79 us -> 10.8 us  [hop(): lax.ppermute(ahead, 'tensor', FORWARD)]
    scatter x1, local copies, waits for them, and re-layouts: 3.98 us -> 1.51 us  [body(): cache = own_pool.at[target].set(arrived, mode='drop').reshape(-1, pair)]
    unnamed x49 -> x43, local copies, waits for them, and re-layouts: 13.3 us -> 13.8 us
  transfers between devices with their start and end apart: 36 -> 36, of which waited for: 15 -> 20; matrix products, arithmetic and copies ran while one was open for 8% -> 7% of each run, Pallas kernels for 33% -> 35%
where the time goes in v4:
time: 217 us; the launch traced here: 216 us
  Pallas kernels  79.6 us (37%)
  waiting for transfers between devices  69.8 us (32%)
  starting transfers between devices  39.5 us (18%)
  local copies, waits for them, and re-layouts  23.2 us (11%)
  other arithmetic  3.13 us (1%)
    ppermute x14, waiting for transfers between devices, hop(): lax.ppermute(ahead, 'tensor', FORWARD)  36.7 us
    pallas_call x5, Pallas kernels, query_part(): pl.pallas_call(functools.partial(query_kernel, count, first, last, weight...  27.8 us
    ppermute x14, waiting for transfers between devices, hop(): lax.ppermute(back, 'tensor', BACKWARD)  22.2 us
    ppermute x14, starting transfers between devices, hop(): lax.ppermute(back, 'tensor', BACKWARD)  20.2 us
    pallas_call x4, Pallas kernels, output_part(): pl.pallas_call(functools.partial(output_kernel, count, tuple(jobs)), grid...  19.6 us
    pallas_call x2, Pallas kernels, contexts(): pl.pallas_call(functools.partial(context_kernel, heads, places), grid_spe...  15.8 us
    unnamed x43, local copies, waits for them, and re-layouts  13.8 us
    ppermute x14, starting transfers between devices, hop(): lax.ppermute(ahead, 'tensor', FORWARD)  10.8 us
  transfers between devices with their start and end apart: 36, of which 20 were waited for; matrix products, arithmetic and copies ran while one was open for 7% of the time, Pallas kernels for 35%

profile of v4, /device:TPU:0, one launch (start us, length us, event | category | flops | bytes accessed | tf_op | source)
XLA Modules:
  0.0 216.4 jit_solution(12014007396420335981)
XLA Ops:
  0.6 3.0 %collective-permute-start = (bf16[512,1024]{1,0:T(8,128)(2,1)}, bf16[512,1024]{1,0:T(8,128)(2,1)}, u32[]{:S(2)}, u32[]{:S(2)}) collective-permute-start(bf16[512,1024]{1,0:T(8,128)(2,1)} %x_ref.2), channel_id=1, source_target_pairs={{4,0},{8,4},{12,8},{14,12},{10,14},{6,10},{2,6},{0,2},{5,1},{9,5},... | collective-permute-start | bytes 3145736 | tf_op jit(solution)/shard_map/ppermute | solution.py:528
  9.1 7.9 %pairs_partial.1 = (bf16[8,512,256]{2,1,0:T(8,128)(2,1)S(1)}, bf16[256,256]{1,0:T(8,128)(2,1)}, bf16[256,256]{1,0:T(8,128)(2,1)S(1)}) custom-call(s32[8]{0:T(128)S(1)} %compare_select_fusion.4.blocks, bf16[512,1024]{1,0:T(8,128)(2,1)S(1)} %copy-done, bf16[1,8192]{1,0:T(2,128)(2,1)S(1)} %broadcast_in_dim.45.refs_0_.gain_ref, bf16[1024,2048]{1,0:T(8,128)(2,1)} %w_ref.1), custom_call_target="tpu_custom_call" | custom-call | flops 2147483648 | bytes 9437184 | tf_op jit(solution)/shard_map/pairs_partial/pallas_call | solution.py:99
  17.0 2.0 collective-permute-start.5
  20.7 7.3 %collective-permute-done.refs_3_ = bf16[512,1024]{1,0:T(8,128)(2,1)} collective-permute-done((bf16[512,1024]{1,0:T(8,128)(2,1)}, bf16[512,1024]{1,0:T(8,128)(2,1)}, u32[]{:S(2)}, u32[]{:S(2)}) %collective-permute-start) | collective-permute-done | bytes 1048608 | tf_op jit(solution)/shard_map/ppermute | solution.py:528
  28.0 2.0 collective-permute-start.2
  30.3 1.8 collective-permute-done.5.a_ref
  33.6 7.8 %query_part.5 = (f32[512,1024]{1,0:T(8,128)S(1)}, f32[512,1]{1,0:T(8,128)S(1)}) custom-call(s32[8]{0:T(128)S(1)} %compare_select_fusion.4.blocks, bf16[1,8192]{1,0:T(2,128)(2,1)S(1)} %broadcast_in_dim.45.refs_0_.gain_ref, bf16[8192,1024]{1,0:T(8,128)(2,1)} %refs_1_.9, bf16[512,1024]{1,0:T(8,128)(2,1)S(1)} %copy-done.1, ...), custom_call_target="tpu_custom_call" | custom-call | flops 3221225472 | bytes 12582912 | tf_op jit(solution)/shard_map/query_part/pallas_call | solution.py:340
  43.5 8.9 %collective-permute-done.2.refs_4_ = bf16[512,1024]{1,0:T(8,128)(2,1)} collective-permute-done((bf16[512,1024]{1,0:T(8,128)(2,1)}, bf16[512,1024]{1,0:T(8,128)(2,1)}, u32[]{:S(2)}, u32[]{:S(2)}) %collective-permute-start.2) | collective-permute-done | bytes 1048608 | tf_op jit(solution)/shard_map/ppermute | solution.py:528
  69.9 6.9 %query_part.6 = (f32[512,1024]{1,0:T(8,128)S(1)}, f32[512,1]{1,0:T(8,128)S(1)}) custom-call(s32[8]{0:T(128)S(1)} %compare_select_fusion.4.blocks, bf16[1,8192]{1,0:T(2,128)(2,1)S(1)} %broadcast_in_dim.45.refs_0_.gain_ref, bf16[8192,1024]{1,0:T(8,128)(2,1)} %refs_1_.9, f32[512,1024]{1,0:T(8,128)} %copy-done.3, f32[512,1]{1,0:T(8,128)S(1)} %copy-done.14, ...), custom_call_target="tpu_custom_call" | custom-call | flops 2147483648 | bytes 8388608 | tf_op jit(solution)/shard_map/query_part/pallas_call | solution.py:340
  78.1 5.6 %collective-permute-done.9.a_ref = bf16[512,256]{1,0:T(8,128)(2,1)} collective-permute-done((bf16[512,256]{1,0:T(8,128)(2,1)}, bf16[512,256]{1,0:T(8,128)(2,1)}, u32[]{:S(2)}, u32[]{:S(2)}) %collective-permute-start.9) | collective-permute-done | bytes 262176 | tf_op jit(solution)/shard_map/ppermute | solution.py:528
  91.2 2.9 %collective-permute-done.14.a_ref = bf16[512,256]{1,0:T(8,128)(2,1)S(1)} collective-permute-done((bf16[512,256]{1,0:T(8,128)(2,1)S(1)}, bf16[512,256]{1,0:T(8,128)(2,1)S(1)}, u32[]{:S(2)}, u32[]{:S(2)}) %collective-permute-start.14) | collective-permute-done | bytes 262176 | tf_op jit(solution)/shard_map/ppermute | solution.py:528
  96.8 6.9 %query_part.7 = (f32[512,1024]{1,0:T(8,128)S(1)}, f32[512,1]{1,0:T(8,128)S(1)}) custom-call(s32[8]{0:T(128)S(1)} %compare_select_fusion.4.blocks, bf16[1,8192]{1,0:T(2,128)(2,1)S(1)} %broadcast_in_dim.45.refs_0_.gain_ref, bf16[8192,1024]{1,0:T(8,128)(2,1)} %refs_1_.9, f32[512,1024]{1,0:T(8,128)} %copy-done.4, f32[512,1]{1,0:T(8,128)S(1)} %get-tuple-element.78.refs_3_, ...), custom_call_target="tpu_custom_call" | custom-call | flops 2147483648 | bytes 8388608 | tf_op jit(solution)/shard_map/query_part/pallas_call | solution.py:340
  103.7 3.6 %collective-permute-done.16.a_ref = bf16[512,256]{1,0:T(8,128)(2,1)S(1)} collective-permute-done((bf16[512,256]{1,0:T(8,128)(2,1)S(1)}, bf16[512,256]{1,0:T(8,128)(2,1)S(1)}, u32[]{:S(2)}, u32[]{:S(2)}) %collective-permute-start.16) | collective-permute-done | bytes 262176 | tf_op jit(solution)/shard_map/ppermute | solution.py:528
  107.6 3.1 %query_part.9 = (bf16[256,1024]{1,0:T(8,128)(2,1)S(1)}, f32[256,1]{1,0:T(8,128)S(1)}) custom-call(s32[8]{0:T(128)S(1)} %compare_select_fusion.4.blocks, bf16[1,8192]{1,0:T(2,128)(2,1)S(1)} %broadcast_in_dim.45.refs_0_.gain_ref, bf16[8192,1024]{1,0:T(8,128)(2,1)} %refs_1_.9, f32[512,1024]{1,0:T(8,128)S(1)} %get-tuple-element.89.refs_2_, ...), custom_call_target="tpu_custom_call" | custom-call | flops 536870912 | bytes 4194304 | tf_op jit(solution)/shard_map/query_part/pallas_call | solution.py:340
  110.7 6.5 %contexts.2 = (bf16[256,1024]{1,0:T(8,128)(2,1)S(1)}, bf16[256,1024]{1,0:T(8,128)(2,1)S(1)}, bf16[256,1024]{1,0:T(8,128)(2,1)S(1)}) custom-call(s32[8]{0:T(128)S(1)} %compare_select_fusion.4.blocks, bf16[256,1024]{1,0:T(8,128)(2,1)S(1)} %get-tuple-element.104.refs_0_, bf16[512,256]{1,0:T(8,128)(2,1)S(1)} %bitcast.20, f32[256,768]{1,0:T(8,128)S(1)} %copy-done.11, ...), custom_call_target="tpu_custom_call" | custom-call | flops 1610612736 | bytes 4194304 | tf_op jit(solution)/shard_map/contexts/pallas_call | solution.py:438
  119.4 3.1 %query_part.8 = (bf16[256,1024]{1,0:T(8,128)(2,1)S(1)}, f32[256,1]{1,0:T(8,128)S(1)}) custom-call(s32[8]{0:T(128)S(1)} %compare_select_fusion.4.blocks, bf16[1,8192]{1,0:T(2,128)(2,1)S(1)} %broadcast_in_dim.45.refs_0_.gain_ref, bf16[8192,1024]{1,0:T(8,128)(2,1)} %refs_1_.9, f32[512,1024]{1,0:T(8,128)S(1)} %get-tuple-element.89.refs_2_, ...), custom_call_target="tpu_custom_call" | custom-call | flops 536870912 | bytes 4194304 | tf_op jit(solution)/shard_map/query_part/pallas_call | solution.py:340
  122.5 9.2 %contexts.3 = (bf16[256,1024]{1,0:T(8,128)(2,1)S(1)}, bf16[256,1024]{1,0:T(8,128)(2,1)S(1)}, bf16[256,1024]{1,0:T(8,128)(2,1)S(1)}) custom-call(s32[8]{0:T(128)S(1)} %compare_select_fusion.4.blocks, bf16[256,1024]{1,0:T(8,128)(2,1)S(1)} %get-tuple-element.114.refs_0_, bf16[1536,256]{1,0:T(8,128)(2,1)S(1)} %bitcast.19, f32[256,1536]{1,0:T(8,128)S(1)} %copy-done.7, ...), custom_call_target="tpu_custom_call" | custom-call | flops 3221225472 | bytes 4194304 | tf_op jit(solution)/shard_map/contexts/pallas_call | solution.py:438
  133.8 4.6 %output_part.4 = (bf16[256,1024]{1,0:T(8,128)(2,1)S(1)}, bf16[256,1024]{1,0:T(8,128)(2,1)S(1)}) custom-call(s32[8]{0:T(128)S(1)} %compare_select_fusion.4.blocks, bf16[256,1024]{1,0:T(8,128)(2,1)S(1)} %get-tuple-element.121.refs_0_, bf16[256,1024]{1,0:T(8,128)(2,1)S(1)} %get-tuple-element.122.refs_1_, bf16[1024,8192]{1,0:T(8,128)(2,1)} %refs_2_.9, ...), custom_call_target="tpu_custom_call" | custom-call | flops 1073741824 | bytes 4194304 | tf_op jit(solution)/shard_map/output_part/pallas_call | solution.py:505
  138.4 5.5 %output_part.5 = (bf16[256,1024]{1,0:T(8,128)(2,1)S(1)}, bf16[256,1024]{1,0:T(8,128)(2,1)S(1)}, bf16[256,1024]{1,0:T(8,128)(2,1)S(1)}, bf16[256,1024]{1,0:T(8,128)(2,1)S(1)}) custom-call(s32[8]{0:T(128)S(1)} %compare_select_fusion.4.blocks, bf16[256,1024]{1,0:T(8,128)(2,1)S(1)} %get-tuple-element.121.refs_0_, ...), custom_call_target="tpu_custom_call" | custom-call | flops 2147483648 | bytes 4194304 | tf_op jit(solution)/shard_map/output_part/pallas_call | solution.py:505
  148.5 5.5 %output_part.6 = (bf16[256,1024]{1,0:T(8,128)(2,1)S(1)}, bf16[256,1024]{1,0:T(8,128)(2,1)S(1)}, bf16[256,1024]{1,0:T(8,128)(2,1)S(1)}, bf16[256,1024]{1,0:T(8,128)(2,1)S(1)}) custom-call(s32[8]{0:T(128)S(1)} %compare_select_fusion.4.blocks, bf16[256,1024]{1,0:T(8,128)(2,1)S(1)} %get-tuple-element.121.refs_0_, ...), custom_call_target="tpu_custom_call" | custom-call | flops 2147483648 | bytes 4194304 | tf_op jit(solution)/shard_map/output_part/pallas_call | solution.py:505
  154.0 5.0 %collective-permute-done.20.refs_0_ = bf16[256,1024]{1,0:T(8,128)(2,1)S(1)} collective-permute-done((bf16[256,1024]{1,0:T(8,128)(2,1)S(1)}, bf16[256,1024]{1,0:T(8,128)(2,1)S(1)}, u32[]{:S(2)}, u32[]{:S(2)}) %collective-permute-start.20) | collective-permute-done | bytes 524320 | tf_op jit(solution)/shard_map/ppermute | solution.py:528
  161.3 9.0 %collective-permute-done.27.refs_0_ = bf16[256,1024]{1,0:T(8,128)(2,1)S(1)} collective-permute-done((bf16[256,1024]{1,0:T(8,128)(2,1)S(1)}, bf16[256,1024]{1,0:T(8,128)(2,1)S(1)}, u32[]{:S(2)}, u32[]{:S(2)}) %collective-permute-start.27) | collective-permute-done | bytes 524320 | tf_op jit(solution)/shard_map/ppermute | solution.py:528
  174.2 7.3 %collective-permute-done.22.refs_0_ = bf16[256,1024]{1,0:T(8,128)(2,1)S(1)} collective-permute-done((bf16[256,1024]{1,0:T(8,128)(2,1)S(1)}, bf16[256,1024]{1,0:T(8,128)(2,1)S(1)}, u32[]{:S(2)}, u32[]{:S(2)}) %collective-permute-start.22) | collective-permute-done | bytes 524320 | tf_op jit(solution)/shard_map/ppermute | solution.py:528
  182.7 2.8 %collective-permute-done.30.refs_0_ = bf16[256,1024]{1,0:T(8,128)(2,1)S(1)} collective-permute-done((bf16[256,1024]{1,0:T(8,128)(2,1)S(1)}, bf16[256,1024]{1,0:T(8,128)(2,1)S(1)}, u32[]{:S(2)}, u32[]{:S(2)}) %collective-permute-start.30) | collective-permute-done | bytes 524320 | tf_op jit(solution)/shard_map/ppermute | solution.py:528
  187.2 4.1 %output_part.7 = (bf16[256,1024]{1,0:T(8,128)(2,1)S(1)}, bf16[256,1024]{1,0:T(8,128)(2,1)S(1)}) custom-call(s32[8]{0:T(128)S(1)} %compare_select_fusion.4.blocks, bf16[256,1024]{1,0:T(8,128)(2,1)S(1)} %get-tuple-element.121.refs_0_, bf16[256,1024]{1,0:T(8,128)(2,1)S(1)} %get-tuple-element.122.refs_1_, bf16[1024,8192]{1,0:T(8,128)(2,1)} %refs_2_.9), custom_call_target="tpu_custom_call" | custom-call | flops 1073741824 | bytes 2097152 | tf_op jit(solution)/shard_map/output_part/pallas_call | solution.py:505
  191.3 2.0 collective-permute-done.24.refs_1_
  193.3 5.1 %collective-permute-done.23.refs_0_ = bf16[256,1024]{1,0:T(8,128)(2,1)S(1)} collective-permute-done((bf16[256,1024]{1,0:T(8,128)(2,1)S(1)}, bf16[256,1024]{1,0:T(8,128)(2,1)S(1)}, u32[]{:S(2)}, u32[]{:S(2)}) %collective-permute-start.23) | collective-permute-done | bytes 524320 | tf_op jit(solution)/shard_map/ppermute | solution.py:659
  198.9 2.3 %last_parts.1 = (f32[512,1024]{1,0:T(8,128)}, bf16[512,1024]{1,0:T(8,128)(2,1)}, f32[8,512]{1,0:T(8,128)S(1)}) custom-call(bf16[512,1024]{1,0:T(8,128)(2,1)S(1)} %copy-done.2, bf16[256,1024]{1,0:T(8,128)(2,1)S(1)} %collective-permute-done.23.refs_0_, bf16[256,1024]{1,0:T(8,128)(2,1)S(1)} %collective-permute-done.24.refs_1_, ...), custom_call_target="tpu_custom_call" | custom-call | flops 2097152 | bytes 6291456 | tf_op jit(solution)/shard_map/last_parts/pallas_call | solution.py:226
  202.4 2.5 %collective-permute-done.32 = f32[8,512]{1,0:T(8,128)S(1)} collective-permute-done((f32[8,512]{1,0:T(8,128)S(1)}, f32[8,512]{1,0:T(8,128)S(1)}, u32[]{:S(2)}, u32[]{:S(2)}) %collective-permute-start.32) | collective-permute-done | bytes 16416 | tf_op jit(solution)/shard_map/ppermute | solution.py:533
  205.0 3.2 %collective-permute-start.35 = (f32[8,512]{1,0:T(8,128)S(1)}, f32[8,512]{1,0:T(8,128)S(1)}, u32[]{:S(2)}, u32[]{:S(2)}) collective-permute-start(f32[8,512]{1,0:T(8,128)S(1)} %add.70), channel_id=1, source_target_pairs={{0,12},{2,14},{4,8},{6,10},{8,4},{10,6},{12,0},{14,2},{1,13},{3,15... | collective-permute-start | bytes 49160 | tf_op jit(solution)/shard_map/ppermute | solution.py:533
  210.5 2.3 %collective-permute-done.34 = f32[8,512]{1,0:T(8,128)S(1)} collective-permute-done((f32[8,512]{1,0:T(8,128)S(1)}, f32[8,512]{1,0:T(8,128)S(1)}, u32[]{:S(2)}, u32[]{:S(2)}) %collective-permute-start.34) | collective-permute-done | bytes 16416 | tf_op jit(solution)/shard_map/ppermute | solution.py:533
  214.4 2.0 norm_out.1
  (141 shorter events, 63.6 us)
Async XLA Ops:
  0.6 27.4 %collective-permute-start = (bf16[512,1024]{1,0:T(8,128)(2,1)}, bf16[512,1024]{1,0:T(8,128)(2,1)}, u32[]{:S(2)}, u32[]{:S(2)}) collective-permute-start(bf16[512,1024]{1,0:T(8,128)(2,1)} %x_ref.2), channel_id=1, source_target_pairs={{4,0},{8,4},{12,8},{14,12},{10,14},{6,10},{2,6},{0,2},{5,1},{9,5},... | collective-permute-start | bytes 3145736 | tf_op jit(solution)/shard_map/ppermute | solution.py:528
  3.6 26.4 %collective-permute-start.1 = (bf16[512,1024]{1,0:T(8,128)(2,1)}, bf16[512,1024]{1,0:T(8,128)(2,1)}, u32[]{:S(2)}, u32[]{:S(2)}) collective-permute-start(bf16[512,1024]{1,0:T(8,128)(2,1)} %x_ref.2), channel_id=1, source_target_pairs={{0,4},{4,8},{8,12},{12,14},{14,10},{10,6},{6,2},{2,0},{1,5},{5,9},... | collective-permute-start | bytes 3145736 | tf_op jit(solution)/shard_map/ppermute | solution.py:528
  17.0 15.2 %collective-permute-start.5 = (bf16[256,256]{1,0:T(8,128)(2,1)}, bf16[256,256]{1,0:T(8,128)(2,1)S(1)}, u32[]{:S(2)}, u32[]{:S(2)}) collective-permute-start(bf16[256,256]{1,0:T(8,128)(2,1)} %get-tuple-element.80), channel_id=1, source_target_pairs={{0,4},{4,8},{8,12},{12,14},{14,10},{10,6},{6,2},{2,0},{1,5},{5,9},... | collective-permute-start | bytes 393224 | tf_op jit(solution)/shard_map/ppermute | solution.py:528
  18.9 13.2 %collective-permute-start.6 = (bf16[256,256]{1,0:T(8,128)(2,1)S(1)}, bf16[256,256]{1,0:T(8,128)(2,1)S(1)}, u32[]{:S(2)}, u32[]{:S(2)}) collective-permute-start(bf16[256,256]{1,0:T(8,128)(2,1)S(1)} %get-tuple-element.81), channel_id=1, source_target_pairs={{4,0},{8,4},{12,8},{14,12},{10,14},{6,10},{2,6},{0,2},{5,1},{9,5},... | collective-permute-start | bytes 393224 | tf_op jit(solution)/shard_map/ppermute | solution.py:528
  20.4 45.3 %collective-permute-start.11 = (bf16[96,16,256]{2,1,0:T(8,128)(2,1)S(1)}, bf16[96,16,256]{2,1,0:T(8,128)(2,1)}, u32[]{:S(2)}, u32[]{:S(2)}) collective-permute-start(bf16[96,16,256]{2,1,0:T(8,128)(2,1)S(1)} %constant_dynamic-slice_fusion), channel_id=1, source_target_pairs={{0,1},{1,0},{2,3},{3,2},{4,5},{5,4},{6,7},{7,6},{8,9},{9,8},{10,11... | collective-permute-start | bytes 2359304 | tf_op jit(solution)/shard_map/ppermute | solution.py:584
  28.0 24.5 %collective-permute-start.2 = (bf16[512,1024]{1,0:T(8,128)(2,1)}, bf16[512,1024]{1,0:T(8,128)(2,1)}, u32[]{:S(2)}, u32[]{:S(2)}) collective-permute-start(bf16[512,1024]{1,0:T(8,128)(2,1)} %collective-permute-done.refs_3_), channel_id=1, source_target_pairs={{4,0},{8,4},{12,8},{14,12},{10,14},{6,10},{2,6},{0,2},{5,1},{9,5},... | collective-permute-start | bytes 3145736 | tf_op jit(solution)/shard_map/ppermute | solution.py:528
  30.0 23.8 %collective-permute-start.3 = (bf16[512,1024]{1,0:T(8,128)(2,1)}, bf16[512,1024]{1,0:T(8,128)(2,1)}, u32[]{:S(2)}, u32[]{:S(2)}) collective-permute-start(bf16[512,1024]{1,0:T(8,128)(2,1)} %collective-permute-done.1.refs_4_), channel_id=1, source_target_pairs={{0,4},{4,8},{8,12},{12,14},{14,10},{10,6},{6,2},{2,0},{1,5},{5,9},... | collective-permute-start | bytes 3145736 | tf_op jit(solution)/shard_map/ppermute | solution.py:528
  53.9 34.2 %collective-permute-start.7 = (bf16[512,1024]{1,0:T(8,128)(2,1)}, bf16[512,1024]{1,0:T(8,128)(2,1)}, u32[]{:S(2)}, u32[]{:S(2)}) collective-permute-start(bf16[512,1024]{1,0:T(8,128)(2,1)} %collective-permute-done.2.refs_4_), channel_id=1, source_target_pairs={{4,0},{8,4},{12,8},{14,12},{10,14},{6,10},{2,6},{0,2},{5,1},{9,5},... | collective-permute-start | bytes 3145736 | tf_op jit(solution)/shard_map/ppermute | solution.py:528
  55.4 31.6 %collective-permute-start.8 = (bf16[512,1024]{1,0:T(8,128)(2,1)}, bf16[512,1024]{1,0:T(8,128)(2,1)}, u32[]{:S(2)}, u32[]{:S(2)}) collective-permute-start(bf16[512,1024]{1,0:T(8,128)(2,1)} %collective-permute-done.3.refs_5_), channel_id=1, source_target_pairs={{0,4},{4,8},{8,12},{12,14},{14,10},{10,6},{6,2},{2,0},{1,5},{5,9},... | collective-permute-start | bytes 3145736 | tf_op jit(solution)/shard_map/ppermute | solution.py:528
  57.1 26.6 %collective-permute-start.9 = (bf16[512,256]{1,0:T(8,128)(2,1)}, bf16[512,256]{1,0:T(8,128)(2,1)}, u32[]{:S(2)}, u32[]{:S(2)}) collective-permute-start(bf16[512,256]{1,0:T(8,128)(2,1)} %copy-done.16), channel_id=1, source_target_pairs={{0,4},{4,8},{8,12},{12,14},{14,10},{10,6},{6,2},{2,0},{1,5},{5,9},... | collective-permute-start | bytes 786440 | tf_op jit(solution)/shard_map/ppermute | solution.py:528
  57.5 26.2 %collective-permute-start.10 = (bf16[512,256]{1,0:T(8,128)(2,1)}, bf16[512,256]{1,0:T(8,128)(2,1)}, u32[]{:S(2)}, u32[]{:S(2)}) collective-permute-start(bf16[512,256]{1,0:T(8,128)(2,1)} %copy-done.15), channel_id=1, source_target_pairs={{4,0},{8,4},{12,8},{14,12},{10,14},{6,10},{2,6},{0,2},{5,1},{9,5},... | collective-permute-start | bytes 786440 | tf_op jit(solution)/shard_map/ppermute | solution.py:528
  84.9 9.2 %collective-permute-start.14 = (bf16[512,256]{1,0:T(8,128)(2,1)S(1)}, bf16[512,256]{1,0:T(8,128)(2,1)S(1)}, u32[]{:S(2)}, u32[]{:S(2)}) collective-permute-start(bf16[512,256]{1,0:T(8,128)(2,1)S(1)} %get-tuple-element.99), channel_id=1, source_target_pairs={{0,4},{4,8},{8,12},{12,14},{14,10},{10,6},{6,2},{2,0},{1,5},{5,9},... | collective-permute-start | bytes 786440 | tf_op jit(solution)/shard_map/ppermute | solution.py:528
  85.4 9.2 %collective-permute-start.15 = (bf16[512,256]{1,0:T(8,128)(2,1)S(1)}, bf16[512,256]{1,0:T(8,128)(2,1)S(1)}, u32[]{:S(2)}, u32[]{:S(2)}) collective-permute-start(bf16[512,256]{1,0:T(8,128)(2,1)S(1)} %get-tuple-element.100), channel_id=1, source_target_pairs={{4,0},{8,4},{12,8},{14,12},{10,14},{6,10},{2,6},{0,2},{5,1},{9,5},... | collective-permute-start | bytes 786440 | tf_op jit(solution)/shard_map/ppermute | solution.py:528
  89.2 18.4 %collective-permute-start.13 = (bf16[256,1024]{1,0:T(8,128)(2,1)S(1)}, bf16[256,1024]{1,0:T(8,128)(2,1)S(1)}, u32[]{:S(2)}, u32[]{:S(2)}) collective-permute-start(bf16[256,1024]{1,0:T(8,128)(2,1)S(1)} %slice.34), channel_id=1, source_target_pairs={{0,4},{4,8},{8,12},{12,14},{14,10},{10,6},{6,2},{2,0},{1,5},{5,9},... | collective-permute-start | bytes 1572872 | tf_op jit(solution)/shard_map/ppermute | solution.py:528
  89.7 29.7 %collective-permute-start.12 = (bf16[256,1024]{1,0:T(8,128)(2,1)S(1)}, bf16[256,1024]{1,0:T(8,128)(2,1)S(1)}, u32[]{:S(2)}, u32[]{:S(2)}) collective-permute-start(bf16[256,1024]{1,0:T(8,128)(2,1)S(1)} %slice.35), channel_id=1, source_target_pairs={{4,0},{8,4},{12,8},{14,12},{10,14},{6,10},{2,6},{0,2},{5,1},{9,5},... | collective-permute-start | bytes 1572872 | tf_op jit(solution)/shard_map/ppermute | solution.py:528
  94.7 12.5 %collective-permute-start.16 = (bf16[512,256]{1,0:T(8,128)(2,1)S(1)}, bf16[512,256]{1,0:T(8,128)(2,1)S(1)}, u32[]{:S(2)}, u32[]{:S(2)}) collective-permute-start(bf16[512,256]{1,0:T(8,128)(2,1)S(1)} %get-tuple-element.107), channel_id=1, source_target_pairs={{0,4},{4,8},{8,12},{12,14},{14,10},{10,6},{6,2},{2,0},{1,5},{5,9},... | collective-permute-start | bytes 786440 | tf_op jit(solution)/shard_map/ppermute | solution.py:528
  95.4 12.0 %collective-permute-start.17 = (bf16[512,256]{1,0:T(8,128)(2,1)S(1)}, bf16[512,256]{1,0:T(8,128)(2,1)S(1)}, u32[]{:S(2)}, u32[]{:S(2)}) collective-permute-start(bf16[512,256]{1,0:T(8,128)(2,1)S(1)} %get-tuple-element.108), channel_id=1, source_target_pairs={{4,0},{8,4},{12,8},{14,12},{10,14},{6,10},{2,6},{0,2},{5,1},{9,5},... | collective-permute-start | bytes 786440 | tf_op jit(solution)/shard_map/ppermute | solution.py:528
  117.3 16.6 %collective-permute-start.18 = (bf16[256,1024]{1,0:T(8,128)(2,1)S(1)}, bf16[256,1024]{1,0:T(8,128)(2,1)S(1)}, u32[]{:S(2)}, u32[]{:S(2)}) collective-permute-start(bf16[256,1024]{1,0:T(8,128)(2,1)S(1)} %get-tuple-element.113), channel_id=1, source_target_pairs={{0,4},{4,8},{8,12},{12,14},{14,10},{10,6},{6,2},{2,0},{1,5},{5,9},... | collective-permute-start | bytes 1572872 | tf_op jit(solution)/shard_map/ppermute | solution.py:528
  118.3 15.6 %collective-permute-start.19 = (bf16[256,1024]{1,0:T(8,128)(2,1)S(1)}, bf16[256,1024]{1,0:T(8,128)(2,1)S(1)}, u32[]{:S(2)}, u32[]{:S(2)}) collective-permute-start(bf16[256,1024]{1,0:T(8,128)(2,1)S(1)} %get-tuple-element.118), channel_id=1, source_target_pairs={{4,0},{8,4},{12,8},{14,12},{10,14},{6,10},{2,6},{0,2},{5,1},{9,5},... | collective-permute-start | bytes 1572872 | tf_op jit(solution)/shard_map/ppermute | solution.py:528
  131.8 14.5 %collective-permute-start.25 = (bf16[256,1024]{1,0:T(8,128)(2,1)S(1)}, bf16[256,1024]{1,0:T(8,128)(2,1)S(1)}, u32[]{:S(2)}, u32[]{:S(2)}) collective-permute-start(bf16[256,1024]{1,0:T(8,128)(2,1)S(1)} %get-tuple-element.133), channel_id=1, source_target_pairs={{0,4},{4,8},{8,12},{12,14},{14,10},{10,6},{6,2},{2,0},{1,5},{5,9},... | collective-permute-start | bytes 1572872 | tf_op jit(solution)/shard_map/ppermute | solution.py:528
  132.8 13.4 %collective-permute-start.26 = (bf16[256,1024]{1,0:T(8,128)(2,1)S(1)}, bf16[256,1024]{1,0:T(8,128)(2,1)S(1)}, u32[]{:S(2)}, u32[]{:S(2)}) collective-permute-start(bf16[256,1024]{1,0:T(8,128)(2,1)S(1)} %get-tuple-element.134), channel_id=1, source_target_pairs={{4,0},{8,4},{12,8},{14,12},{10,14},{6,10},{2,6},{0,2},{5,1},{9,5},... | collective-permute-start | bytes 1572872 | tf_op jit(solution)/shard_map/ppermute | solution.py:528
  144.1 14.9 %collective-permute-start.20 = (bf16[256,1024]{1,0:T(8,128)(2,1)S(1)}, bf16[256,1024]{1,0:T(8,128)(2,1)S(1)}, u32[]{:S(2)}, u32[]{:S(2)}) collective-permute-start(bf16[256,1024]{1,0:T(8,128)(2,1)S(1)} %get-tuple-element.125), channel_id=1, source_target_pairs={{0,4},{4,8},{8,12},{12,14},{14,10},{10,6},{6,2},{2,0},{1,5},{5,9},... | collective-permute-start | bytes 1572872 | tf_op jit(solution)/shard_map/ppermute | solution.py:528
  145.2 14.4 %collective-permute-start.21 = (bf16[256,1024]{1,0:T(8,128)(2,1)S(1)}, bf16[256,1024]{1,0:T(8,128)(2,1)S(1)}, u32[]{:S(2)}, u32[]{:S(2)}) collective-permute-start(bf16[256,1024]{1,0:T(8,128)(2,1)S(1)} %get-tuple-element.126), channel_id=1, source_target_pairs={{4,0},{8,4},{12,8},{14,12},{10,14},{6,10},{2,6},{0,2},{5,1},{9,5},... | collective-permute-start | bytes 1572872 | tf_op jit(solution)/shard_map/ppermute | solution.py:528
  146.4 23.8 %collective-permute-start.27 = (bf16[256,1024]{1,0:T(8,128)(2,1)S(1)}, bf16[256,1024]{1,0:T(8,128)(2,1)S(1)}, u32[]{:S(2)}, u32[]{:S(2)}) collective-permute-start(bf16[256,1024]{1,0:T(8,128)(2,1)S(1)} %get-tuple-element.137), channel_id=1, source_target_pairs={{0,4},{4,8},{8,12},{12,14},{14,10},{10,6},{6,2},{2,0},{1,5},{5,9},... | collective-permute-start | bytes 1572872 | tf_op jit(solution)/shard_map/ppermute | solution.py:528
  147.5 22.8 %collective-permute-start.28 = (bf16[256,1024]{1,0:T(8,128)(2,1)S(1)}, bf16[256,1024]{1,0:T(8,128)(2,1)S(1)}, u32[]{:S(2)}, u32[]{:S(2)}) collective-permute-start(bf16[256,1024]{1,0:T(8,128)(2,1)S(1)} %get-tuple-element.138), channel_id=1, source_target_pairs={{4,0},{8,4},{12,8},{14,12},{10,14},{6,10},{2,6},{0,2},{5,1},{9,5},... | collective-permute-start | bytes 1572872 | tf_op jit(solution)/shard_map/ppermute | solution.py:528
  159.8 21.7 %collective-permute-start.22 = (bf16[256,1024]{1,0:T(8,128)(2,1)S(1)}, bf16[256,1024]{1,0:T(8,128)(2,1)S(1)}, u32[]{:S(2)}, u32[]{:S(2)}) collective-permute-start(bf16[256,1024]{1,0:T(8,128)(2,1)S(1)} %get-tuple-element.129), channel_id=1, source_target_pairs={{0,4},{4,8},{8,12},{12,14},{14,10},{10,6},{6,2},{2,0},{1,5},{5,9},... | collective-permute-start | bytes 1572872 | tf_op jit(solution)/shard_map/ppermute | solution.py:528
  170.5 14.9 %collective-permute-start.30 = (bf16[256,1024]{1,0:T(8,128)(2,1)S(1)}, bf16[256,1024]{1,0:T(8,128)(2,1)S(1)}, u32[]{:S(2)}, u32[]{:S(2)}) collective-permute-start(bf16[256,1024]{1,0:T(8,128)(2,1)S(1)} %get-tuple-element.142), channel_id=1, source_target_pairs={{4,0},{8,4},{12,8},{14,12},{10,14},{6,10},{2,6},{0,2},{5,1},{9,5},... | collective-permute-start | bytes 1572872 | tf_op jit(solution)/shard_map/ppermute | solution.py:528
  172.1 21.2 %collective-permute-start.24 = (bf16[256,1024]{1,0:T(8,128)(2,1)S(1)}, bf16[256,1024]{1,0:T(8,128)(2,1)S(1)}, u32[]{:S(2)}, u32[]{:S(2)}) collective-permute-start(bf16[256,1024]{1,0:T(8,128)(2,1)S(1)} %get-tuple-element.131), channel_id=1, source_target_pairs={{4,0},{8,4},{12,8},{14,12},{10,14},{6,10},{2,6},{0,2},{5,1},{9,5},... | collective-permute-start | bytes 1572872 | tf_op jit(solution)/shard_map/ppermute | solution.py:528
  173.7 19.6 %collective-permute-start.29 = (bf16[256,1024]{1,0:T(8,128)(2,1)S(1)}, bf16[256,1024]{1,0:T(8,128)(2,1)S(1)}, u32[]{:S(2)}, u32[]{:S(2)}) collective-permute-start(bf16[256,1024]{1,0:T(8,128)(2,1)S(1)} %get-tuple-element.141), channel_id=1, source_target_pairs={{0,4},{4,8},{8,12},{12,14},{14,10},{10,6},{6,2},{2,0},{1,5},{5,9},... | collective-permute-start | bytes 1572872 | tf_op jit(solution)/shard_map/ppermute | solution.py:528
  181.6 16.7 %collective-permute-start.23 = (bf16[256,1024]{1,0:T(8,128)(2,1)S(1)}, bf16[256,1024]{1,0:T(8,128)(2,1)S(1)}, u32[]{:S(2)}, u32[]{:S(2)}) collective-permute-start(bf16[256,1024]{1,0:T(8,128)(2,1)S(1)} %add_parts.8), channel_id=1, source_target_pairs={{0,4},{4,8},{8,12},{12,14},{14,10},{10,6},{6,2},{2,0},{1,5},{5,9},... | collective-permute-start | bytes 1572872 | tf_op jit(solution)/shard_map/ppermute | solution.py:659
  185.6 13.3 %collective-permute-start.31 = (bf16[256,1024]{1,0:T(8,128)(2,1)S(1)}, bf16[256,1024]{1,0:T(8,128)(2,1)S(1)}, u32[]{:S(2)}, u32[]{:S(2)}) collective-permute-start(bf16[256,1024]{1,0:T(8,128)(2,1)S(1)} %add_parts.11), channel_id=1, source_target_pairs={{4,0},{8,4},{12,8},{14,12},{10,14},{6,10},{2,6},{0,2},{5,1},{9,5},... | collective-permute-start | bytes 1572872 | tf_op jit(solution)/shard_map/ppermute | solution.py:660
  205.0 5.5 %collective-permute-start.35 = (f32[8,512]{1,0:T(8,128)S(1)}, f32[8,512]{1,0:T(8,128)S(1)}, u32[]{:S(2)}, u32[]{:S(2)}) collective-permute-start(f32[8,512]{1,0:T(8,128)S(1)} %add.70), channel_id=1, source_target_pairs={{0,12},{2,14},{4,8},{6,10},{8,4},{10,6},{12,0},{14,2},{1,13},{3,15... | collective-permute-start | bytes 49160 | tf_op jit(solution)/shard_map/ppermute | solution.py:533
  (24 other events, 111.0 us)

commit v5 on v4

--- a/solution.py
+++ b/solution.py
@@ -246,16 +246,11 @@
 
 def norm_out(mixed, squares, gain, width):
     rows, columns = mixed.shape
-    block = pl.BlockSpec((128, columns), lambda i: (i, 0))
     return pl.pallas_call(
         functools.partial(norm_kernel, width),
-        grid=(rows // 128,),
-        in_specs=[
-            block,
-            pl.BlockSpec((8, 128), lambda i: (0, i)),
-            pl.BlockSpec((1, columns), lambda i: (0, 0)),
-        ],
-        out_specs=block,
+        grid=(1,),
+        in_specs=[pl.BlockSpec(a.shape, lambda i: (0, 0)) for a in (mixed, squares, gain)],
+        out_specs=pl.BlockSpec((rows, columns), lambda i: (0, 0)),
         out_shape=shaped((rows, columns), jnp.bfloat16),
         compiler_params=VMEM,
         cost_estimate=cost(3 * mixed.size, 6 * mixed.size),
@@ -420,10 +415,12 @@
             product[:, at] = dot(out_ref[...], held[i, :, at]).astype(jnp.bfloat16)
 
 
-def contexts(heads, q, pages, bias, pairs, inv, angles, blocks, weight=None, places=()):
-    rows, width = q.shape
+def contexts(at, heads, q, pages, bias, pairs, inv, angles, blocks, weight=None, places=()):
+    rows, width = bias.shape[0], q.shape[1]
     operands = [q, pages, bias, pairs, inv, *angles]
     in_specs = [pl.BlockSpec(a.shape, lambda i, b: (0, 0)) for a in operands]
+    in_specs[0] = pl.BlockSpec((rows, width), lambda i, b: (at, 0))
+    in_specs[4] = pl.BlockSpec((rows, 1), lambda i, b: (at, 0))
     out_shape = [shaped((rows, width), jnp.bfloat16)]
     scratch = []
     if places:
@@ -600,7 +597,9 @@
 
     def attend(which, q, pairs, inv, blocks, *product):
         heads, pages = ((prefill_heads, prefix_rows), (decode_heads, cache))[which]
-        return contexts(heads, q, pages, bias[which], pairs, inv, angles[which], blocks, *product)
+        return contexts(
+            which, heads, q, pages, bias[which], pairs, inv, angles[which], blocks, *product
+        )
 
     exit_row = lax.dynamic_slice_in_dim(exit_gain, me * width, width, 0)
     exit_row = exit_row.astype(jnp.float32)[None, :]
@@ -614,11 +613,6 @@
         def query(places, sums=None, **more):
             pieces = [back[k] if k < FAR else ahead[RING - k] for k in places]
             return query_part(places, pieces, gain_row, query_weight, blocks, sums, **more)
-
-        def query_end(pieces, which, sums):
-            return query_part(
-                (FAR,), pieces, gain_row, query_weight, blocks, sums, angles[which], which
-            )
 
         def settled(arrived, *others):
             return lax.optimization_barrier((*arrived, *others))[:2]
@@ -639,12 +633,12 @@
         sums = query((3, 5), sums)
         pairs = end_pairs(*settled(hop(*moving), sums[1]), parts)
 
-        q, inv = query_end([ahead[FAR]], 0, sums)
+        q, inv = query_part(
+            (FAR,), [ahead[FAR], back[FAR]], gain_row, query_weight, blocks, sums, (cosine, sine)
+        )
         prefilled, p4, p5 = attend(0, q, pairs[0], inv, blocks, output_weight, (4, 5))
         p_ahead, p_back = hop(p4, p5)
-        q, inv = query_end([back[FAR]], 1, sums)
-        q = after(q, p4)
-        decoded, d4, d3 = attend(1, q, pairs[1], inv, blocks, output_weight, (4, 3))
+        decoded, d4, d3 = attend(1, after(q, p4), pairs[1], inv, blocks, output_weight, (4, 3))
         decoded, p_ahead, p_back = lax.optimization_barrier((decoded, p_ahead, p_back))
         d_ahead, d_back = hop(d3, d4)
         both = [prefilled, decoded]
@@ -674,8 +668,8 @@
     one = jnp.ones_like(inv)
     none = jnp.zeros((1,), jnp.int32)
     context = [
-        attend(0, q[:prefill], pairs[:prefill], one[:prefill], none)[0],
-        attend(1, q[prefill:], pairs[prefill:], one[prefill:], none)[0],
+        attend(0, q, pairs[:prefill], one, none)[0],
+        attend(1, q, pairs[prefill:], one, none)[0],
     ]
     context = jnp.concatenate(context, axis=0)
     summed = lax.psum_scatter(

time: 217 us -> 214 us (0.986)
  Pallas kernels: 79.6 us -> 77.3 us
    pallas_call x5 -> x4, Pallas kernels: 27.8 us -> 25.4 us  [query_part(): pl.pallas_call(functools.partial(query_kernel, count, first, last, weight...]
    unnamed x43 -> x51, local copies, waits for them, and re-layouts: 13.8 us -> 12.3 us
  transfers between devices with their start and end apart: 36 -> 36, of which waited for: 20 -> 20; matrix products, arithmetic and copies ran while one was open for 7% -> 7% of each run, Pallas kernels for 35% -> 30%
where the time goes in v5:
time: 214 us; the launch traced here: 213 us
  Pallas kernels  77.3 us (36%)
  waiting for transfers between devices  70.3 us (33%)
  starting transfers between devices  39.5 us (18%)
  local copies, waits for them, and re-layouts  21.8 us (10%)
  other arithmetic  3.34 us (2%)
    ppermute x14, waiting for transfers between devices, hop(): lax.ppermute(ahead, 'tensor', FORWARD)  36.5 us
    pallas_call x4, Pallas kernels, query_part(): pl.pallas_call(functools.partial(query_kernel, count, first, last, weight...  25.4 us
    ppermute x14, waiting for transfers between devices, hop(): lax.ppermute(back, 'tensor', BACKWARD)  22.9 us
    ppermute x14, starting transfers between devices, hop(): lax.ppermute(back, 'tensor', BACKWARD)  20.1 us
    pallas_call x4, Pallas kernels, output_part(): pl.pallas_call(functools.partial(output_kernel, count, tuple(jobs)), grid...  19.6 us
    pallas_call x2, Pallas kernels, contexts(): pl.pallas_call(functools.partial(context_kernel, heads, places), grid_spe...  15.8 us
    unnamed x51, local copies, waits for them, and re-layouts  12.3 us
    ppermute x14, starting transfers between devices, hop(): lax.ppermute(ahead, 'tensor', FORWARD)  10.9 us
  transfers between devices with their start and end apart: 36, of which 20 were waited for; matrix products, arithmetic and copies ran while one was open for 7% of the time, Pallas kernels for 30%

profile of v5, /device:TPU:0, one launch (start us, length us, event | category | flops | bytes accessed | tf_op | source)
XLA Modules:
  0.0 213.4 jit_solution(7209955990747013936)
XLA Ops:
  0.6 3.0 %collective-permute-start = (bf16[512,1024]{1,0:T(8,128)(2,1)}, bf16[512,1024]{1,0:T(8,128)(2,1)}, u32[]{:S(2)}, u32[]{:S(2)}) collective-permute-start(bf16[512,1024]{1,0:T(8,128)(2,1)} %x_ref.2), channel_id=1, source_target_pairs={{4,0},{8,4},{12,8},{14,12},{10,14},{6,10},{2,6},{0,2},{5,1},{9,5},... | collective-permute-start | bytes 3145736 | tf_op jit(solution)/shard_map/ppermute | solution.py:525
  9.1 7.9 %pairs_partial.1 = (bf16[8,512,256]{2,1,0:T(8,128)(2,1)S(1)}, bf16[256,256]{1,0:T(8,128)(2,1)}, bf16[256,256]{1,0:T(8,128)(2,1)S(1)}) custom-call(s32[8]{0:T(128)S(1)} %compare_select_fusion.4.blocks, bf16[512,1024]{1,0:T(8,128)(2,1)S(1)} %copy-done, bf16[1,8192]{1,0:T(2,128)(2,1)S(1)} %broadcast_in_dim.45.refs_0_.gain_ref, bf16[1024,2048]{1,0:T(8,128)(2,1)} %w_ref.1), custom_call_target="tpu_custom_call" | custom-call | flops 2147483648 | bytes 9437184 | tf_op jit(solution)/shard_map/pairs_partial/pallas_call | solution.py:99
  17.0 2.0 collective-permute-start.5
  20.8 7.2 %collective-permute-done.refs_3_ = bf16[512,1024]{1,0:T(8,128)(2,1)} collective-permute-done((bf16[512,1024]{1,0:T(8,128)(2,1)}, bf16[512,1024]{1,0:T(8,128)(2,1)}, u32[]{:S(2)}, u32[]{:S(2)}) %collective-permute-start) | collective-permute-done | bytes 1048608 | tf_op jit(solution)/shard_map/ppermute | solution.py:525
  28.0 2.0 collective-permute-start.2
  30.3 1.8 collective-permute-done.5.a_ref
  33.6 7.8 %query_part.4 = (f32[512,1024]{1,0:T(8,128)S(1)}, f32[512,1]{1,0:T(8,128)S(1)}) custom-call(s32[8]{0:T(128)S(1)} %compare_select_fusion.4.blocks, bf16[1,8192]{1,0:T(2,128)(2,1)S(1)} %broadcast_in_dim.45.refs_0_.gain_ref, bf16[8192,1024]{1,0:T(8,128)(2,1)} %refs_1_.7, bf16[512,1024]{1,0:T(8,128)(2,1)S(1)} %copy-done.1, ...), custom_call_target="tpu_custom_call" | custom-call | flops 3221225472 | bytes 12582912 | tf_op jit(solution)/shard_map/query_part/pallas_call | solution.py:335
  42.8 9.7 %collective-permute-done.2.refs_4_ = bf16[512,1024]{1,0:T(8,128)(2,1)} collective-permute-done((bf16[512,1024]{1,0:T(8,128)(2,1)}, bf16[512,1024]{1,0:T(8,128)(2,1)}, u32[]{:S(2)}, u32[]{:S(2)}) %collective-permute-start.2) | collective-permute-done | bytes 1048608 | tf_op jit(solution)/shard_map/ppermute | solution.py:525
  65.6 1.7 gather_fusion
  69.8 6.9 %query_part.5 = (f32[512,1024]{1,0:T(8,128)S(1)}, f32[512,1]{1,0:T(8,128)S(1)}) custom-call(s32[8]{0:T(128)S(1)} %compare_select_fusion.4.blocks, bf16[1,8192]{1,0:T(2,128)(2,1)S(1)} %broadcast_in_dim.45.refs_0_.gain_ref, bf16[8192,1024]{1,0:T(8,128)(2,1)} %refs_1_.7, f32[512,1024]{1,0:T(8,128)} %copy-done.4, f32[512,1]{1,0:T(8,128)S(1)} %copy-done.14, ...), custom_call_target="tpu_custom_call" | custom-call | flops 2147483648 | bytes 8388608 | tf_op jit(solution)/shard_map/query_part/pallas_call | solution.py:335
  78.0 5.7 %collective-permute-done.9.a_ref = bf16[512,256]{1,0:T(8,128)(2,1)} collective-permute-done((bf16[512,256]{1,0:T(8,128)(2,1)}, bf16[512,256]{1,0:T(8,128)(2,1)}, u32[]{:S(2)}, u32[]{:S(2)}) %collective-permute-start.9) | collective-permute-done | bytes 262176 | tf_op jit(solution)/shard_map/ppermute | solution.py:525
  91.3 2.9 %collective-permute-done.14.a_ref = bf16[512,256]{1,0:T(8,128)(2,1)S(1)} collective-permute-done((bf16[512,256]{1,0:T(8,128)(2,1)S(1)}, bf16[512,256]{1,0:T(8,128)(2,1)S(1)}, u32[]{:S(2)}, u32[]{:S(2)}) %collective-permute-start.14) | collective-permute-done | bytes 262176 | tf_op jit(solution)/shard_map/ppermute | solution.py:525
  97.0 6.9 %query_part.6 = (f32[512,1024]{1,0:T(8,128)S(1)}, f32[512,1]{1,0:T(8,128)S(1)}) custom-call(s32[8]{0:T(128)S(1)} %compare_select_fusion.4.blocks, bf16[1,8192]{1,0:T(2,128)(2,1)S(1)} %broadcast_in_dim.45.refs_0_.gain_ref, bf16[8192,1024]{1,0:T(8,128)(2,1)} %refs_1_.7, f32[512,1024]{1,0:T(8,128)} %copy-done.3, f32[512,1]{1,0:T(8,128)S(1)} %get-tuple-element.76.refs_3_, ...), custom_call_target="tpu_custom_call" | custom-call | flops 2147483648 | bytes 8388608 | tf_op jit(solution)/shard_map/query_part/pallas_call | solution.py:335
  103.9 3.4 %collective-permute-done.16.a_ref = bf16[512,256]{1,0:T(8,128)(2,1)S(1)} collective-permute-done((bf16[512,256]{1,0:T(8,128)(2,1)S(1)}, bf16[512,256]{1,0:T(8,128)(2,1)S(1)}, u32[]{:S(2)}, u32[]{:S(2)}) %collective-permute-start.16) | collective-permute-done | bytes 262176 | tf_op jit(solution)/shard_map/ppermute | solution.py:525
  107.6 3.8 %query_part.7 = (bf16[512,1024]{1,0:T(8,128)(2,1)S(1)}, f32[512,1]{1,0:T(8,128)S(1)}) custom-call(s32[8]{0:T(128)S(1)} %compare_select_fusion.4.blocks, bf16[1,8192]{1,0:T(2,128)(2,1)S(1)} %broadcast_in_dim.45.refs_0_.gain_ref, bf16[8192,1024]{1,0:T(8,128)(2,1)} %refs_1_.7, f32[512,1024]{1,0:T(8,128)S(1)} %get-tuple-element.87.refs_2_, ...), custom_call_target="tpu_custom_call" | custom-call | flops 1073741824 | bytes 4194304 | tf_op jit(solution)/shard_map/query_part/pallas_call | solution.py:335
  111.5 6.5 %contexts.2 = (bf16[256,1024]{1,0:T(8,128)(2,1)S(1)}, bf16[256,1024]{1,0:T(8,128)(2,1)S(1)}, bf16[256,1024]{1,0:T(8,128)(2,1)S(1)}) custom-call(s32[8]{0:T(128)S(1)} %compare_select_fusion.4.blocks, bf16[512,1024]{1,0:T(8,128)(2,1)S(1)} %get-tuple-element.111.refs_0_, bf16[512,256]{1,0:T(8,128)(2,1)S(1)} %bitcast.20, f32[256,768]{1,0:T(8,128)S(1)} %copy-done.9, ...), custom_call_target="tpu_custom_call" | custom-call | flops 1610612736 | bytes 4194304 | tf_op jit(solution)/shard_map/contexts/pallas_call | solution.py:435
  120.1 9.2 %contexts.3 = (bf16[256,1024]{1,0:T(8,128)(2,1)S(1)}, bf16[256,1024]{1,0:T(8,128)(2,1)S(1)}, bf16[256,1024]{1,0:T(8,128)(2,1)S(1)}) custom-call(s32[8]{0:T(128)S(1)} %compare_select_fusion.4.blocks, bf16[512,1024]{1,0:T(8,128)(2,1)S(1)} %get-tuple-element.111.refs_0_, bf16[1536,256]{1,0:T(8,128)(2,1)S(1)} %bitcast.19, f32[256,1536]{1,0:T(8,128)S(1)} %copy-done.7, ...), custom_call_target="tpu_custom_call" | custom-call | flops 3221225472 | bytes 4194304 | tf_op jit(solution)/shard_map/contexts/pallas_call | solution.py:435
  131.5 4.6 %output_part.4 = (bf16[256,1024]{1,0:T(8,128)(2,1)S(1)}, bf16[256,1024]{1,0:T(8,128)(2,1)S(1)}) custom-call(s32[8]{0:T(128)S(1)} %compare_select_fusion.4.blocks, bf16[256,1024]{1,0:T(8,128)(2,1)S(1)} %get-tuple-element.117.refs_0_, bf16[256,1024]{1,0:T(8,128)(2,1)S(1)} %get-tuple-element.118.refs_1_, bf16[1024,8192]{1,0:T(8,128)(2,1)} %refs_2_.9, ...), custom_call_target="tpu_custom_call" | custom-call | flops 1073741824 | bytes 4194304 | tf_op jit(solution)/shard_map/output_part/pallas_call | solution.py:502
  136.0 5.5 %output_part.5 = (bf16[256,1024]{1,0:T(8,128)(2,1)S(1)}, bf16[256,1024]{1,0:T(8,128)(2,1)S(1)}, bf16[256,1024]{1,0:T(8,128)(2,1)S(1)}, bf16[256,1024]{1,0:T(8,128)(2,1)S(1)}) custom-call(s32[8]{0:T(128)S(1)} %compare_select_fusion.4.blocks, bf16[256,1024]{1,0:T(8,128)(2,1)S(1)} %get-tuple-element.117.refs_0_, ...), custom_call_target="tpu_custom_call" | custom-call | flops 2147483648 | bytes 4194304 | tf_op jit(solution)/shard_map/output_part/pallas_call | solution.py:502
  146.1 5.5 %output_part.6 = (bf16[256,1024]{1,0:T(8,128)(2,1)S(1)}, bf16[256,1024]{1,0:T(8,128)(2,1)S(1)}, bf16[256,1024]{1,0:T(8,128)(2,1)S(1)}, bf16[256,1024]{1,0:T(8,128)(2,1)S(1)}) custom-call(s32[8]{0:T(128)S(1)} %compare_select_fusion.4.blocks, bf16[256,1024]{1,0:T(8,128)(2,1)S(1)} %get-tuple-element.117.refs_0_, ...), custom_call_target="tpu_custom_call" | custom-call | flops 2147483648 | bytes 4194304 | tf_op jit(solution)/shard_map/output_part/pallas_call | solution.py:502
  151.6 5.0 %collective-permute-done.20.refs_0_ = bf16[256,1024]{1,0:T(8,128)(2,1)S(1)} collective-permute-done((bf16[256,1024]{1,0:T(8,128)(2,1)S(1)}, bf16[256,1024]{1,0:T(8,128)(2,1)S(1)}, u32[]{:S(2)}, u32[]{:S(2)}) %collective-permute-start.20) | collective-permute-done | bytes 524320 | tf_op jit(solution)/shard_map/ppermute | solution.py:525
  158.9 9.0 %collective-permute-done.27.refs_0_ = bf16[256,1024]{1,0:T(8,128)(2,1)S(1)} collective-permute-done((bf16[256,1024]{1,0:T(8,128)(2,1)S(1)}, bf16[256,1024]{1,0:T(8,128)(2,1)S(1)}, u32[]{:S(2)}, u32[]{:S(2)}) %collective-permute-start.27) | collective-permute-done | bytes 524320 | tf_op jit(solution)/shard_map/ppermute | solution.py:525
  171.8 7.3 %collective-permute-done.22.refs_0_ = bf16[256,1024]{1,0:T(8,128)(2,1)S(1)} collective-permute-done((bf16[256,1024]{1,0:T(8,128)(2,1)S(1)}, bf16[256,1024]{1,0:T(8,128)(2,1)S(1)}, u32[]{:S(2)}, u32[]{:S(2)}) %collective-permute-start.22) | collective-permute-done | bytes 524320 | tf_op jit(solution)/shard_map/ppermute | solution.py:525
  180.3 2.7 %collective-permute-done.30.refs_0_ = bf16[256,1024]{1,0:T(8,128)(2,1)S(1)} collective-permute-done((bf16[256,1024]{1,0:T(8,128)(2,1)S(1)}, bf16[256,1024]{1,0:T(8,128)(2,1)S(1)}, u32[]{:S(2)}, u32[]{:S(2)}) %collective-permute-start.30) | collective-permute-done | bytes 524320 | tf_op jit(solution)/shard_map/ppermute | solution.py:525
  183.2 1.6 collective-permute-start.31
  184.8 4.1 %output_part.7 = (bf16[256,1024]{1,0:T(8,128)(2,1)S(1)}, bf16[256,1024]{1,0:T(8,128)(2,1)S(1)}) custom-call(s32[8]{0:T(128)S(1)} %compare_select_fusion.4.blocks, bf16[256,1024]{1,0:T(8,128)(2,1)S(1)} %get-tuple-element.117.refs_0_, bf16[256,1024]{1,0:T(8,128)(2,1)S(1)} %get-tuple-element.118.refs_1_, bf16[1024,8192]{1,0:T(8,128)(2,1)} %refs_2_.9), custom_call_target="tpu_custom_call" | custom-call | flops 1073741824 | bytes 2097152 | tf_op jit(solution)/shard_map/output_part/pallas_call | solution.py:502
  188.9 2.0 collective-permute-done.24.refs_1_
  190.9 5.1 %collective-permute-done.23.refs_0_ = bf16[256,1024]{1,0:T(8,128)(2,1)S(1)} collective-permute-done((bf16[256,1024]{1,0:T(8,128)(2,1)S(1)}, bf16[256,1024]{1,0:T(8,128)(2,1)S(1)}, u32[]{:S(2)}, u32[]{:S(2)}) %collective-permute-start.23) | collective-permute-done | bytes 524320 | tf_op jit(solution)/shard_map/ppermute | solution.py:653
  196.6 2.3 %last_parts.1 = (f32[512,1024]{1,0:T(8,128)}, bf16[512,1024]{1,0:T(8,128)(2,1)}, f32[8,512]{1,0:T(8,128)S(1)}) custom-call(bf16[512,1024]{1,0:T(8,128)(2,1)S(1)} %copy-done.2, bf16[256,1024]{1,0:T(8,128)(2,1)S(1)} %collective-permute-done.23.refs_0_, bf16[256,1024]{1,0:T(8,128)(2,1)S(1)} %collective-permute-done.24.refs_1_, ...), custom_call_target="tpu_custom_call" | custom-call | flops 2097152 | bytes 6291456 | tf_op jit(solution)/shard_map/last_parts/pallas_call | solution.py:226
  200.1 2.5 %collective-permute-done.32 = f32[8,512]{1,0:T(8,128)S(1)} collective-permute-done((f32[8,512]{1,0:T(8,128)S(1)}, f32[8,512]{1,0:T(8,128)S(1)}, u32[]{:S(2)}, u32[]{:S(2)}) %collective-permute-start.32) | collective-permute-done | bytes 16416 | tf_op jit(solution)/shard_map/ppermute | solution.py:530
  202.6 3.2 %collective-permute-start.35 = (f32[8,512]{1,0:T(8,128)S(1)}, f32[8,512]{1,0:T(8,128)S(1)}, u32[]{:S(2)}, u32[]{:S(2)}) collective-permute-start(f32[8,512]{1,0:T(8,128)S(1)} %add.70), channel_id=1, source_target_pairs={{0,12},{2,14},{4,8},{6,10},{8,4},{10,6},{12,0},{14,2},{1,13},{3,15... | collective-permute-start | bytes 49160 | tf_op jit(solution)/shard_map/ppermute | solution.py:530
  208.1 2.3 %collective-permute-done.34 = f32[8,512]{1,0:T(8,128)S(1)} collective-permute-done((f32[8,512]{1,0:T(8,128)S(1)}, f32[8,512]{1,0:T(8,128)S(1)}, u32[]{:S(2)}, u32[]{:S(2)}) %collective-permute-start.34) | collective-permute-done | bytes 16416 | tf_op jit(solution)/shard_map/ppermute | solution.py:530
  (149 shorter events, 61.1 us)
Async XLA Ops:
  0.6 27.4 %collective-permute-start = (bf16[512,1024]{1,0:T(8,128)(2,1)}, bf16[512,1024]{1,0:T(8,128)(2,1)}, u32[]{:S(2)}, u32[]{:S(2)}) collective-permute-start(bf16[512,1024]{1,0:T(8,128)(2,1)} %x_ref.2), channel_id=1, source_target_pairs={{4,0},{8,4},{12,8},{14,12},{10,14},{6,10},{2,6},{0,2},{5,1},{9,5},... | collective-permute-start | bytes 3145736 | tf_op jit(solution)/shard_map/ppermute | solution.py:525
  3.6 26.4 %collective-permute-start.1 = (bf16[512,1024]{1,0:T(8,128)(2,1)}, bf16[512,1024]{1,0:T(8,128)(2,1)}, u32[]{:S(2)}, u32[]{:S(2)}) collective-permute-start(bf16[512,1024]{1,0:T(8,128)(2,1)} %x_ref.2), channel_id=1, source_target_pairs={{0,4},{4,8},{8,12},{12,14},{14,10},{10,6},{6,2},{2,0},{1,5},{5,9},... | collective-permute-start | bytes 3145736 | tf_op jit(solution)/shard_map/ppermute | solution.py:525
  17.0 15.1 %collective-permute-start.5 = (bf16[256,256]{1,0:T(8,128)(2,1)}, bf16[256,256]{1,0:T(8,128)(2,1)S(1)}, u32[]{:S(2)}, u32[]{:S(2)}) collective-permute-start(bf16[256,256]{1,0:T(8,128)(2,1)} %get-tuple-element.78), channel_id=1, source_target_pairs={{0,4},{4,8},{8,12},{12,14},{14,10},{10,6},{6,2},{2,0},{1,5},{5,9},... | collective-permute-start | bytes 393224 | tf_op jit(solution)/shard_map/ppermute | solution.py:525
  19.0 13.2 %collective-permute-start.6 = (bf16[256,256]{1,0:T(8,128)(2,1)S(1)}, bf16[256,256]{1,0:T(8,128)(2,1)S(1)}, u32[]{:S(2)}, u32[]{:S(2)}) collective-permute-start(bf16[256,256]{1,0:T(8,128)(2,1)S(1)} %get-tuple-element.79), channel_id=1, source_target_pairs={{4,0},{8,4},{12,8},{14,12},{10,14},{6,10},{2,6},{0,2},{5,1},{9,5},... | collective-permute-start | bytes 393224 | tf_op jit(solution)/shard_map/ppermute | solution.py:525
  20.6 45.1 %collective-permute-start.11 = (bf16[96,16,256]{2,1,0:T(8,128)(2,1)S(1)}, bf16[96,16,256]{2,1,0:T(8,128)(2,1)}, u32[]{:S(2)}, u32[]{:S(2)}) collective-permute-start(bf16[96,16,256]{2,1,0:T(8,128)(2,1)S(1)} %constant_dynamic-slice_fusion), channel_id=1, source_target_pairs={{0,1},{1,0},{2,3},{3,2},{4,5},{5,4},{6,7},{7,6},{8,9},{9,8},{10,11... | collective-permute-start | bytes 2359304 | tf_op jit(solution)/shard_map/ppermute | solution.py:581
  28.0 24.5 %collective-permute-start.2 = (bf16[512,1024]{1,0:T(8,128)(2,1)}, bf16[512,1024]{1,0:T(8,128)(2,1)}, u32[]{:S(2)}, u32[]{:S(2)}) collective-permute-start(bf16[512,1024]{1,0:T(8,128)(2,1)} %collective-permute-done.refs_3_), channel_id=1, source_target_pairs={{4,0},{8,4},{12,8},{14,12},{10,14},{6,10},{2,6},{0,2},{5,1},{9,5},... | collective-permute-start | bytes 3145736 | tf_op jit(solution)/shard_map/ppermute | solution.py:525
  30.0 23.8 %collective-permute-start.3 = (bf16[512,1024]{1,0:T(8,128)(2,1)}, bf16[512,1024]{1,0:T(8,128)(2,1)}, u32[]{:S(2)}, u32[]{:S(2)}) collective-permute-start(bf16[512,1024]{1,0:T(8,128)(2,1)} %collective-permute-done.1.refs_4_), channel_id=1, source_target_pairs={{0,4},{4,8},{8,12},{12,14},{14,10},{10,6},{6,2},{2,0},{1,5},{5,9},... | collective-permute-start | bytes 3145736 | tf_op jit(solution)/shard_map/ppermute | solution.py:525
  53.9 34.2 %collective-permute-start.7 = (bf16[512,1024]{1,0:T(8,128)(2,1)}, bf16[512,1024]{1,0:T(8,128)(2,1)}, u32[]{:S(2)}, u32[]{:S(2)}) collective-permute-start(bf16[512,1024]{1,0:T(8,128)(2,1)} %collective-permute-done.2.refs_4_), channel_id=1, source_target_pairs={{4,0},{8,4},{12,8},{14,12},{10,14},{6,10},{2,6},{0,2},{5,1},{9,5},... | collective-permute-start | bytes 3145736 | tf_op jit(solution)/shard_map/ppermute | solution.py:525
  55.4 31.6 %collective-permute-start.8 = (bf16[512,1024]{1,0:T(8,128)(2,1)}, bf16[512,1024]{1,0:T(8,128)(2,1)}, u32[]{:S(2)}, u32[]{:S(2)}) collective-permute-start(bf16[512,1024]{1,0:T(8,128)(2,1)} %collective-permute-done.3.refs_5_), channel_id=1, source_target_pairs={{0,4},{4,8},{8,12},{12,14},{14,10},{10,6},{6,2},{2,0},{1,5},{5,9},... | collective-permute-start | bytes 3145736 | tf_op jit(solution)/shard_map/ppermute | solution.py:525
  57.0 26.7 %collective-permute-start.9 = (bf16[512,256]{1,0:T(8,128)(2,1)}, bf16[512,256]{1,0:T(8,128)(2,1)}, u32[]{:S(2)}, u32[]{:S(2)}) collective-permute-start(bf16[512,256]{1,0:T(8,128)(2,1)} %get-tuple-element.83), channel_id=1, source_target_pairs={{0,4},{4,8},{8,12},{12,14},{14,10},{10,6},{6,2},{2,0},{1,5},{5,9},... | collective-permute-start | bytes 786440 | tf_op jit(solution)/shard_map/ppermute | solution.py:525
  57.4 26.3 %collective-permute-start.10 = (bf16[512,256]{1,0:T(8,128)(2,1)}, bf16[512,256]{1,0:T(8,128)(2,1)}, u32[]{:S(2)}, u32[]{:S(2)}) collective-permute-start(bf16[512,256]{1,0:T(8,128)(2,1)} %get-tuple-element.84), channel_id=1, source_target_pairs={{4,0},{8,4},{12,8},{14,12},{10,14},{6,10},{2,6},{0,2},{5,1},{9,5},... | collective-permute-start | bytes 786440 | tf_op jit(solution)/shard_map/ppermute | solution.py:525
  84.9 9.2 %collective-permute-start.14 = (bf16[512,256]{1,0:T(8,128)(2,1)S(1)}, bf16[512,256]{1,0:T(8,128)(2,1)S(1)}, u32[]{:S(2)}, u32[]{:S(2)}) collective-permute-start(bf16[512,256]{1,0:T(8,128)(2,1)S(1)} %get-tuple-element.97), channel_id=1, source_target_pairs={{0,4},{4,8},{8,12},{12,14},{14,10},{10,6},{6,2},{2,0},{1,5},{5,9},... | collective-permute-start | bytes 786440 | tf_op jit(solution)/shard_map/ppermute | solution.py:525
  85.4 9.2 %collective-permute-start.15 = (bf16[512,256]{1,0:T(8,128)(2,1)S(1)}, bf16[512,256]{1,0:T(8,128)(2,1)S(1)}, u32[]{:S(2)}, u32[]{:S(2)}) collective-permute-start(bf16[512,256]{1,0:T(8,128)(2,1)S(1)} %get-tuple-element.98), channel_id=1, source_target_pairs={{4,0},{8,4},{12,8},{14,12},{10,14},{6,10},{2,6},{0,2},{5,1},{9,5},... | collective-permute-start | bytes 786440 | tf_op jit(solution)/shard_map/ppermute | solution.py:525
  89.2 18.4 %collective-permute-start.12 = (bf16[256,1024]{1,0:T(8,128)(2,1)S(1)}, bf16[256,1024]{1,0:T(8,128)(2,1)S(1)}, u32[]{:S(2)}, u32[]{:S(2)}) collective-permute-start(bf16[256,1024]{1,0:T(8,128)(2,1)S(1)} %slice.30), channel_id=1, source_target_pairs={{0,4},{4,8},{8,12},{12,14},{14,10},{10,6},{6,2},{2,0},{1,5},{5,9},... | collective-permute-start | bytes 1572872 | tf_op jit(solution)/shard_map/ppermute | solution.py:525
  89.7 17.9 %collective-permute-start.13 = (bf16[256,1024]{1,0:T(8,128)(2,1)S(1)}, bf16[256,1024]{1,0:T(8,128)(2,1)S(1)}, u32[]{:S(2)}, u32[]{:S(2)}) collective-permute-start(bf16[256,1024]{1,0:T(8,128)(2,1)S(1)} %slice.31), channel_id=1, source_target_pairs={{4,0},{8,4},{12,8},{14,12},{10,14},{6,10},{2,6},{0,2},{5,1},{9,5},... | collective-permute-start | bytes 1572872 | tf_op jit(solution)/shard_map/ppermute | solution.py:525
  94.7 12.5 %collective-permute-start.16 = (bf16[512,256]{1,0:T(8,128)(2,1)S(1)}, bf16[512,256]{1,0:T(8,128)(2,1)S(1)}, u32[]{:S(2)}, u32[]{:S(2)}) collective-permute-start(bf16[512,256]{1,0:T(8,128)(2,1)S(1)} %get-tuple-element.104), channel_id=1, source_target_pairs={{0,4},{4,8},{8,12},{12,14},{14,10},{10,6},{6,2},{2,0},{1,5},{5,9},... | collective-permute-start | bytes 786440 | tf_op jit(solution)/shard_map/ppermute | solution.py:525
  95.4 12.0 %collective-permute-start.17 = (bf16[512,256]{1,0:T(8,128)(2,1)S(1)}, bf16[512,256]{1,0:T(8,128)(2,1)S(1)}, u32[]{:S(2)}, u32[]{:S(2)}) collective-permute-start(bf16[512,256]{1,0:T(8,128)(2,1)S(1)} %get-tuple-element.105), channel_id=1, source_target_pairs={{4,0},{8,4},{12,8},{14,12},{10,14},{6,10},{2,6},{0,2},{5,1},{9,5},... | collective-permute-start | bytes 786440 | tf_op jit(solution)/shard_map/ppermute | solution.py:525
  118.0 13.4 %collective-permute-start.18 = (bf16[256,1024]{1,0:T(8,128)(2,1)S(1)}, bf16[256,1024]{1,0:T(8,128)(2,1)S(1)}, u32[]{:S(2)}, u32[]{:S(2)}) collective-permute-start(bf16[256,1024]{1,0:T(8,128)(2,1)S(1)} %get-tuple-element.110), channel_id=1, source_target_pairs={{0,4},{4,8},{8,12},{12,14},{14,10},{10,6},{6,2},{2,0},{1,5},{5,9},... | collective-permute-start | bytes 1572872 | tf_op jit(solution)/shard_map/ppermute | solution.py:525
  119.1 12.4 %collective-permute-start.19 = (bf16[256,1024]{1,0:T(8,128)(2,1)S(1)}, bf16[256,1024]{1,0:T(8,128)(2,1)S(1)}, u32[]{:S(2)}, u32[]{:S(2)}) collective-permute-start(bf16[256,1024]{1,0:T(8,128)(2,1)S(1)} %get-tuple-element.114), channel_id=1, source_target_pairs={{4,0},{8,4},{12,8},{14,12},{10,14},{6,10},{2,6},{0,2},{5,1},{9,5},... | collective-permute-start | bytes 1572872 | tf_op jit(solution)/shard_map/ppermute | solution.py:525
  129.4 14.5 %collective-permute-start.25 = (bf16[256,1024]{1,0:T(8,128)(2,1)S(1)}, bf16[256,1024]{1,0:T(8,128)(2,1)S(1)}, u32[]{:S(2)}, u32[]{:S(2)}) collective-permute-start(bf16[256,1024]{1,0:T(8,128)(2,1)S(1)} %get-tuple-element.129), channel_id=1, source_target_pairs={{0,4},{4,8},{8,12},{12,14},{14,10},{10,6},{6,2},{2,0},{1,5},{5,9},... | collective-permute-start | bytes 1572872 | tf_op jit(solution)/shard_map/ppermute | solution.py:525
  130.4 13.4 %collective-permute-start.26 = (bf16[256,1024]{1,0:T(8,128)(2,1)S(1)}, bf16[256,1024]{1,0:T(8,128)(2,1)S(1)}, u32[]{:S(2)}, u32[]{:S(2)}) collective-permute-start(bf16[256,1024]{1,0:T(8,128)(2,1)S(1)} %get-tuple-element.130), channel_id=1, source_target_pairs={{4,0},{8,4},{12,8},{14,12},{10,14},{6,10},{2,6},{0,2},{5,1},{9,5},... | collective-permute-start | bytes 1572872 | tf_op jit(solution)/shard_map/ppermute | solution.py:525
  141.7 14.9 %collective-permute-start.20 = (bf16[256,1024]{1,0:T(8,128)(2,1)S(1)}, bf16[256,1024]{1,0:T(8,128)(2,1)S(1)}, u32[]{:S(2)}, u32[]{:S(2)}) collective-permute-start(bf16[256,1024]{1,0:T(8,128)(2,1)S(1)} %get-tuple-element.121), channel_id=1, source_target_pairs={{0,4},{4,8},{8,12},{12,14},{14,10},{10,6},{6,2},{2,0},{1,5},{5,9},... | collective-permute-start | bytes 1572872 | tf_op jit(solution)/shard_map/ppermute | solution.py:525
  142.8 14.4 %collective-permute-start.21 = (bf16[256,1024]{1,0:T(8,128)(2,1)S(1)}, bf16[256,1024]{1,0:T(8,128)(2,1)S(1)}, u32[]{:S(2)}, u32[]{:S(2)}) collective-permute-start(bf16[256,1024]{1,0:T(8,128)(2,1)S(1)} %get-tuple-element.122), channel_id=1, source_target_pairs={{4,0},{8,4},{12,8},{14,12},{10,14},{6,10},{2,6},{0,2},{5,1},{9,5},... | collective-permute-start | bytes 1572872 | tf_op jit(solution)/shard_map/ppermute | solution.py:525
  144.1 23.8 %collective-permute-start.27 = (bf16[256,1024]{1,0:T(8,128)(2,1)S(1)}, bf16[256,1024]{1,0:T(8,128)(2,1)S(1)}, u32[]{:S(2)}, u32[]{:S(2)}) collective-permute-start(bf16[256,1024]{1,0:T(8,128)(2,1)S(1)} %get-tuple-element.133), channel_id=1, source_target_pairs={{0,4},{4,8},{8,12},{12,14},{14,10},{10,6},{6,2},{2,0},{1,5},{5,9},... | collective-permute-start | bytes 1572872 | tf_op jit(solution)/shard_map/ppermute | solution.py:525
  145.1 22.8 %collective-permute-start.28 = (bf16[256,1024]{1,0:T(8,128)(2,1)S(1)}, bf16[256,1024]{1,0:T(8,128)(2,1)S(1)}, u32[]{:S(2)}, u32[]{:S(2)}) collective-permute-start(bf16[256,1024]{1,0:T(8,128)(2,1)S(1)} %get-tuple-element.134), channel_id=1, source_target_pairs={{4,0},{8,4},{12,8},{14,12},{10,14},{6,10},{2,6},{0,2},{5,1},{9,5},... | collective-permute-start | bytes 1572872 | tf_op jit(solution)/shard_map/ppermute | solution.py:525
  157.5 21.6 %collective-permute-start.22 = (bf16[256,1024]{1,0:T(8,128)(2,1)S(1)}, bf16[256,1024]{1,0:T(8,128)(2,1)S(1)}, u32[]{:S(2)}, u32[]{:S(2)}) collective-permute-start(bf16[256,1024]{1,0:T(8,128)(2,1)S(1)} %get-tuple-element.125), channel_id=1, source_target_pairs={{0,4},{4,8},{8,12},{12,14},{14,10},{10,6},{6,2},{2,0},{1,5},{5,9},... | collective-permute-start | bytes 1572872 | tf_op jit(solution)/shard_map/ppermute | solution.py:525
  168.1 14.9 %collective-permute-start.30 = (bf16[256,1024]{1,0:T(8,128)(2,1)S(1)}, bf16[256,1024]{1,0:T(8,128)(2,1)S(1)}, u32[]{:S(2)}, u32[]{:S(2)}) collective-permute-start(bf16[256,1024]{1,0:T(8,128)(2,1)S(1)} %get-tuple-element.138), channel_id=1, source_target_pairs={{4,0},{8,4},{12,8},{14,12},{10,14},{6,10},{2,6},{0,2},{5,1},{9,5},... | collective-permute-start | bytes 1572872 | tf_op jit(solution)/shard_map/ppermute | solution.py:525
  169.8 21.2 %collective-permute-start.24 = (bf16[256,1024]{1,0:T(8,128)(2,1)S(1)}, bf16[256,1024]{1,0:T(8,128)(2,1)S(1)}, u32[]{:S(2)}, u32[]{:S(2)}) collective-permute-start(bf16[256,1024]{1,0:T(8,128)(2,1)S(1)} %get-tuple-element.127), channel_id=1, source_target_pairs={{4,0},{8,4},{12,8},{14,12},{10,14},{6,10},{2,6},{0,2},{5,1},{9,5},... | collective-permute-start | bytes 1572872 | tf_op jit(solution)/shard_map/ppermute | solution.py:525
  171.3 19.6 %collective-permute-start.29 = (bf16[256,1024]{1,0:T(8,128)(2,1)S(1)}, bf16[256,1024]{1,0:T(8,128)(2,1)S(1)}, u32[]{:S(2)}, u32[]{:S(2)}) collective-permute-start(bf16[256,1024]{1,0:T(8,128)(2,1)S(1)} %get-tuple-element.137), channel_id=1, source_target_pairs={{0,4},{4,8},{8,12},{12,14},{14,10},{10,6},{6,2},{2,0},{1,5},{5,9},... | collective-permute-start | bytes 1572872 | tf_op jit(solution)/shard_map/ppermute | solution.py:525
  179.2 16.8 %collective-permute-start.23 = (bf16[256,1024]{1,0:T(8,128)(2,1)S(1)}, bf16[256,1024]{1,0:T(8,128)(2,1)S(1)}, u32[]{:S(2)}, u32[]{:S(2)}) collective-permute-start(bf16[256,1024]{1,0:T(8,128)(2,1)S(1)} %add_parts.8), channel_id=1, source_target_pairs={{0,4},{4,8},{8,12},{12,14},{14,10},{10,6},{6,2},{2,0},{1,5},{5,9},... | collective-permute-start | bytes 1572872 | tf_op jit(solution)/shard_map/ppermute | solution.py:653
  183.2 13.4 %collective-permute-start.31 = (bf16[256,1024]{1,0:T(8,128)(2,1)S(1)}, bf16[256,1024]{1,0:T(8,128)(2,1)S(1)}, u32[]{:S(2)}, u32[]{:S(2)}) collective-permute-start(bf16[256,1024]{1,0:T(8,128)(2,1)S(1)} %add_parts.11), channel_id=1, source_target_pairs={{4,0},{8,4},{12,8},{14,12},{10,14},{6,10},{2,6},{0,2},{5,1},{9,5},... | collective-permute-start | bytes 1572872 | tf_op jit(solution)/shard_map/ppermute | solution.py:654
  202.6 5.5 %collective-permute-start.35 = (f32[8,512]{1,0:T(8,128)S(1)}, f32[8,512]{1,0:T(8,128)S(1)}, u32[]{:S(2)}, u32[]{:S(2)}) collective-permute-start(f32[8,512]{1,0:T(8,128)S(1)} %add.70), channel_id=1, source_target_pairs={{0,12},{2,14},{4,8},{6,10},{8,4},{10,6},{12,0},{14,2},{1,13},{3,15... | collective-permute-start | bytes 49160 | tf_op jit(solution)/shard_map/ppermute | solution.py:530
  (28 other events, 151.3 us)
